TPU v7x, 32 devices: a whole 2x2x4 slice. The times are simulated.
32 devices in a mesh: feat: 8 (over z, x), tok: 4 (over y, core).
Axes of the slice: x: 2, y: 2, z: 4, core: 2. Of those that a mesh axis runs over, the one named last changes fastest.
Arguments:
- activations: bfloat16 [512, 8192], P('tok', 'feat'), may hold values from -6 to 6
- w_base: bfloat16 [8192, 8192], P('feat', 'tok'), may hold values from -0.0625 to 0.0625
- blk_vals: bfloat16 [24, 128, 128], P('feat'), may hold values from -0.5 to 0.5
- blk_index: int32 [24, 2], P('feat'), may hold values from 0 to 63, as said below
- blk_count: int32 [8], P('feat'), may hold values from 1 to 3, as said below
- a_down: bfloat16 [8192, 64], P('feat'), may hold values from -0.0625 to 0.0625
- b_up: bfloat16 [64, 8192], P(None, 'feat'), may hold values from -0.75 to 0.75
- grad_out: bfloat16 [512, 8192], P('tok', 'feat'), may hold values from -6 to 6
Outputs:
- projected: bfloat16 [512, 8192], P('tok', 'feat')
- grad_x: bfloat16 [512, 8192], P('tok', 'feat')
- grad_blocks: float32 [24, 128, 128], P('feat')
- grad_a: float32 [8192, 64], P('feat')
- grad_b: float32 [64, 8192], P(None, 'feat')
Inputs may be any that keep to these rules, and one draw needn't show every extreme that they name: `blk_index`: column 0 is below 8 and column 1 below 64; both largest values occur in every draw. `blk_count`: some feature shard holds exactly 3 live slots in every draw.
All inputs are finite; a program needn't handle non-finite values.
Results may differ from a plain program's by a relative error of at most 0.014.
Values may be sent and summed in bfloat16 or wider, within the bound.
No kernel may reach another device: no remote copies, remote signals or barrier semaphores. Data moves between devices by JAX's collectives and lax.ppermute only.
A program may use at most 64 MiB of HBM per device.

v0:
```python
import jax
import jax.numpy as jnp
from jax import lax
from jax.sharding import PartitionSpec as P

BLK = 128


def on_device(activations, w_base, blk_vals, blk_index, blk_count, a_down, b_up, grad_out):
    tok_rows = activations.shape[0]
    grad_scale = float(tok_rows * lax.axis_size("tok")) ** (-0.5)
    live_count = blk_count[0]
    u_part = jnp.dot(activations, a_down, preferred_element_type=jnp.float32)
    v_part = jnp.dot(grad_out, b_up.T, preferred_element_type=jnp.float32)
    u_total = lax.psum(u_part, "feat")
    u_half = u_total.astype(jnp.bfloat16)
    w_rows = lax.all_gather(w_base, "tok", axis=1, tiled=True)
    own_cols = b_up.shape[1]
    col_term = lax.dot_general(
        w_rows, activations, (((0,), (1,)), ((), ())), preferred_element_type=jnp.float32
    )
    for column_slot_idx in range(blk_vals.shape[0]):
        column_is_live = (column_slot_idx < live_count).astype(jnp.float32)
        column_row_start = blk_index[column_slot_idx, 0] * BLK
        column_col_start = blk_index[column_slot_idx, 1] * BLK
        column_x_cols = lax.dynamic_slice_in_dim(activations, column_row_start, BLK, 1)
        blk_term = lax.dot_general(
            blk_vals[column_slot_idx],
            column_x_cols,
            (((0,), (1,)), ((), ())),
            preferred_element_type=jnp.float32,
        )
        inside = jnp.logical_and(
            column_col_start >= 0, column_col_start < lax.axis_size("feat") * own_cols
        ).astype(jnp.float32)
        put_at = jnp.clip(column_col_start, 0, lax.axis_size("feat") * own_cols - BLK)
        column_current = lax.dynamic_slice_in_dim(col_term, put_at, BLK, 0)
        col_term = lax.dynamic_update_slice_in_dim(
            col_term, column_current + blk_term * (column_is_live * inside), put_at, 0
        )
    own_sums = (
        lax.psum_scatter(col_term.astype(jnp.bfloat16), "feat", scatter_dimension=0, tiled=True)
        .astype(jnp.float32)
        .T
    )
    projected = (own_sums + jnp.dot(u_half, b_up, preferred_element_type=jnp.float32)).astype(
        jnp.bfloat16
    )
    v_total = lax.psum(v_part, "feat")
    v_half = v_total.astype(jnp.bfloat16)
    cot_rows = lax.all_gather(grad_out, "feat", axis=1, tiled=True)
    backward = jnp.dot(cot_rows, w_rows.T, preferred_element_type=jnp.float32)
    block_terms = []
    for slot_idx in range(blk_vals.shape[0]):
        is_live = (slot_idx < live_count).astype(jnp.float32)
        row_start = blk_index[slot_idx, 0] * BLK
        col_start = blk_index[slot_idx, 1] * BLK
        x_cols = lax.dynamic_slice_in_dim(activations, row_start, BLK, 1)
        g_cols = lax.dynamic_slice_in_dim(cot_rows, col_start, BLK, 1)
        back_add = (
            jnp.dot(g_cols, blk_vals[slot_idx].T, preferred_element_type=jnp.float32) * is_live
        )
        current = lax.dynamic_slice_in_dim(backward, row_start, BLK, 1)
        backward = lax.dynamic_update_slice_in_dim(backward, current + back_add, row_start, 1)
        block_terms.append(jnp.dot(x_cols.T, g_cols, preferred_element_type=jnp.float32) * is_live)
    grad_x = (backward + jnp.dot(v_half, a_down.T, preferred_element_type=jnp.float32)).astype(
        jnp.bfloat16
    )
    block_local = jnp.stack(block_terms, axis=0)
    down_local = jnp.dot(activations.T, v_half, preferred_element_type=jnp.float32)
    up_local = jnp.dot(u_half.T, grad_out, preferred_element_type=jnp.float32)
    block_sum, down_sum, up_sum = lax.psum((block_local, down_local, up_local), "tok")
    return (projected, grad_x, block_sum * grad_scale, down_sum * grad_scale, up_sum * grad_scale)


def solution(mesh):
    in_specs = (
        P("tok", "feat"),
        P("feat", "tok"),
        P("feat", None, None),
        P("feat", None),
        P("feat"),
        P("feat", None),
        P(None, "feat"),
        P("tok", "feat"),
    )
    out_specs = (
        P("tok", "feat"),
        P("tok", "feat"),
        P("feat", None, None),
        P("feat", None),
        P(None, "feat"),
    )
    return jax.shard_map(
        on_device, mesh=mesh, in_specs=in_specs, out_specs=out_specs, check_vma=False
    )
```

profile of v0, /device:TPU:0, one launch (start us, length us, event | category | flops | bytes accessed | tf_op | source)
XLA Modules:
  0.0 286.5 jit_solution(16922306528854053145)
XLA Ops:
  14.4 40.1 %all-reduce = (bf16[128,64]{0,1:T(8,128)(2,1)S(1)}, bf16[128,64]{0,1:T(8,128)(2,1)S(1)}) all-reduce(f32[128,64]{0,1:T(8,128)S(1)} %fusion.57, f32[128,64]{0,1:T(8,128)S(1)} %fusion.59), channel_id=1, replica_groups=mesh['feat'=8,'tok'=4] {'feat'}, use_global_device_ids=true, to_apply=%region_1.2 | all-reduce | flops 16384 | bytes 98304 | tf_op jit(solution)/shard_map/psum | solution.py:15
  54.5 0.9 fusion.60
  55.4 0.9 convolution_bitcast_fusion
  56.3 6.2 %all-gather.5.cloned.1.call-done = bf16[128,8192]{1,0:T(8,128)(2,1)} async-done(((bf16[128,1024]{1,0:T(8,128)(2,1)}), bf16[128,8192]{1,0:T(8,128)(2,1)}) %all-gather.5.cloned.1.call-update) | async-done | bytes 2097168 | tf_op jit(solution)/shard_map/all_gather | solution.py:51
  62.5 0.9 fusion.2
  63.5 1.0 fusion.3
  64.4 1.0 fusion.4
  66.2 103.0 %all-gather.3.cloned.1.call-done = bf16[1024,8192]{1,0:T(8,128)(2,1)} async-done(((bf16[1024,2048]{1,0:T(8,128)(2,1)}), bf16[1024,8192]{1,0:T(8,128)(2,1)}) %all-gather.3.cloned.1.call-update) | async-done | bytes 16777232 | tf_op jit(solution)/shard_map/all_gather | solution.py:17
  169.2 8.2 %fusion.56 = f32[8192,128]{1,0:T(8,128)S(1)} fusion(bf16[1024,8192]{1,0:T(8,128)(2,1)} %all-gather.3.cloned.1.call-done, bf16[128,1024]{1,0:T(8,128)(2,1)S(1)} %copy-done), kind=kOutput, calls=%fused_computation.72 | convolution fusion | flops 2147483648 | bytes 21233664 | tf_op jit(solution)/shard_map/dot_general | solution.py:19
  177.5 1.9 copy-done.1
  179.6 1.5 dynamic_update_slice.18
  181.1 1.1 fusion.14
  182.2 1.5 dynamic_update_slice.19
  183.7 1.1 fusion.12
  184.8 1.5 dynamic_update_slice.20
  186.3 3.8 %convert_element_type.46 = bf16[8192,128]{1,0:T(8,128)(2,1)} convert(f32[8192,128]{1,0:T(8,128)} %dynamic_update_slice.20) | non-fusion elementwise | flops 1048576 | bytes 6291456 | tf_op jit(solution)/shard_map/convert_element_type | solution.py:42
  190.1 16.7 %all-reduce.4.cloned.1.call-done = (f32[3,128,128]{2,1,0:T(8,128)}, f32[1024,64]{0,1:T(8,128)}, f32[64,1024]{1,0:T(8,128)}) async-done(((f32[3,128,128]{2,1,0:T(8,128)}, f32[1024,64]{0,1:T(8,128)}, f32[64,1024]{1,0:T(8,128)}), (f32[3,128,128]{2,1,0:T(8,128)}, f32[1024,64]{0,1:T(8,128)}, f32[64,1024]{1,0:T(8,128)})) %all-reduce.4.cloned.1.call-update) | async-done | bytes 720912 | tf_op jit(solution)/shard_map/psum | solution.py:72
  206.8 1.6 broadcast_multiply_fusion.2
  208.4 1.7 broadcast_multiply_fusion.1
  210.1 1.7 broadcast_multiply_fusion
  211.8 11.4 %fusion.58 = f32[128,1024]{1,0:T(8,128)S(1)} fusion(bf16[128,8192]{1,0:T(8,128)(2,1)S(1)} %copy-done.2, bf16[1024,8192]{1,0:T(8,128)(2,1)} %all-gather.3.cloned.1.call-done), kind=kOutput, calls=%fused_computation.74 | convolution fusion | flops 2147483648 | bytes 19398656 | tf_op jit(solution)/shard_map/dot_general | solution.py:52
  223.7 1.0 fusion.1
  224.7 53.2 %reduce-scatter.2.cloned.1.call-done = bf16[1024,128]{1,0:T(8,128)(2,1)} async-done(((bf16[8192,128]{1,0:T(8,128)(2,1)}), bf16[1024,128]{1,0:T(8,128)(2,1)}) %reduce-scatter.2.cloned.1.call-update) | async-done | bytes 262160 | tf_op jit(solution)/shard_map/reduce_scatter | solution.py:42
  277.9 1.2 fusion
  (32 shorter events, 4.9 us)
Async XLA Ops:
  7.2 7.0 %copy-start = (bf16[128,1024]{1,0:T(8,128)(2,1)S(1)}, bf16[128,1024]{1,0:T(8,128)(2,1)}, u32[]{:S(2)}) copy-start(bf16[128,1024]{1,0:T(8,128)(2,1)} %param.8) | copy-start | bytes 786436
  7.2 55.4 %all-gather.5.cloned.1.call-start = ((), (), s32[]{:S(2)}) async-start(), calls=%async_computation.3 | async-start | bytes 2359296 | tf_op jit(solution)/shard_map/all_gather | solution.py:51
  7.9 0.8 copy-start.7
  7.9 6.0 %copy-start.3 = (bf16[128,1024]{1,0:T(8,128)(2,1)S(1)}, bf16[128,1024]{1,0:T(8,128)(2,1)}, u32[]{:S(2)}) copy-start(bf16[128,1024]{1,0:T(8,128)(2,1)} %param.15) | copy-start | bytes 786436
  7.9 6.0 %copy-start.5 = (bf16[64,1024]{1,0:T(8,128)(2,1)S(1)}, bf16[64,1024]{1,0:T(8,128)(2,1)}, u32[]{:S(2)}) copy-start(bf16[64,1024]{1,0:T(8,128)(2,1)} %param.14) | copy-start | bytes 393220
  7.9 6.3 %copy-start.4 = (bf16[1024,64]{0,1:T(8,128)(2,1)S(1)}, bf16[1024,64]{0,1:T(8,128)(2,1)}, u32[]{:S(2)}) copy-start(bf16[1024,64]{0,1:T(8,128)(2,1)} %param.13) | copy-start | bytes 393220
  8.0 161.2 %all-gather.3.cloned.1.call-start = ((), (), s32[]{:S(2)}) async-start(), calls=%async_computation.1 | async-start | bytes 20971520 | tf_op jit(solution)/shard_map/all_gather | solution.py:17
  8.7 198.1 %all-reduce.4.cloned.1.call-start = ((), (), s32[]{:S(2)}) async-start(), calls=%async_computation.4 | async-start | bytes 1441792 | tf_op jit(solution)/shard_map/psum | solution.py:72
  66.1 113.3 %copy-start.6 = (bf16[3,128,128]{2,1,0:T(8,128)(2,1)S(1)}, bf16[3,128,128]{2,1,0:T(8,128)(2,1)}, u32[]{:S(2)}) copy-start(bf16[3,128,128]{2,1,0:T(8,128)(2,1)} %param.10) | copy-start | bytes 294916
  66.1 211.7 %reduce-scatter.2.cloned.1.call-start = ((), (), s32[]{:S(2)}) async-start(), calls=%async_computation.2 | async-start | bytes 2359296 | tf_op jit(solution)/shard_map/reduce_scatter | solution.py:42
  177.5 1.9 copy-start.1
  190.1 21.7 %copy-start.2 = (bf16[128,8192]{1,0:T(8,128)(2,1)S(1)}, bf16[128,8192]{1,0:T(8,128)(2,1)}, u32[]{:S(2)}) copy-start(bf16[128,8192]{1,0:T(8,128)(2,1)} %all-gather.5.cloned.1.call-done) | copy-start | bytes 6291460
Sparse Core Ops, SparseCore 0:
  10.2 52.2 all-gather.4
  64.1 105.0 all-gather.2
  172.3 34.4 all-reduce.3
  210.2 67.6 reduce-scatter.1
where the time goes:
time: 287 us; the launch traced here: 286 us
  waiting for transfers between devices  181 us (63%)
  blocking collectives  40.1 us (14%)
  matrix products  29.7 us (10%)
  between operations  18.5 us (6%)
  other arithmetic  9.43 us (3%)
  local copies, waits for them, and re-layouts  7.99 us (3%)
    all_gather x1, waiting for transfers between devices, on_device(): w_rows = lax.all_gather(w_base, 'tok', axis=1, tiled=True)  103 us
    reduce_scatter x1, waiting for transfers between devices, on_device(): lax.psum_scatter(col_term.astype(jnp.bfloat16), 'feat', scatter_dimension...  53.2 us
    psum x1, blocking collectives, on_device(): u_total = lax.psum(u_part, 'feat')  40.1 us
    psum x1, waiting for transfers between devices, on_device(): lax.psum((block_local, down_local, up_local), 'tok')  16.7 us
    dot_general x1, matrix products, on_device(): backward = jnp.dot(cot_rows, w_rows.T, preferred_element_type=jnp.float32)  11.4 us
    dot_general x1, matrix products, on_device(): lax.dot_general(w_rows, activations, (((0,), (1,)), ((), ())), preferred_...  8.24 us
    all_gather x1, waiting for transfers between devices, on_device(): cot_rows = lax.all_gather(grad_out, 'feat', axis=1, tiled=True)  6.24 us
  transfers between devices with their start and end apart: 4, of which 4 were waited for; matrix products, arithmetic and copies ran while one was open for 15% of the time, Pallas kernels for 0%

commit v1 on v0

v1 whole, which is shorter than its diff:
```python
import functools

import jax
import jax.numpy as jnp
from jax import lax
from jax.experimental import pallas as pl
from jax.experimental.pallas import tpu as pltpu
from jax.sharding import PartitionSpec as P

BLK = 128
F32 = jnp.float32
BF16 = jnp.bfloat16
VMEM_BYTES = 48 * 1024 * 1024


def swap(value, axis, mask):
    size = lax.axis_size(axis)
    return lax.ppermute(value, axis, [(i, i ^ mask) for i in range(size)])


def tree_sum(terms):
    while len(terms) > 1:
        terms = [terms[i] + terms[i + 1] for i in range(0, len(terms), 2)]
    return terms[0]


def pick(options, index):
    value = options[0]
    for place in range(1, len(options)):
        value = jnp.where(index == place, options[place], value)
    return value


def added(left, right):
    return (left.astype(F32) + right.astype(F32)).astype(BF16)


def project_kernel(slots, which, scal, x_ref, *refs):
    n_tiles = 2 if which is None else 1
    w_refs, vals_ref = refs[:n_tiles], refs[n_tiles]
    out_refs, acc = refs[n_tiles + 1 : -1], refs[-1]
    step, tile = pl.program_id(0), pl.program_id(1)
    wide, shard = acc.shape[1], x_ref.shape[1]
    far = 1 - step % 2
    held = (1 - step // 2) ^ scal[1] if which is None else which
    for place, w_ref in enumerate(w_refs):

        @pl.when(True if which is not None else held == place)
        def _():
            acc[...] = jnp.dot(x_ref[...], w_ref[...], preferred_element_type=F32)

    first = (2 * (scal[2] ^ held) + (far ^ scal[0])) * shard + tile * wide
    for slot in range(slots):
        local = scal[5 + 2 * slot] * BLK - first

        @pl.when((slot < scal[3]) & (local >= 0) & (local < wide))
        def _():
            columns = pl.ds(pl.multiple_of(local, BLK), BLK)
            x_cols = x_ref[:, pl.ds(pl.multiple_of(scal[4 + 2 * slot] * BLK, BLK), BLK)]
            acc[:, columns] += jnp.dot(x_cols, vals_ref[slot], preferred_element_type=F32)

    for place, out_ref in enumerate(out_refs):

        @pl.when(step == place)
        def _():
            out_ref[...] = acc[...].astype(BF16)


def project(scal, x, tiles, vals, which=None):
    rows, shard = x.shape
    wide = min(512, shard)
    per = shard // wide
    steps = 2 * len(tiles)

    def tile_map(place):
        def index(step, tile, scal):
            if which is not None:
                return 0, ((1 - step) ^ scal[0]) * per + tile
            early = place == (1 ^ scal[1])
            used = early == (step < 2)
            now = ((1 - step % 2) ^ scal[0]) * per + tile
            idle = jnp.where(early, scal[0] * per + per - 1, (1 ^ scal[0]) * per)
            return 0, jnp.where(used, now, idle)

        return index

    def out_map(place):
        return lambda step, tile, scal: (
            0,
            jnp.where(step == place, tile, jnp.where(step < place, 0, per - 1)),
        )

    return pl.pallas_call(
        functools.partial(project_kernel, vals.shape[0], which),
        out_shape=[jax.ShapeDtypeStruct((rows, shard), BF16)] * steps,
        grid_spec=pltpu.PrefetchScalarGridSpec(
            num_scalar_prefetch=1,
            grid=(steps, per),
            in_specs=[pl.BlockSpec((rows, shard), lambda step, tile, scal: (0, 0))]
            + [pl.BlockSpec((shard, wide), tile_map(i)) for i in range(len(tiles))]
            + [pl.BlockSpec(vals.shape, lambda step, tile, scal: (0, 0, 0))],
            out_specs=[pl.BlockSpec((rows, wide), out_map(i)) for i in range(steps)],
            scratch_shapes=[pltpu.VMEM((rows, wide), F32)],
        ),
        compiler_params=pltpu.CompilerParams(
            vmem_limit_bytes=VMEM_BYTES, dimension_semantics=("arbitrary", "arbitrary")
        ),
        cost_estimate=pl.CostEstimate(
            flops=2 * rows * shard * shard * steps,
            bytes_accessed=2 * (shard * shard * steps + rows * shard * (1 + steps)),
            transcendentals=0,
        ),
    )(scal, x, *tiles, vals)


def pull_kernel(slots, groups, scal, *refs):
    x_refs, g_refs, w_refs = refs[:2], refs[2:10], refs[10:12]
    vals_ref, own_ref = refs[12], refs[13]
    rest_refs, blocks_ref, acc = refs[14:-2], refs[-2], refs[-1]
    step = pl.program_id(0)
    shard = acc.shape[1]
    half = acc.shape[0] // 2
    apart, far = step // 2, step % 2
    held = apart ^ scal[1]

    @pl.when(step == 0)
    def _():
        acc[...] = jnp.zeros_like(acc)
        blocks_ref[...] = jnp.zeros_like(blocks_ref)

    first = (2 * (scal[2] ^ held) + (far ^ scal[0])) * shard
    for chunk in range(4):

        @pl.when(step == chunk)
        def _():
            pair = g_refs[2 * chunk : 2 * chunk + 2]
            for place, w_ref in enumerate(w_refs):

                @pl.when(held == place)
                def _():
                    for part, g_ref in enumerate(pair):
                        acc[part * half : (part + 1) * half, :] += lax.dot_general(
                            g_ref[...], w_ref[...], (((1,), (1,)), ((), ())), preferred_element_type=F32
                        )

            for slot in range(slots):
                local = scal[5 + 2 * slot] * BLK - first

                @pl.when((slot < scal[3]) & (local >= 0) & (local < shard))
                def _():
                    columns = pl.ds(pl.multiple_of(local, BLK), BLK)
                    rows = pl.ds(pl.multiple_of(scal[4 + 2 * slot] * BLK, BLK), BLK)
                    for part, g_ref in enumerate(pair):
                        g_cols = g_ref[:, columns]
                        acc[part * half : (part + 1) * half, rows] += lax.dot_general(
                            g_cols, vals_ref[slot], (((1,), (1,)), ((), ())), preferred_element_type=F32
                        )
                        blocks_ref[slot] += lax.dot_general(
                            x_refs[part][:, rows], g_cols, (((0,), (0,)), ((), ())), preferred_element_type=F32
                        )

    @pl.when(step == 3)
    def _():
        rows = acc.shape[0] // groups
        own_ref[...] = acc[:rows, :]
        for place, rest_ref in enumerate(rest_refs):
            rest_ref[...] = acc[(place + 1) * rows : (place + 2) * rows, :].astype(BF16)


def pull(scal, x_pair, chunks, tiles, vals, groups):
    half, shard = x_pair[0].shape
    rows = 2 * half // groups

    def tile_map(place):
        def index(step, scal):
            early = place == scal[1]
            used = early == (step < 2)
            idle = jnp.where(early, 1 ^ scal[0], scal[0])
            return 0, jnp.where(used, (step % 2) ^ scal[0], idle)

        return index

    def whole(shape):
        return pl.BlockSpec(shape, lambda step, scal: (0,) * len(shape))

    return pl.pallas_call(
        functools.partial(pull_kernel, vals.shape[0], groups),
        out_shape=[jax.ShapeDtypeStruct((rows, shard), F32)]
        + [jax.ShapeDtypeStruct((rows, shard), BF16)] * (groups - 1)
        + [jax.ShapeDtypeStruct(vals.shape, F32)],
        grid_spec=pltpu.PrefetchScalarGridSpec(
            num_scalar_prefetch=1,
            grid=(4,),
            in_specs=[whole((half, shard))] * 10
            + [pl.BlockSpec((shard, shard), tile_map(i)) for i in range(2)]
            + [whole(vals.shape)],
            out_specs=[whole((rows, shard))] * groups + [whole(vals.shape)],
            scratch_shapes=[pltpu.VMEM((2 * half, shard), F32)],
        ),
        compiler_params=pltpu.CompilerParams(
            vmem_limit_bytes=VMEM_BYTES, dimension_semantics=("arbitrary",)
        ),
        cost_estimate=pl.CostEstimate(
            flops=2 * 2 * half * shard * shard * 4,
            bytes_accessed=2 * (shard * shard * 4 + half * shard * 12),
            transcendentals=0,
        ),
    )(scal, *x_pair, *chunks, *tiles, vals)


def on_device(activations, w_base, blk_vals, blk_index, blk_count, a_down, b_up, grad_out):
    tok_rows = activations.shape[0]
    n_tok = lax.axis_size("tok")
    grad_scale = float(tok_rows * n_tok) ** (-0.5)
    groups = n_tok // 2
    half_groups = groups // 2
    feat_at, tok_at = lax.axis_index("feat"), lax.axis_index("tok")
    row_at, col_at = feat_at // 2, feat_at % 2
    twist = (row_at ^ tok_at) & 1
    turn = (row_at ^ tok_at) >> 1
    scal = jnp.concatenate(
        [
            jnp.stack([col_at, twist, tok_at]).astype(jnp.int32),
            blk_count,
            blk_index.reshape(-1),
        ]
    )

    def joined(parts):
        return parts[0] if len(parts) == 1 else jnp.concatenate(parts, axis=0)

    cot_seen = [grad_out] + [swap(grad_out, "feat", 4 * step) for step in range(1, groups)]
    other_tile = swap(w_base, "tok", 1)
    x_groups = [activations] + [swap(activations, "tok", 2 * j) for j in range(1, groups)]
    x_near, x_far = joined(x_groups[:half_groups]), joined(x_groups[half_groups:])

    low = jnp.concatenate(
        [
            jnp.dot(activations, a_down, preferred_element_type=F32),
            jnp.dot(grad_out, b_up.T, preferred_element_type=F32),
        ],
        axis=1,
    )
    mask = 1
    while mask < lax.axis_size("feat"):
        low = low + swap(low, "feat", mask)
        mask *= 2
    low = low.astype(BF16)
    rank = a_down.shape[1]
    u_half, v_half = low[:, :rank], low[:, rank:]

    cot_own = [pick(cot_seen, turn)]
    for j in range(1, groups):
        cot_own.append(swap(pick(cot_seen, turn ^ j), "tok", 2 * j))
    g_near, g_far = joined(cot_own[:half_groups]), joined(cot_own[half_groups:])

    sums = []
    for which, tile in enumerate((w_base, other_tile)):
        send, keep = project(scal, x_near, [tile], blk_vals, which)
        sums.append(added(keep, swap(send, "feat", 1)))
    far_11, far_10, far_01, far_00 = project(scal, x_far, [w_base, other_tile], blk_vals)
    far_01 = added(far_01, swap(far_11, "feat", 2))
    far_00 = added(far_00, swap(far_10, "feat", 2))
    near = added(pick(sums, twist), swap(pick(sums, 1 ^ twist), "feat", 2))
    far = added(far_00, swap(far_01, "feat", 1))
    parts = [near[j * tok_rows : (j + 1) * tok_rows] for j in range(half_groups)]
    parts += [far[j * tok_rows : (j + 1) * tok_rows] for j in range(half_groups)]
    parts = [parts[0]] + [swap(parts[j], "tok", 2 * j) for j in range(1, groups)]
    total = pick(parts, turn).astype(F32)
    for step in range(1, groups):
        total = total + swap(pick(parts, turn ^ step), "feat", 4 * step).astype(F32)
    projected = (total + jnp.dot(u_half, b_up, preferred_element_type=F32)).astype(BF16)

    g_near_01, g_far_01 = swap(g_near, "feat", 1), swap(g_far, "feat", 1)
    g_near_10, g_far_10 = swap(g_near, "feat", 2), swap(g_far, "feat", 2)
    g_near_11, g_far_11 = swap(g_near_10, "feat", 1), swap(g_far_01, "feat", 2)
    own, *rest, blocks = pull(
        scal,
        (x_near, x_far),
        (g_near, g_far, g_near_01, g_far_01, g_near_10, g_far_10, g_near_11, g_far_11),
        (w_base, other_tile),
        blk_vals,
        groups,
    )
    for j in range(1, groups):
        own = own + swap(rest[j - 1], "tok", 2 * j).astype(F32)
    grad_x = (own + jnp.dot(v_half, a_down.T, preferred_element_type=F32)).astype(BF16)

    blocks = blocks.astype(BF16)
    up = jnp.dot(u_half.T, grad_out, preferred_element_type=F32)
    v_groups = [v_half] + [swap(v_half, "tok", 2 * j) for j in range(1, groups)]
    down = tree_sum(
        [jnp.dot(x.T, v, preferred_element_type=F32) for x, v in zip(x_groups, v_groups)]
    )
    down = down + swap(down, "tok", 1)
    up = up + swap(up, "tok", 1)
    mask = 2
    while mask < n_tok:
        up = up.astype(BF16)
        up = up.astype(F32) + swap(up, "tok", mask).astype(F32)
        blocks = blocks + swap(blocks, "tok", mask)
        mask *= 2
    blocks = blocks.astype(F32) + swap(blocks, "tok", 1).astype(F32)
    return projected, grad_x, blocks * grad_scale, down * grad_scale, up * grad_scale


def solution(mesh):
    in_specs = (
        P("tok", "feat"),
        P("feat", "tok"),
        P("feat", None, None),
        P("feat", None),
        P("feat"),
        P("feat", None),
        P(None, "feat"),
        P("tok", "feat"),
    )
    out_specs = (
        P("tok", "feat"),
        P("tok", "feat"),
        P("feat", None, None),
        P("feat", None),
        P(None, "feat"),
    )
    return jax.shard_map(
        on_device, mesh=mesh, in_specs=in_specs, out_specs=out_specs, check_vma=False
    )
```

time: 287 us -> 107 us (0.37)
  waiting for transfers between devices: 181 us -> 34.9 us
  blocking collectives: 40.1 us -> 0 us
  starting transfers between devices: 0.16 us -> 33.1 us
  matrix products: 29.7 us -> 4.05 us
  Pallas kernels: 0 us -> 23.3 us
  between operations: 18.5 us -> 1.61 us
  other arithmetic: 9.43 us -> 3.75 us
    all_gather x2 -> x0, waiting for transfers between devices: 109 us -> none  [the longest x1 103 us: on_device(): w_rows = lax.all_gather(w_base, 'tok', axis=1, tiled=True)]
    reduce_scatter x1 -> x0, waiting for transfers between devices: 53.2 us -> none  [on_device(): lax.psum_scatter(col_term.astype(jnp.bfloat16), 'feat', scatter_dimension...]
    psum x1 -> x0, blocking collectives: 40.1 us -> none  [on_device(): u_total = lax.psum(u_part, 'feat')]
    ppermute x0 -> x28, waiting for transfers between devices: none -> 34.9 us  [swap(): return lax.ppermute(value, axis, [(i, i ^ mask) for i in range(size)])]
    ppermute x0 -> x28, starting transfers between devices: none -> 33.1 us  [swap(): return lax.ppermute(value, axis, [(i, i ^ mask) for i in range(size)])]
    dot_general x17 -> x7, matrix products: 29.7 us -> 4.05 us  [the longest x1 1.19 us: on_device(): jnp.dot(grad_out, b_up.T, preferred_element_type=F32)]
    pallas_call x0 -> x4, Pallas kernels: none -> 23.3 us  [the longest x3 13.9 us: project(): pl.pallas_call(functools.partial(project_kernel, vals.shape[0], which), o...]
    psum x1 -> x0, waiting for transfers between devices: 16.7 us -> none  [on_device(): lax.psum((block_local, down_local, up_local), 'tok')]
  transfers between devices with their start and end apart: 4 -> 28, of which waited for: 4 -> 12; matrix products, arithmetic and copies ran while one was open for 15% -> 7% of each run, Pallas kernels for 0% -> 22%
where the time goes in v1:
time: 107 us; the launch traced here: 106 us
  waiting for transfers between devices  34.9 us (33%)
  starting transfers between devices  33.1 us (31%)
  Pallas kernels  23.3 us (22%)
  local copies, waits for them, and re-layouts  5.36 us (5%)
  matrix products  4.05 us (4%)
  other arithmetic  3.75 us (4%)
  between operations  1.61 us (2%)
    ppermute x28, waiting for transfers between devices, swap(): return lax.ppermute(value, axis, [(i, i ^ mask) for i in range(size)])  34.9 us
    ppermute x28, starting transfers between devices, swap(): return lax.ppermute(value, axis, [(i, i ^ mask) for i in range(size)])  33.1 us
    pallas_call x3, Pallas kernels, project(): pl.pallas_call(functools.partial(project_kernel, vals.shape[0], which), o...  13.9 us
    pallas_call x1, Pallas kernels, pull(): pl.pallas_call(functools.partial(pull_kernel, vals.shape[0], groups), out...  9.42 us
    unnamed x17, local copies, waits for them, and re-layouts  5.19 us
  transfers between devices with their start and end apart: 28, of which 12 were waited for; matrix products, arithmetic and copies ran while one was open for 7% of the time, Pallas kernels for 22%

profile of v1, /device:TPU:0, one launch (start us, length us, event | category | flops | bytes accessed | tf_op | source)
XLA Modules:
  0.0 106.1 jit_solution(1628683372127221324)
XLA Ops:
  3.9 3.0 %collective-permute-start.10 = (f32[128,128]{0,1:T(8,128)S(1)}, f32[128,128]{0,1:T(8,128)S(1)}, u32[]{:S(2)}, u32[]{:S(2)}) collective-permute-start(f32[128,128]{0,1:T(8,128)S(1)} %pad_maximum_fusion), channel_id=1, source_target_pairs={{0,4},{4,0},{8,12},{12,8},{16,20},{20,16},{24,28},{28,24},{1,5},{5... | collective-permute-start | bytes 196616 | tf_op jit(solution)/shard_map/ppermute | solution.py:18
  6.9 2.2 %collective-permute-done.10 = f32[128,128]{0,1:T(8,128)S(1)} collective-permute-done((f32[128,128]{0,1:T(8,128)S(1)}, f32[128,128]{0,1:T(8,128)S(1)}, u32[]{:S(2)}, u32[]{:S(2)}) %collective-permute-start.10) | collective-permute-done | bytes 65568 | tf_op jit(solution)/shard_map/ppermute | solution.py:18
  9.2 2.2 %collective-permute-start.11 = (f32[128,128]{0,1:T(8,128)S(1)}, f32[128,128]{0,1:T(8,128)S(1)}, u32[]{:S(2)}, u32[]{:S(2)}) collective-permute-start(f32[128,128]{0,1:T(8,128)S(1)} %fusion.10), channel_id=1, source_target_pairs={{0,8},{4,12},{8,0},{12,4},{16,24},{20,28},{24,16},{28,20},{1,9},{5... | collective-permute-start | bytes 196616 | tf_op jit(solution)/shard_map/ppermute | solution.py:18
  11.3 2.2 %collective-permute-done.11 = f32[128,128]{0,1:T(8,128)S(1)} collective-permute-done((f32[128,128]{0,1:T(8,128)S(1)}, f32[128,128]{0,1:T(8,128)S(1)}, u32[]{:S(2)}, u32[]{:S(2)}) %collective-permute-start.11) | collective-permute-done | bytes 65568 | tf_op jit(solution)/shard_map/ppermute | solution.py:18
  13.6 3.1 %collective-permute-start.12 = (f32[128,128]{0,1:T(8,128)S(1)}, f32[128,128]{0,1:T(8,128)S(1)}, u32[]{:S(2)}, u32[]{:S(2)}) collective-permute-start(f32[128,128]{0,1:T(8,128)S(1)} %add.74), channel_id=1, source_target_pairs={{0,16},{4,20},{8,24},{12,28},{16,0},{20,4},{24,8},{28,12},{1,17},{... | collective-permute-start | bytes 196616 | tf_op jit(solution)/shard_map/ppermute | solution.py:18
  16.8 1.8 %collective-permute-start = (bf16[128,1024]{1,0:T(8,128)(2,1)}, bf16[128,1024]{1,0:T(8,128)(2,1)S(1)}, u32[]{:S(2)}, u32[]{:S(2)}) collective-permute-start(bf16[128,1024]{1,0:T(8,128)(2,1)} %refs_0_.5), channel_id=1, source_target_pairs={{0,2},{1,3},{2,0},{3,1},{4,6},{5,7},{6,4},{7,5},{8,10},{9,11},{10,... | collective-permute-start | bytes 786440 | tf_op jit(solution)/shard_map/ppermute | solution.py:18
  20.2 2.2 %copy-done.1 = bf16[1024,2048]{1,0:T(8,128)(2,1)S(1)} copy-done((bf16[1024,2048]{1,0:T(8,128)(2,1)S(1)}, bf16[1024,2048]{1,0:T(8,128)(2,1)}, u32[]{:S(2)}) %copy-start.1) | copy-done | bytes 4194328
  24.2 2.5 %shard_map.121 = (bf16[128,1024]{1,0:T(8,128)(2,1)S(1)}, bf16[128,1024]{1,0:T(8,128)(2,1)S(1)}) custom-call(s32[10]{0:T(128)S(1)} %concatenate.6.scal, bf16[128,1024]{1,0:T(8,128)(2,1)S(1)} %copy-done.3, bf16[1024,2048]{1,0:T(8,128)(2,1)S(1)} %copy-done.1, bf16[3,128,128]{2,1,0:T(8,128)(2,1)S(1)} %copy-done.5), custom_call_target="tpu_custom_call" | custom-call | flops 536870912 | bytes 4980736 | tf_op jit(solution)/shard_map/pallas_call | solution.py:93
  28.1 2.2 %collective-permute-done.13 = bf16[128,1024]{1,0:T(8,128)(2,1)S(1)} collective-permute-done((bf16[128,1024]{1,0:T(8,128)(2,1)}, bf16[128,1024]{1,0:T(8,128)(2,1)S(1)}, u32[]{:S(2)}, u32[]{:S(2)}) %collective-permute-start.13) | collective-permute-done | bytes 262176 | tf_op jit(solution)/shard_map/ppermute | solution.py:18
  30.3 1.6 %collective-permute-start.14 = (bf16[128,1024]{1,0:T(8,128)(2,1)S(1)}, bf16[128,1024]{1,0:T(8,128)(2,1)S(1)}, u32[]{:S(2)}, u32[]{:S(2)}) collective-permute-start(bf16[128,1024]{1,0:T(8,128)(2,1)S(1)} %get-tuple-element.29), channel_id=1, source_target_pairs={{0,2},{1,3},{2,0},{3,1},{4,6},{5,7},{6,4},{7,5},{8,10},{9,11},{10,... | collective-permute-start | bytes 786440 | tf_op jit(solution)/shard_map/ppermute | solution.py:18
  32.3 1.6 %collective-permute-start.15 = (bf16[128,1024]{1,0:T(8,128)(2,1)S(1)}, bf16[128,1024]{1,0:T(8,128)(2,1)S(1)}, u32[]{:S(2)}, u32[]{:S(2)}) collective-permute-start(bf16[128,1024]{1,0:T(8,128)(2,1)S(1)} %get-tuple-element.30.refs_2_), channel_id=1, source_target_pairs={{0,4},{4,0},{8,12},{12,8},{16,20},{20,16},{24,28},{28,24},{1,5},{5... | collective-permute-start | bytes 786440 | tf_op jit(solution)/shard_map/ppermute | solution.py:18
  34.1 3.4 %collective-permute-done.14.refs_3_ = bf16[128,1024]{1,0:T(8,128)(2,1)S(1)} collective-permute-done((bf16[128,1024]{1,0:T(8,128)(2,1)S(1)}, bf16[128,1024]{1,0:T(8,128)(2,1)S(1)}, u32[]{:S(2)}, u32[]{:S(2)}) %collective-permute-start.14) | collective-permute-done | bytes 262176 | tf_op jit(solution)/shard_map/ppermute | solution.py:18
  38.9 2.0 %collective-permute-done.17.refs_6_ = bf16[128,1024]{1,0:T(8,128)(2,1)S(1)} collective-permute-done((bf16[128,1024]{1,0:T(8,128)(2,1)S(1)}, bf16[128,1024]{1,0:T(8,128)(2,1)S(1)}, u32[]{:S(2)}, u32[]{:S(2)}) %collective-permute-start.17) | collective-permute-done | bytes 262176 | tf_op jit(solution)/shard_map/ppermute | solution.py:18
  41.2 5.4 %collective-permute-done.16.refs_5_ = bf16[128,1024]{1,0:T(8,128)(2,1)S(1)} collective-permute-done((bf16[128,1024]{1,0:T(8,128)(2,1)S(1)}, bf16[128,1024]{1,0:T(8,128)(2,1)S(1)}, u32[]{:S(2)}, u32[]{:S(2)}) %collective-permute-start.16) | collective-permute-done | bytes 262176 | tf_op jit(solution)/shard_map/ppermute | solution.py:18
  48.1 1.7 %collective-permute-start.20 = (bf16[128,1024]{1,0:T(8,128)(2,1)S(1)}, bf16[128,1024]{1,0:T(8,128)(2,1)S(1)}, u32[]{:S(2)}, u32[]{:S(2)}) collective-permute-start(bf16[128,1024]{1,0:T(8,128)(2,1)S(1)} %collective-permute-done.16.refs_5_), channel_id=1, source_target_pairs={{0,8},{4,12},{8,0},{12,4},{16,24},{20,28},{24,16},{28,20},{1,9},{5... | collective-permute-start | bytes 786440 | tf_op jit(solution)/shard_map/ppermute | solution.py:18
  49.8 7.0 %shard_map.119 = (bf16[128,1024]{1,0:T(8,128)(2,1)S(1)}, bf16[128,1024]{1,0:T(8,128)(2,1)S(1)}, bf16[128,1024]{1,0:T(8,128)(2,1)S(1)}, bf16[128,1024]{1,0:T(8,128)(2,1)S(1)}) custom-call(s32[10]{0:T(128)S(1)} %concatenate.6.scal, bf16[128,1024]{1,0:T(8,128)(2,1)S(1)} %collective-permute-done.x_ref.refs_1_, bf16[1024,2048]{1,0:T(8,128)(2,1)S(1)} %copy-done.2, ...), custom_call_target="tpu_custom_call" | custom-call | flops 1073741824 | bytes 9699328 | tf_op jit(solution)/shard_map/pallas_call | solution.py:93
  59.7 9.4 %shard_map.122 = (f32[128,1024]{1,0:T(8,128)S(1)}, bf16[128,1024]{1,0:T(8,128)(2,1)S(1)}, f32[3,128,128]{2,1,0:T(8,128)S(1)}) custom-call(s32[10]{0:T(128)S(1)} %concatenate.6.scal, bf16[128,1024]{1,0:T(8,128)(2,1)S(1)} %copy-done.4, bf16[128,1024]{1,0:T(8,128)(2,1)S(1)} %collective-permute-done.x_ref.refs_1_, ...), custom_call_target="tpu_custom_call" | custom-call | flops 2147483648 | bytes 11534336 | tf_op jit(solution)/shard_map/pallas_call | solution.py:186
  69.1 2.0 %collective-permute-start.22 = (bf16[3,128,128]{2,1,0:T(8,128)(2,1)S(1)}, bf16[3,128,128]{2,1,0:T(8,128)(2,1)S(1)}, u32[]{:S(2)}, u32[]{:S(2)}) collective-permute-start(bf16[3,128,128]{2,1,0:T(8,128)(2,1)S(1)} %convert_element_type.114), channel_id=1, source_target_pairs={{0,2},{1,3},{2,0},{3,1},{4,6},{5,7},{6,4},{7,5},{8,10},{9,11},{10,... | collective-permute-start | bytes 294920 | tf_op jit(solution)/shard_map/ppermute | solution.py:18
  71.1 4.3 %shard_map.120 = (bf16[128,1024]{1,0:T(8,128)(2,1)S(1)}, bf16[128,1024]{1,0:T(8,128)(2,1)S(1)}) custom-call(s32[10]{0:T(128)S(1)} %concatenate.6.scal, bf16[128,1024]{1,0:T(8,128)(2,1)S(1)} %copy-done.4, bf16[1024,2048]{1,0:T(8,128)(2,1)} %collective-permute-done.1.refs_1_.refs_0_.refs_11_, bf16[3,128,128]{2,1,0:T(8,128)(2,1)S(1)} %copy-done.5), custom_call_target="tpu_custom_call" | custom-call | flops 536870912 | bytes 4980736 | tf_op jit(solution)/shard_map/pallas_call | solution.py:93
  78.9 5.1 %collective-permute-done.6 = bf16[128,1024]{1,0:T(8,128)(2,1)S(1)} collective-permute-done((bf16[128,1024]{1,0:T(8,128)(2,1)S(1)}, bf16[128,1024]{1,0:T(8,128)(2,1)S(1)}, u32[]{:S(2)}, u32[]{:S(2)}) %collective-permute-start.6) | collective-permute-done | bytes 262176 | tf_op jit(solution)/shard_map/ppermute | solution.py:18
  84.2 1.9 %collective-permute-start.8 = (bf16[128,1024]{1,0:T(8,128)(2,1)S(1)}, bf16[128,1024]{1,0:T(8,128)(2,1)S(1)}, u32[]{:S(2)}, u32[]{:S(2)}) collective-permute-start(bf16[128,1024]{1,0:T(8,128)(2,1)S(1)} %broadcast_select_fusion.2), channel_id=1, source_target_pairs={{0,8},{4,12},{8,0},{12,4},{16,24},{20,28},{24,16},{28,20},{1,9},{5... | collective-permute-start | bytes 786440 | tf_op jit(solution)/shard_map/ppermute | solution.py:18
  90.6 4.1 %collective-permute-done.5 = bf16[128,1024]{1,0:T(8,128)(2,1)S(1)} collective-permute-done((bf16[128,1024]{1,0:T(8,128)(2,1)S(1)}, bf16[128,1024]{1,0:T(8,128)(2,1)S(1)}, u32[]{:S(2)}, u32[]{:S(2)}) %collective-permute-start.5) | collective-permute-done | bytes 262176 | tf_op jit(solution)/shard_map/ppermute | solution.py:18
  95.0 2.0 %collective-permute-start.9 = (bf16[128,1024]{1,0:T(8,128)(2,1)S(1)}, bf16[128,1024]{1,0:T(8,128)(2,1)S(1)}, u32[]{:S(2)}, u32[]{:S(2)}) collective-permute-start(bf16[128,1024]{1,0:T(8,128)(2,1)S(1)} %get-tuple-element.27), channel_id=1, source_target_pairs={{0,16},{4,20},{8,24},{12,28},{16,0},{20,4},{24,8},{28,12},{1,17},{... | collective-permute-start | bytes 786440 | tf_op jit(solution)/shard_map/ppermute | solution.py:18
  98.3 6.8 %collective-permute-done.9 = bf16[128,1024]{1,0:T(8,128)(2,1)S(1)} collective-permute-done((bf16[128,1024]{1,0:T(8,128)(2,1)S(1)}, bf16[128,1024]{1,0:T(8,128)(2,1)S(1)}, u32[]{:S(2)}, u32[]{:S(2)}) %collective-permute-start.9) | collective-permute-done | bytes 262176 | tf_op jit(solution)/shard_map/ppermute | solution.py:18
  (79 shorter events, 24.8 us)
Async XLA Ops:
  0.7 47.4 %collective-permute-start.1 = (bf16[1024,2048]{1,0:T(8,128)(2,1)}, bf16[1024,2048]{1,0:T(8,128)(2,1)}, u32[]{:S(2)}, u32[]{:S(2)}) collective-permute-start(bf16[1024,2048]{1,0:T(8,128)(2,1)} %refs_10_.1), channel_id=1, source_target_pairs={{0,1},{1,0},{2,3},{3,2},{4,5},{5,4},{6,7},{7,6},{8,9},{9,8},{10,11... | collective-permute-start | bytes 12582920 | tf_op jit(solution)/shard_map/ppermute | solution.py:18
  13.6 13.1 %collective-permute-start.12 = (f32[128,128]{0,1:T(8,128)S(1)}, f32[128,128]{0,1:T(8,128)S(1)}, u32[]{:S(2)}, u32[]{:S(2)}) collective-permute-start(f32[128,128]{0,1:T(8,128)S(1)} %add.74), channel_id=1, source_target_pairs={{0,16},{4,20},{8,24},{12,28},{16,0},{20,4},{24,8},{28,12},{1,17},{... | collective-permute-start | bytes 196616 | tf_op jit(solution)/shard_map/ppermute | solution.py:18
  16.7 13.6 %collective-permute-start.13 = (bf16[128,1024]{1,0:T(8,128)(2,1)}, bf16[128,1024]{1,0:T(8,128)(2,1)S(1)}, u32[]{:S(2)}, u32[]{:S(2)}) collective-permute-start(bf16[128,1024]{1,0:T(8,128)(2,1)} %param.15), channel_id=1, source_target_pairs={{0,16},{4,20},{8,24},{12,28},{16,0},{20,4},{24,8},{28,12},{1,17},{... | collective-permute-start | bytes 786440 | tf_op jit(solution)/shard_map/ppermute | solution.py:18
  16.8 15.5 %collective-permute-start = (bf16[128,1024]{1,0:T(8,128)(2,1)}, bf16[128,1024]{1,0:T(8,128)(2,1)S(1)}, u32[]{:S(2)}, u32[]{:S(2)}) collective-permute-start(bf16[128,1024]{1,0:T(8,128)(2,1)} %refs_0_.5), channel_id=1, source_target_pairs={{0,2},{1,3},{2,0},{3,1},{4,6},{5,7},{6,4},{7,5},{8,10},{9,11},{10,... | collective-permute-start | bytes 786440 | tf_op jit(solution)/shard_map/ppermute | solution.py:18
  30.3 7.2 %collective-permute-start.14 = (bf16[128,1024]{1,0:T(8,128)(2,1)S(1)}, bf16[128,1024]{1,0:T(8,128)(2,1)S(1)}, u32[]{:S(2)}, u32[]{:S(2)}) collective-permute-start(bf16[128,1024]{1,0:T(8,128)(2,1)S(1)} %get-tuple-element.29), channel_id=1, source_target_pairs={{0,2},{1,3},{2,0},{3,1},{4,6},{5,7},{6,4},{7,5},{8,10},{9,11},{10,... | collective-permute-start | bytes 786440 | tf_op jit(solution)/shard_map/ppermute | solution.py:18
  32.1 6.7 %collective-permute-start.26 = (f32[64,1024]{1,0:T(8,128)S(1)}, f32[64,1024]{1,0:T(8,128)S(1)}, u32[]{:S(2)}, u32[]{:S(2)}) collective-permute-start(f32[64,1024]{1,0:T(8,128)S(1)} %fusion.1), channel_id=1, source_target_pairs={{0,1},{1,0},{2,3},{3,2},{4,5},{5,4},{6,7},{7,6},{8,9},{9,8},{10,11... | collective-permute-start | bytes 786440 | tf_op jit(solution)/shard_map/ppermute | solution.py:18
  32.2 8.7 %collective-permute-start.17 = (bf16[128,1024]{1,0:T(8,128)(2,1)S(1)}, bf16[128,1024]{1,0:T(8,128)(2,1)S(1)}, u32[]{:S(2)}, u32[]{:S(2)}) collective-permute-start(bf16[128,1024]{1,0:T(8,128)(2,1)S(1)} %get-tuple-element.30.refs_2_), channel_id=1, source_target_pairs={{0,8},{4,12},{8,0},{12,4},{16,24},{20,28},{24,16},{28,20},{1,9},{5... | collective-permute-start | bytes 786440 | tf_op jit(solution)/shard_map/ppermute | solution.py:18
  32.3 26.2 %collective-permute-start.15 = (bf16[128,1024]{1,0:T(8,128)(2,1)S(1)}, bf16[128,1024]{1,0:T(8,128)(2,1)S(1)}, u32[]{:S(2)}, u32[]{:S(2)}) collective-permute-start(bf16[128,1024]{1,0:T(8,128)(2,1)S(1)} %get-tuple-element.30.refs_2_), channel_id=1, source_target_pairs={{0,4},{4,0},{8,12},{12,8},{16,20},{20,16},{24,28},{28,24},{1,5},{5... | collective-permute-start | bytes 786440 | tf_op jit(solution)/shard_map/ppermute | solution.py:18
  37.5 9.1 %collective-permute-start.16 = (bf16[128,1024]{1,0:T(8,128)(2,1)S(1)}, bf16[128,1024]{1,0:T(8,128)(2,1)S(1)}, u32[]{:S(2)}, u32[]{:S(2)}) collective-permute-start(bf16[128,1024]{1,0:T(8,128)(2,1)S(1)} %collective-permute-done.14.refs_3_), channel_id=1, source_target_pairs={{0,4},{4,0},{8,12},{12,8},{16,20},{20,16},{24,28},{28,24},{1,5},{5... | collective-permute-start | bytes 786440 | tf_op jit(solution)/shard_map/ppermute | solution.py:18
  38.8 18.0 %collective-permute-start.25 = (f32[1024,64]{0,1:T(8,128)S(1)}, f32[1024,64]{0,1:T(8,128)S(1)}, u32[]{:S(2)}, u32[]{:S(2)}) collective-permute-start(f32[1024,64]{0,1:T(8,128)S(1)} %fusion), channel_id=1, source_target_pairs={{0,1},{1,0},{2,3},{3,2},{4,5},{5,4},{6,7},{7,6},{8,9},{9,8},{10,11... | collective-permute-start | bytes 786440 | tf_op jit(solution)/shard_map/ppermute | solution.py:18
  40.9 18.4 %collective-permute-start.18 = (bf16[128,1024]{1,0:T(8,128)(2,1)S(1)}, bf16[128,1024]{1,0:T(8,128)(2,1)S(1)}, u32[]{:S(2)}, u32[]{:S(2)}) collective-permute-start(bf16[128,1024]{1,0:T(8,128)(2,1)S(1)} %collective-permute-done.14.refs_3_), channel_id=1, source_target_pairs={{0,8},{4,12},{8,0},{12,4},{16,24},{20,28},{24,16},{28,20},{1,9},{5... | collective-permute-start | bytes 786440 | tf_op jit(solution)/shard_map/ppermute | solution.py:18
  46.6 13.0 %collective-permute-start.19 = (bf16[128,1024]{1,0:T(8,128)(2,1)S(1)}, bf16[128,1024]{1,0:T(8,128)(2,1)S(1)}, u32[]{:S(2)}, u32[]{:S(2)}) collective-permute-start(bf16[128,1024]{1,0:T(8,128)(2,1)S(1)} %collective-permute-done.17.refs_6_), channel_id=1, source_target_pairs={{0,4},{4,0},{8,12},{12,8},{16,20},{20,16},{24,28},{28,24},{1,5},{5... | collective-permute-start | bytes 786440 | tf_op jit(solution)/shard_map/ppermute | solution.py:18
  48.1 11.6 %collective-permute-start.20 = (bf16[128,1024]{1,0:T(8,128)(2,1)S(1)}, bf16[128,1024]{1,0:T(8,128)(2,1)S(1)}, u32[]{:S(2)}, u32[]{:S(2)}) collective-permute-start(bf16[128,1024]{1,0:T(8,128)(2,1)S(1)} %collective-permute-done.16.refs_5_), channel_id=1, source_target_pairs={{0,8},{4,12},{8,0},{12,4},{16,24},{20,28},{24,16},{28,20},{1,9},{5... | collective-permute-start | bytes 786440 | tf_op jit(solution)/shard_map/ppermute | solution.py:18
  56.8 19.9 %collective-permute-start.3 = (bf16[128,1024]{1,0:T(8,128)(2,1)S(1)}, bf16[128,1024]{1,0:T(8,128)(2,1)S(1)}, u32[]{:S(2)}, u32[]{:S(2)}) collective-permute-start(bf16[128,1024]{1,0:T(8,128)(2,1)S(1)} %get-tuple-element.19), channel_id=1, source_target_pairs={{0,8},{4,12},{8,0},{12,4},{16,24},{20,28},{24,16},{28,20},{1,9},{5... | collective-permute-start | bytes 786440 | tf_op jit(solution)/shard_map/ppermute | solution.py:18
  58.5 20.3 %collective-permute-start.7 = (bf16[128,1024]{1,0:T(8,128)(2,1)S(1)}, bf16[128,1024]{1,0:T(8,128)(2,1)S(1)}, u32[]{:S(2)}, u32[]{:S(2)}) collective-permute-start(bf16[128,1024]{1,0:T(8,128)(2,1)S(1)} %get-tuple-element.23), channel_id=1, source_target_pairs={{0,4},{4,0},{8,12},{12,8},{16,20},{20,16},{24,28},{28,24},{1,5},{5... | collective-permute-start | bytes 786440 | tf_op jit(solution)/shard_map/ppermute | solution.py:18
  59.3 28.3 %collective-permute-start.27 = (bf16[64,1024]{1,0:T(8,128)(2,1)S(1)}, bf16[64,1024]{1,0:T(8,128)(2,1)S(1)}, u32[]{:S(2)}, u32[]{:S(2)}) collective-permute-start(bf16[64,1024]{1,0:T(8,128)(2,1)S(1)} %add_convert_fusion.8), channel_id=1, source_target_pairs={{0,2},{1,3},{2,0},{3,1},{4,6},{5,7},{6,4},{7,5},{8,10},{9,11},{10,... | collective-permute-start | bytes 393224 | tf_op jit(solution)/shard_map/ppermute | solution.py:18
  69.1 8.8 %collective-permute-start.22 = (bf16[3,128,128]{2,1,0:T(8,128)(2,1)S(1)}, bf16[3,128,128]{2,1,0:T(8,128)(2,1)S(1)}, u32[]{:S(2)}, u32[]{:S(2)}) collective-permute-start(bf16[3,128,128]{2,1,0:T(8,128)(2,1)S(1)} %convert_element_type.114), channel_id=1, source_target_pairs={{0,2},{1,3},{2,0},{3,1},{4,6},{5,7},{6,4},{7,5},{8,10},{9,11},{10,... | collective-permute-start | bytes 294920 | tf_op jit(solution)/shard_map/ppermute | solution.py:18
  75.4 8.6 %collective-permute-start.6 = (bf16[128,1024]{1,0:T(8,128)(2,1)S(1)}, bf16[128,1024]{1,0:T(8,128)(2,1)S(1)}, u32[]{:S(2)}, u32[]{:S(2)}) collective-permute-start(bf16[128,1024]{1,0:T(8,128)(2,1)S(1)} %get-tuple-element.21), channel_id=1, source_target_pairs={{0,4},{4,0},{8,12},{12,8},{16,20},{20,16},{24,28},{28,24},{1,5},{5... | collective-permute-start | bytes 786440 | tf_op jit(solution)/shard_map/ppermute | solution.py:18
  76.7 9.4 %collective-permute-start.2 = (bf16[128,1024]{1,0:T(8,128)(2,1)S(1)}, bf16[128,1024]{1,0:T(8,128)(2,1)S(1)}, u32[]{:S(2)}, u32[]{:S(2)}) collective-permute-start(bf16[128,1024]{1,0:T(8,128)(2,1)S(1)} %get-tuple-element.17), channel_id=1, source_target_pairs={{0,8},{4,12},{8,0},{12,4},{16,24},{20,28},{24,16},{28,20},{1,9},{5... | collective-permute-start | bytes 786440 | tf_op jit(solution)/shard_map/ppermute | solution.py:18
  77.9 8.9 %collective-permute-start.4 = (bf16[128,1024]{1,0:T(8,128)(2,1)S(1)}, bf16[128,1024]{1,0:T(8,128)(2,1)S(1)}, u32[]{:S(2)}, u32[]{:S(2)}) collective-permute-start(bf16[128,1024]{1,0:T(8,128)(2,1)S(1)} %add_convert_fusion.6), channel_id=1, source_target_pairs={{0,4},{4,0},{8,12},{12,8},{16,20},{20,16},{24,28},{28,24},{1,5},{5... | collective-permute-start | bytes 786440 | tf_op jit(solution)/shard_map/ppermute | solution.py:18
  78.9 10.9 %collective-permute-start.23 = (bf16[3,128,128]{2,1,0:T(8,128)(2,1)S(1)}, bf16[3,128,128]{2,1,0:T(8,128)(2,1)S(1)}, u32[]{:S(2)}, u32[]{:S(2)}) collective-permute-start(bf16[3,128,128]{2,1,0:T(8,128)(2,1)S(1)} %convert_add_fusion), channel_id=1, source_target_pairs={{0,1},{1,0},{2,3},{3,2},{4,5},{5,4},{6,7},{7,6},{8,9},{9,8},{10,11... | collective-permute-start | bytes 294920 | tf_op jit(solution)/shard_map/ppermute | solution.py:18
  87.0 7.8 %collective-permute-start.5 = (bf16[128,1024]{1,0:T(8,128)(2,1)S(1)}, bf16[128,1024]{1,0:T(8,128)(2,1)S(1)}, u32[]{:S(2)}, u32[]{:S(2)}) collective-permute-start(bf16[128,1024]{1,0:T(8,128)(2,1)S(1)} %add_convert_fusion.5), channel_id=1, source_target_pairs={{0,2},{1,3},{2,0},{3,1},{4,6},{5,7},{6,4},{7,5},{8,10},{9,11},{10,... | collective-permute-start | bytes 786440 | tf_op jit(solution)/shard_map/ppermute | solution.py:18
  88.4 9.1 %collective-permute-start.21 = (bf16[128,1024]{1,0:T(8,128)(2,1)S(1)}, bf16[128,1024]{1,0:T(8,128)(2,1)S(1)}, u32[]{:S(2)}, u32[]{:S(2)}) collective-permute-start(bf16[128,1024]{1,0:T(8,128)(2,1)S(1)} %get-tuple-element.25), channel_id=1, source_target_pairs={{0,2},{1,3},{2,0},{3,1},{4,6},{5,7},{6,4},{7,5},{8,10},{9,11},{10,... | collective-permute-start | bytes 786440 | tf_op jit(solution)/shard_map/ppermute | solution.py:18
  95.0 10.1 %collective-permute-start.9 = (bf16[128,1024]{1,0:T(8,128)(2,1)S(1)}, bf16[128,1024]{1,0:T(8,128)(2,1)S(1)}, u32[]{:S(2)}, u32[]{:S(2)}) collective-permute-start(bf16[128,1024]{1,0:T(8,128)(2,1)S(1)} %get-tuple-element.27), channel_id=1, source_target_pairs={{0,16},{4,20},{8,24},{12,28},{16,0},{20,4},{24,8},{28,12},{1,17},{... | collective-permute-start | bytes 786440 | tf_op jit(solution)/shard_map/ppermute | solution.py:18
  (12 other events, 132.1 us)

commit v2 on v0

v2 whole, which is shorter than its diff:
```python
import functools

import jax
import jax.numpy as jnp
from jax import lax
from jax.experimental import pallas as pl
from jax.experimental.pallas import tpu as pltpu
from jax.sharding import PartitionSpec as P

BLK = 128
F32 = jnp.float32
BF16 = jnp.bfloat16
VMEM_BYTES = 32 * 1024 * 1024


def swap(value, axis, mask):
    size = lax.axis_size(axis)
    return lax.ppermute(value, axis, [(i, i ^ mask) for i in range(size)])


def tree_sum(terms):
    while len(terms) > 1:
        terms = [terms[i] + terms[i + 1] for i in range(0, len(terms), 2)]
    return terms[0]


def pick(options, index):
    value = options[0]
    for place in range(1, len(options)):
        value = jnp.where(index == place, options[place], value)
    return value


def after(value, *others):
    return lax.optimization_barrier((value, *others))[0]


def added(left, right):
    return (left.astype(F32) + right.astype(F32)).astype(BF16)


def position():
    feat_at, tok_at = lax.axis_index("feat"), lax.axis_index("tok")
    return feat_at // 2, feat_at % 2, tok_at


def call(kernel, out_shapes, scratch, flops, scalars, arrays):
    space = pl.BlockSpec(memory_space=pltpu.VMEM)
    shapes = [jax.ShapeDtypeStruct(shape, dtype) for shape, dtype in out_shapes]
    size = sum(a.size * a.dtype.itemsize for a in arrays)
    return pl.pallas_call(
        kernel,
        out_shape=shapes,
        in_specs=[pl.BlockSpec(memory_space=pltpu.SMEM)] * len(scalars) + [space] * len(arrays),
        out_specs=[space] * len(shapes),
        scratch_shapes=[pltpu.VMEM(shape, dtype) for shape, dtype in scratch],
        compiler_params=pltpu.CompilerParams(vmem_limit_bytes=VMEM_BYTES),
        cost_estimate=pl.CostEstimate(flops=flops, bytes_accessed=size, transcendentals=0),
    )(*scalars, *arrays)


def for_slots(index_ref, count_ref, slots, first, wide, body):
    for slot in range(slots):
        local = index_ref[1, slot] * BLK - first

        @pl.when((slot < count_ref[0]) & (local >= 0) & (local < wide))
        def _():
            rows = pl.ds(pl.multiple_of(index_ref[0, slot] * BLK, BLK), BLK)
            body(slot, rows, pl.ds(pl.multiple_of(local, BLK), BLK))


def low_kernel(x_ref, g_ref, down_ref, up_ref, out_ref):
    rank = up_ref.shape[0]
    nt = (((1,), (1,)), ((), ()))
    out_ref[:, :rank] = lax.dot_general(x_ref[...], down_ref[...], nt, preferred_element_type=F32)
    out_ref[:, rank:] = lax.dot_general(g_ref[...], up_ref[...], nt, preferred_element_type=F32)


def project(index_ref, count_ref, x_ref, w_ref, vals_ref, acc, held, half):
    shard = x_ref.shape[1]
    columns = pl.ds(pl.multiple_of(half * shard, shard), shard)
    acc[...] = jnp.dot(x_ref[...], w_ref[:, columns], preferred_element_type=F32)

    def body(slot, rows, columns):
        acc[:, columns] += jnp.dot(x_ref[:, rows], vals_ref[slot], preferred_element_type=F32)

    first = (2 * held + half) * shard
    for_slots(index_ref, count_ref, vals_ref.shape[0], first, shard, body)


def own_kernel(index_ref, count_ref, x_ref, w_ref, vals_ref, send_ref, keep_ref, acc):
    _, c, t = position()
    for p, out_ref in ((1, send_ref), (0, keep_ref)):
        project(index_ref, count_ref, x_ref, w_ref, vals_ref, acc, t, p ^ c)
        out_ref[...] = acc[...].astype(BF16)


def rest_kernel(index_ref, count_ref, near_ref, far_ref, own_ref, other_ref, vals_ref, *refs):
    far_refs, near_refs, both, acc, acc_far = refs[:4], refs[4:6], refs[6], refs[7], refs[8]
    r, c, t = position()
    twist = (r ^ t) & 1
    rows = far_ref.shape[0]
    both[:rows, :] = far_ref[...]
    both[rows:, :] = near_ref[...]
    for tile in (1, 0):
        for p in (1, 0):
            x_ref, w_ref, into = (both, other_ref, acc) if tile else (far_ref, own_ref, acc_far)
            project(index_ref, count_ref, x_ref, w_ref, vals_ref, into, t ^ tile, p ^ c)
            if tile:
                near_refs[1 - p][...] = into[rows:, :].astype(BF16)
            for q in (1, 0):

                @pl.when(q ^ twist == tile)
                def _():
                    far_refs[2 * (1 - q) + 1 - p][...] = into[:rows, :].astype(BF16)


def pull(index_ref, count_ref, x_refs, g_refs, w_refs, vals_ref, acc, both, blocks_ref, q, p):
    r, c, t = position()
    held = q ^ ((r ^ t) & 1)
    half = p ^ c
    rows, shard = x_refs[0].shape
    nt = (((1,), (1,)), ((), ()))
    tn = (((0,), (0,)), ((), ()))
    for part in range(2):
        both[part * rows : (part + 1) * rows, :] = g_refs[part][...]
    columns = pl.ds(pl.multiple_of(half * shard, shard), shard)
    for tile, w_ref in enumerate(w_refs):

        @pl.when(held == tile)
        def _():
            acc[...] += lax.dot_general(both[...], w_ref[:, columns], nt, preferred_element_type=F32)

    def body(slot, block_rows, block_columns):
        g_columns = both[:, block_columns]
        acc[:, block_rows] += lax.dot_general(g_columns, vals_ref[slot], nt, preferred_element_type=F32)
        for part in range(2):
            blocks_ref[slot] += lax.dot_general(
                x_refs[part][:, block_rows],
                g_columns[part * rows : (part + 1) * rows],
                tn,
                preferred_element_type=F32,
            )

    first = (2 * (t ^ held) + half) * shard
    for_slots(index_ref, count_ref, vals_ref.shape[0], first, shard, body)


def early_kernel(index_ref, count_ref, *refs):
    x_refs, g_refs, w_refs = refs[:2], refs[2:8], refs[8:10]
    vals_ref, acc, blocks_ref, both = refs[10:]
    acc[...] = jnp.zeros_like(acc)
    blocks_ref[...] = jnp.zeros_like(blocks_ref)
    for place, (q, p) in enumerate(((0, 0), (0, 1), (1, 0))):
        pair = g_refs[2 * place : 2 * place + 2]
        pull(index_ref, count_ref, x_refs, pair, w_refs, vals_ref, acc, both, blocks_ref, q, p)


def late_kernel(index_ref, count_ref, *refs):
    x_refs, g_refs, w_refs = refs[:2], refs[2:4], refs[4:6]
    vals_ref, acc_in, blocks_in = refs[6:9]
    own_ref, *rest_refs, blocks_ref, acc, both = refs[9:]
    acc[...] = acc_in[...]
    blocks_ref[...] = blocks_in[...]
    pull(index_ref, count_ref, x_refs, g_refs, w_refs, vals_ref, acc, both, blocks_ref, 1, 1)
    rows = own_ref.shape[0]
    own_ref[...] = acc[:rows, :]
    for place, rest_ref in enumerate(rest_refs):
        rest_ref[...] = acc[(place + 1) * rows : (place + 2) * rows, :].astype(BF16)


def on_device(activations, w_base, blk_vals, blk_index, blk_count, a_down, b_up, grad_out):
    tok_rows, shard = activations.shape
    n_tok = lax.axis_size("tok")
    grad_scale = float(tok_rows * n_tok) ** (-0.5)
    groups = n_tok // 2
    half_groups = groups // 2
    set_rows = half_groups * tok_rows
    rank = a_down.shape[1]
    r, c, t = position()
    twist = (r ^ t) & 1
    turn = (r ^ t) >> 1
    scalars = (blk_index.T, blk_count)
    product = 2 * set_rows * shard * shard

    def joined(parts):
        return parts[0] if len(parts) == 1 else jnp.concatenate(parts, axis=0)

    other_tile = swap(w_base, "tok", 1)
    x_groups = [activations] + [swap(activations, "tok", 2 * j) for j in range(1, groups)]
    x_near, x_far = joined(x_groups[:half_groups]), joined(x_groups[half_groups:])
    x_pair, tiles = (x_near, x_far), (w_base, other_tile)

    (low,) = call(
        low_kernel,
        [((tok_rows, 2 * rank), F32)],
        [],
        4 * tok_rows * shard * rank,
        (),
        (after(activations, x_far), grad_out, a_down.T, b_up),
    )
    cot_seen = [grad_out] + [swap(grad_out, "feat", 4 * step) for step in range(1, groups)]
    mask = 4
    while mask < lax.axis_size("feat"):
        low = low + swap(low, "feat", mask)
        mask *= 2

    send_own, keep_own = call(
        own_kernel,
        [((set_rows, shard), BF16)] * 2,
        [((set_rows, shard), F32)],
        2 * product,
        scalars,
        (x_near, w_base, blk_vals),
    )
    keep_own = added(keep_own, swap(send_own, "feat", 1))
    far_11, far_10, far_01, far_00, send_other, keep_other = call(
        rest_kernel,
        [((set_rows, shard), BF16)] * 6,
        [((2 * set_rows, shard), BF16), ((2 * set_rows, shard), F32), ((set_rows, shard), F32)],
        6 * product,
        scalars,
        (*x_pair, *tiles, blk_vals),
    )
    low = after(low, far_11)
    low = low + swap(low, "feat", 1)
    keep_other = added(keep_other, swap(send_other, "feat", 1))
    low = after(low, keep_other)
    low = low + swap(low, "feat", 2)
    low = low.astype(BF16)
    u_half, v_half = low[:, :rank], low[:, rank:]
    far_01 = added(far_01, swap(far_11, "feat", 2))
    far_00 = added(far_00, swap(far_10, "feat", 2))
    sums = [keep_own, keep_other]
    near = added(pick(sums, twist), swap(pick(sums, 1 ^ twist), "feat", 2))
    far = added(far_00, swap(far_01, "feat", 1))
    parts = [near[j * tok_rows : (j + 1) * tok_rows] for j in range(half_groups)]
    parts += [far[j * tok_rows : (j + 1) * tok_rows] for j in range(half_groups)]
    parts = [parts[0]] + [swap(parts[j], "tok", 2 * j) for j in range(1, groups)]
    total = pick(parts, turn).astype(F32)
    for step in range(1, groups):
        total = total + swap(pick(parts, turn ^ step), "feat", 4 * step).astype(F32)
    projected = (total + jnp.dot(u_half, b_up, preferred_element_type=F32)).astype(BF16)

    cot_seen = lax.optimization_barrier((*cot_seen, far_11))[:-1]
    cot_own = [pick(cot_seen, turn)]
    for j in range(1, groups):
        cot_own.append(swap(pick(cot_seen, turn ^ j), "tok", 2 * j))
    g_near, g_far = joined(cot_own[:half_groups]), joined(cot_own[half_groups:])
    g_near, g_far = lax.optimization_barrier((g_near, g_far, far_01))[:2]
    g_near_01, g_far_01 = swap(g_near, "feat", 1), swap(g_far, "feat", 1)
    g_near_10, g_far_10 = swap(g_near, "feat", 2), swap(g_far, "feat", 2)
    g_near_11, g_far_11 = swap(g_near_10, "feat", 1), swap(g_far_01, "feat", 2)
    acc, blocks = call(
        early_kernel,
        [((2 * set_rows, shard), F32), (blk_vals.shape, F32)],
        [((2 * set_rows, shard), BF16)],
        6 * product,
        scalars,
        (*x_pair, g_near, g_far, g_near_01, g_far_01, g_near_10, g_far_10, *tiles, blk_vals),
    )
    own, *rest, blocks = call(
        late_kernel,
        [((tok_rows, shard), F32)]
        + [((tok_rows, shard), BF16)] * (groups - 1)
        + [(blk_vals.shape, F32)],
        [((2 * set_rows, shard), F32), ((2 * set_rows, shard), BF16)],
        2 * product,
        scalars,
        (*x_pair, g_near_11, g_far_11, *tiles, blk_vals, acc, blocks),
    )
    for j in range(1, groups):
        own = own + swap(rest[j - 1], "tok", 2 * j).astype(F32)
    grad_x = (own + jnp.dot(v_half, a_down.T, preferred_element_type=F32)).astype(BF16)

    blocks = blocks.astype(BF16)
    up = jnp.dot(u_half.T, grad_out, preferred_element_type=F32)
    v_groups = [v_half] + [swap(v_half, "tok", 2 * j) for j in range(1, groups)]
    down = tree_sum(
        [jnp.dot(x.T, v, preferred_element_type=F32) for x, v in zip(x_groups, v_groups)]
    )
    down = down + swap(down, "tok", 1)
    up = up + swap(up, "tok", 1)
    mask = 2
    while mask < n_tok:
        up = up.astype(BF16)
        up = up.astype(F32) + swap(up, "tok", mask).astype(F32)
        blocks = blocks + swap(blocks, "tok", mask)
        mask *= 2
    blocks = blocks.astype(F32) + swap(blocks, "tok", 1).astype(F32)
    return projected, grad_x, blocks * grad_scale, down * grad_scale, up * grad_scale


def solution(mesh):
    in_specs = (
        P("tok", "feat"),
        P("feat", "tok"),
        P("feat", None, None),
        P("feat", None),
        P("feat"),
        P("feat", None),
        P(None, "feat"),
        P("tok", "feat"),
    )
    out_specs = (
        P("tok", "feat"),
        P("tok", "feat"),
        P("feat", None, None),
        P("feat", None),
        P(None, "feat"),
    )
    return jax.shard_map(
        on_device, mesh=mesh, in_specs=in_specs, out_specs=out_specs, check_vma=False
    )
```

time: 287 us -> 85.3 us (0.30)
  waiting for transfers between devices: 181 us -> 25.6 us
  blocking collectives: 40.1 us -> 0 us
  starting transfers between devices: 0.16 us -> 30.7 us
  matrix products: 29.7 us -> 1.86 us
  between operations: 18.5 us -> 1.6 us
  Pallas kernels: 0 us -> 9.64 us
  other arithmetic: 9.43 us -> 5.64 us
    all_gather x2 -> x0, waiting for transfers between devices: 109 us -> none  [the longest x1 103 us: on_device(): w_rows = lax.all_gather(w_base, 'tok', axis=1, tiled=True)]
    reduce_scatter x1 -> x0, waiting for transfers between devices: 53.2 us -> none  [on_device(): lax.psum_scatter(col_term.astype(jnp.bfloat16), 'feat', scatter_dimension...]
    psum x1 -> x0, blocking collectives: 40.1 us -> none  [on_device(): u_total = lax.psum(u_part, 'feat')]
    ppermute x0 -> x28, starting transfers between devices: none -> 30.7 us  [swap(): return lax.ppermute(value, axis, [(i, i ^ mask) for i in range(size)])]
    dot_general x17 -> x5, matrix products: 29.7 us -> 1.86 us  [the longest x1 0.92 us: on_device(): jnp.dot(u_half, b_up, preferred_element_type=F32)]
    ppermute x0 -> x28, waiting for transfers between devices: none -> 25.6 us  [swap(): return lax.ppermute(value, axis, [(i, i ^ mask) for i in range(size)])]
    psum x1 -> x0, waiting for transfers between devices: 16.7 us -> none  [on_device(): lax.psum((block_local, down_local, up_local), 'tok')]
    pallas_call x0 -> x5, Pallas kernels: none -> 9.64 us  [call(): pl.pallas_call(kernel, out_shape=shapes, in_specs=[pl.BlockSpec(memory_sp...]
  transfers between devices with their start and end apart: 4 -> 28, of which waited for: 4 -> 9; matrix products, arithmetic and copies ran while one was open for 15% -> 8% of each run, Pallas kernels for 0% -> 11%
where the time goes in v2:
time: 85.3 us; the launch traced here: 84.9 us
  starting transfers between devices  30.7 us (36%)
  waiting for transfers between devices  25.6 us (30%)
  local copies, waits for them, and re-layouts  9.77 us (11%)
  Pallas kernels  9.64 us (11%)
  other arithmetic  5.64 us (7%)
  matrix products  1.86 us (2%)
  between operations  1.6 us (2%)
    ppermute x28, starting transfers between devices, swap(): return lax.ppermute(value, axis, [(i, i ^ mask) for i in range(size)])  30.7 us
    ppermute x28, waiting for transfers between devices, swap(): return lax.ppermute(value, axis, [(i, i ^ mask) for i in range(size)])  25.6 us
    unnamed x34, local copies, waits for them, and re-layouts  9.69 us
    pallas_call x5, Pallas kernels, call(): pl.pallas_call(kernel, out_shape=shapes, in_specs=[pl.BlockSpec(memory_sp...  9.64 us
    select_n x3, other arithmetic, pick(): value = jnp.where(index == place, options[place], value)  2.37 us
  transfers between devices with their start and end apart: 28, of which 9 were waited for; matrix products, arithmetic and copies ran while one was open for 8% of the time, Pallas kernels for 11%

profile of v2, /device:TPU:0, one launch (start us, length us, event | category | flops | bytes accessed | tf_op | source)
XLA Modules:
  0.0 84.9 jit_solution(11655434990888468880)
XLA Ops:
  1.2 2.6 %collective-permute-start = (bf16[128,1024]{1,0:T(8,128)(2,1)}, bf16[128,1024]{1,0:T(8,128)(2,1)S(1)}, u32[]{:S(2)}, u32[]{:S(2)}) collective-permute-start(bf16[128,1024]{1,0:T(8,128)(2,1)} %refs_0_.3), channel_id=1, source_target_pairs={{0,2},{1,3},{2,0},{3,1},{4,6},{5,7},{6,4},{7,5},{8,10},{9,11},{10,... | collective-permute-start | bytes 786440 | tf_op jit(solution)/shard_map/ppermute | solution.py:18
  3.8 2.6 %collective-permute-start.13 = (bf16[128,1024]{1,0:T(8,128)(2,1)}, bf16[128,1024]{1,0:T(8,128)(2,1)}, u32[]{:S(2)}, u32[]{:S(2)}) collective-permute-start(bf16[128,1024]{1,0:T(8,128)(2,1)} %g_ref.1), channel_id=1, source_target_pairs={{0,16},{4,20},{8,24},{12,28},{16,0},{20,4},{24,8},{28,12},{1,17},{... | collective-permute-start | bytes 786440 | tf_op jit(solution)/shard_map/ppermute | solution.py:18
  7.0 2.2 %copy-done = bf16[1024,2048]{1,0:T(8,128)(2,1)S(1)} copy-done((bf16[1024,2048]{1,0:T(8,128)(2,1)S(1)}, bf16[1024,2048]{1,0:T(8,128)(2,1)}, u32[]{:S(2)}) %copy-start) | copy-done | bytes 4194328
  11.7 1.5 %shard_map.120 = (bf16[128,1024]{1,0:T(8,128)(2,1)S(1)}, bf16[128,1024]{1,0:T(8,128)(2,1)S(1)}) custom-call(s32[2,3]{1,0:T(2,128)S(1)} %bitcast.11, s32[1]{0:T(128)S(6)} %copy.13.count_ref, bf16[128,1024]{1,0:T(8,128)(2,1)S(1)} %copy-done.5, bf16[1024,2048]{1,0:T(8,128)(2,1)S(1)} %copy-done, bf16[3,128,128]{2,1,0:T(8,128)(2,1)S(1)} %copy-done.9), custom_call_target="tpu_custom_call" | custom-call | flops 536870912 | bytes 4554752 | tf_op jit(solution)/shard_map/pallas_call | solution.py:51
  13.3 1.5 %collective-permute-start.7 = (bf16[128,1024]{1,0:T(8,128)(2,1)S(1)}, bf16[128,1024]{1,0:T(8,128)(2,1)S(1)}, u32[]{:S(2)}, u32[]{:S(2)}) collective-permute-start(bf16[128,1024]{1,0:T(8,128)(2,1)S(1)} %get-tuple-element.32), channel_id=1, source_target_pairs={{0,4},{4,0},{8,12},{12,8},{16,20},{20,16},{24,28},{28,24},{1,5},{5... | collective-permute-start | bytes 786440 | tf_op jit(solution)/shard_map/ppermute | solution.py:18
  18.4 3.2 %shard_map.119 = (bf16[128,1024]{1,0:T(8,128)(2,1)S(1)}, bf16[128,1024]{1,0:T(8,128)(2,1)S(1)}, bf16[128,1024]{1,0:T(8,128)(2,1)S(1)}, bf16[128,1024]{1,0:T(8,12...) custom-call(s32[2,3]{1,0:T(2,128)S(1)} %bitcast.12, s32[1]{0:T(128)S(6)} %copy.13.count_ref, ...), custom_call_target="tpu_custom_call" | custom-call | flops 1610612736 | bytes 9011200 | tf_op jit(solution)/shard_map/pallas_call | solution.py:51
  23.5 1.4 %collective-permute-start.3 = (bf16[128,1024]{1,0:T(8,128)(2,1)S(1)}, bf16[128,1024]{1,0:T(8,128)(2,1)S(1)}, u32[]{:S(2)}, u32[]{:S(2)}) collective-permute-start(bf16[128,1024]{1,0:T(8,128)(2,1)S(1)} %get-tuple-element.28), channel_id=1, source_target_pairs={{0,8},{4,12},{8,0},{12,4},{16,24},{20,28},{24,16},{28,20},{1,9},{5... | collective-permute-start | bytes 786440 | tf_op jit(solution)/shard_map/ppermute | solution.py:18
  25.6 1.5 %collective-permute-start.11 = (f32[128,128]{1,0:T(8,128)S(1)}, f32[128,128]{1,0:T(8,128)S(1)}, u32[]{:S(2)}, u32[]{:S(2)}) collective-permute-start(f32[128,128]{1,0:T(8,128)S(1)} %add.68), channel_id=1, source_target_pairs={{0,4},{4,0},{8,12},{12,8},{16,20},{20,16},{24,28},{28,24},{1,5},{5... | collective-permute-start | bytes 196616 | tf_op jit(solution)/shard_map/ppermute | solution.py:18
  28.1 2.6 %collective-permute-done.11 = f32[128,128]{1,0:T(8,128)S(1)} collective-permute-done((f32[128,128]{1,0:T(8,128)S(1)}, f32[128,128]{1,0:T(8,128)S(1)}, u32[]{:S(2)}, u32[]{:S(2)}) %collective-permute-start.11) | collective-permute-done | bytes 65568 | tf_op jit(solution)/shard_map/ppermute | solution.py:18
  32.6 1.6 %collective-permute-start.12 = (f32[128,128]{1,0:T(8,128)S(1)}, f32[128,128]{1,0:T(8,128)S(1)}, u32[]{:S(2)}, u32[]{:S(2)}) collective-permute-start(f32[128,128]{1,0:T(8,128)S(1)} %add.69), channel_id=1, source_target_pairs={{0,8},{4,12},{8,0},{12,4},{16,24},{20,28},{24,16},{28,20},{1,9},{5... | collective-permute-start | bytes 196616 | tf_op jit(solution)/shard_map/ppermute | solution.py:18
  35.4 2.1 %collective-permute-done.14.refs_3_ = bf16[128,1024]{1,0:T(8,128)(2,1)S(1)} collective-permute-done((bf16[128,1024]{1,0:T(8,128)(2,1)S(1)}, bf16[128,1024]{1,0:T(8,128)(2,1)S(1)}, u32[]{:S(2)}, u32[]{:S(2)}) %collective-permute-start.14) | collective-permute-done | bytes 262176 | tf_op jit(solution)/shard_map/ppermute | solution.py:18
  37.5 1.6 %collective-permute-start.15 = (bf16[128,1024]{1,0:T(8,128)(2,1)S(1)}, bf16[128,1024]{1,0:T(8,128)(2,1)S(1)}, u32[]{:S(2)}, u32[]{:S(2)}) collective-permute-start(bf16[128,1024]{1,0:T(8,128)(2,1)S(1)} %get-tuple-element.38.refs_2_), channel_id=1, source_target_pairs={{0,8},{4,12},{8,0},{12,4},{16,24},{20,28},{24,16},{28,20},{1,9},{5... | collective-permute-start | bytes 786440 | tf_op jit(solution)/shard_map/ppermute | solution.py:18
  41.4 2.7 %collective-permute-done.24 = bf16[128,64]{1,0:T(8,128)(2,1)S(1)} collective-permute-done((bf16[128,64]{1,0:T(8,128)(2,1)S(1)}, bf16[128,64]{1,0:T(8,128)(2,1)S(1)}, u32[]{:S(2)}, u32[]{:S(2)}) %collective-permute-start.24) | collective-permute-done | bytes 16416 | tf_op jit(solution)/shard_map/ppermute | solution.py:18
  46.6 1.7 %collective-permute-start.8 = (bf16[128,1024]{1,0:T(8,128)(2,1)S(1)}, bf16[128,1024]{1,0:T(8,128)(2,1)S(1)}, u32[]{:S(2)}, u32[]{:S(2)}) collective-permute-start(bf16[128,1024]{1,0:T(8,128)(2,1)S(1)} %get-tuple-element.47), channel_id=1, source_target_pairs={{0,8},{4,12},{8,0},{12,4},{16,24},{20,28},{24,16},{28,20},{1,9},{5... | collective-permute-start | bytes 786440 | tf_op jit(solution)/shard_map/ppermute | solution.py:18
  48.3 3.6 %collective-permute-done.17.refs_5_ = bf16[128,1024]{1,0:T(8,128)(2,1)S(1)} collective-permute-done((bf16[128,1024]{1,0:T(8,128)(2,1)S(1)}, bf16[128,1024]{1,0:T(8,128)(2,1)S(1)}, u32[]{:S(2)}, u32[]{:S(2)}) %collective-permute-start.17) | collective-permute-done | bytes 262176 | tf_op jit(solution)/shard_map/ppermute | solution.py:18
  51.9 1.5 %collective-permute-start.5 = (bf16[128,1024]{1,0:T(8,128)(2,1)S(1)}, bf16[128,1024]{1,0:T(8,128)(2,1)S(1)}, u32[]{:S(2)}, u32[]{:S(2)}) collective-permute-start(bf16[128,1024]{1,0:T(8,128)(2,1)S(1)} %add_convert_fusion.5), channel_id=1, source_target_pairs={{0,2},{1,3},{2,0},{3,1},{4,6},{5,7},{6,4},{7,5},{8,10},{9,11},{10,... | collective-permute-start | bytes 786440 | tf_op jit(solution)/shard_map/ppermute | solution.py:18
  55.4 2.2 %copy-done.4 = bf16[1024,2048]{1,0:T(8,128)(2,1)S(1)} copy-done((bf16[1024,2048]{1,0:T(8,128)(2,1)S(1)}, bf16[1024,2048]{1,0:T(8,128)(2,1)}, u32[]{:S(2)}) %copy-start.4) | copy-done | bytes 4194328
  57.5 3.1 %shard_map.122 = (f32[256,1024]{1,0:T(8,128)S(1)}, f32[3,128,128]{2,1,0:T(8,128)S(1)}) custom-call(s32[2,3]{1,0:T(2,128)S(1)} %bitcast.13, s32[1]{0:T(128)S(6)} %copy.13.count_ref, bf16[128,1024]{1,0:T(8,128)(2,1)S(1)} %copy-done.6, bf16[128,1024]{1,0:T(8,128)(2,1)S(1)} %collective-permute-done.far_ref.refs_1_, ...), custom_call_target="tpu_custom_call" | custom-call | flops 1610612736 | bytes 10584064 | tf_op jit(solution)/shard_map/pallas_call | solution.py:51
  62.7 4.9 %collective-permute-done.18.refs_3_ = bf16[128,1024]{1,0:T(8,128)(2,1)S(1)} collective-permute-done((bf16[128,1024]{1,0:T(8,128)(2,1)S(1)}, bf16[128,1024]{1,0:T(8,128)(2,1)S(1)}, u32[]{:S(2)}, u32[]{:S(2)}) %collective-permute-start.18) | collective-permute-done | bytes 262176 | tf_op jit(solution)/shard_map/ppermute | solution.py:18
  67.6 1.5 %shard_map.123 = (f32[128,1024]{1,0:T(8,128)S(1)}, bf16[128,1024]{1,0:T(8,128)(2,1)S(1)}, f32[3,128,128]{2,1,0:T(8,128)S(1)}) custom-call(s32[2,3]{1,0:T(2,128)S(1)} %bitcast.14, s32[1]{0:T(128)S(6)} %copy.13.count_ref, bf16[128,1024]{1,0:T(8,128)(2,1)S(1)} %copy-done.6, bf16[128,1024]{1,0:T(8,128)(2,1)S(1)} %collective-permute-done.far_ref.refs_1_, ...), custom_call_target="tpu_custom_call" | custom-call | flops 536870912 | bytes 10780672 | tf_op jit(solution)/shard_map/pallas_call | solution.py:51
  69.1 1.5 %collective-permute-start.22 = (bf16[3,128,128]{2,1,0:T(8,128)(2,1)S(1)}, bf16[3,128,128]{2,1,0:T(8,128)(2,1)S(1)}, u32[]{:S(2)}, u32[]{:S(2)}) collective-permute-start(bf16[3,128,128]{2,1,0:T(8,128)(2,1)S(1)} %convert_element_type.114), channel_id=1, source_target_pairs={{0,2},{1,3},{2,0},{3,1},{4,6},{5,7},{6,4},{7,5},{8,10},{9,11},{10,... | collective-permute-start | bytes 294920 | tf_op jit(solution)/shard_map/ppermute | solution.py:18
  70.8 1.8 %collective-permute-start.9 = (bf16[128,1024]{1,0:T(8,128)(2,1)S(1)}, bf16[128,1024]{1,0:T(8,128)(2,1)S(1)}, u32[]{:S(2)}, u32[]{:S(2)}) collective-permute-start(bf16[128,1024]{1,0:T(8,128)(2,1)S(1)} %get-tuple-element.45), channel_id=1, source_target_pairs={{0,16},{4,20},{8,24},{12,28},{16,0},{20,4},{24,8},{28,12},{1,17},{... | collective-permute-start | bytes 786440 | tf_op jit(solution)/shard_map/ppermute | solution.py:18
  74.6 1.4 %collective-permute-start.21 = (bf16[128,1024]{1,0:T(8,128)(2,1)S(1)}, bf16[128,1024]{1,0:T(8,128)(2,1)S(1)}, u32[]{:S(2)}, u32[]{:S(2)}) collective-permute-start(bf16[128,1024]{1,0:T(8,128)(2,1)S(1)} %get-tuple-element.43), channel_id=1, source_target_pairs={{0,2},{1,3},{2,0},{3,1},{4,6},{5,7},{6,4},{7,5},{8,10},{9,11},{10,... | collective-permute-start | bytes 786440 | tf_op jit(solution)/shard_map/ppermute | solution.py:18
  76.8 6.4 %collective-permute-done.9 = bf16[128,1024]{1,0:T(8,128)(2,1)S(1)} collective-permute-done((bf16[128,1024]{1,0:T(8,128)(2,1)S(1)}, bf16[128,1024]{1,0:T(8,128)(2,1)S(1)}, u32[]{:S(2)}, u32[]{:S(2)}) %collective-permute-start.9) | collective-permute-done | bytes 262176 | tf_op jit(solution)/shard_map/ppermute | solution.py:18
  (92 shorter events, 26.7 us)
Async XLA Ops:
  0.6 17.7 %collective-permute-start.1 = (bf16[1024,2048]{1,0:T(8,128)(2,1)}, bf16[1024,2048]{1,0:T(8,128)(2,1)S(1)}, u32[]{:S(2)}, u32[]{:S(2)}) collective-permute-start(bf16[1024,2048]{1,0:T(8,128)(2,1)} %refs_4_.1), channel_id=1, source_target_pairs={{0,1},{1,0},{2,3},{3,2},{4,5},{5,4},{6,7},{7,6},{8,9},{9,8},{10,11... | collective-permute-start | bytes 12582920 | tf_op jit(solution)/shard_map/ppermute | solution.py:18
  1.2 13.7 %collective-permute-start = (bf16[128,1024]{1,0:T(8,128)(2,1)}, bf16[128,1024]{1,0:T(8,128)(2,1)S(1)}, u32[]{:S(2)}, u32[]{:S(2)}) collective-permute-start(bf16[128,1024]{1,0:T(8,128)(2,1)} %refs_0_.3), channel_id=1, source_target_pairs={{0,2},{1,3},{2,0},{3,1},{4,6},{5,7},{6,4},{7,5},{8,10},{9,11},{10,... | collective-permute-start | bytes 786440 | tf_op jit(solution)/shard_map/ppermute | solution.py:18
  3.8 21.9 %collective-permute-start.13 = (bf16[128,1024]{1,0:T(8,128)(2,1)}, bf16[128,1024]{1,0:T(8,128)(2,1)}, u32[]{:S(2)}, u32[]{:S(2)}) collective-permute-start(bf16[128,1024]{1,0:T(8,128)(2,1)} %g_ref.1), channel_id=1, source_target_pairs={{0,16},{4,20},{8,24},{12,28},{16,0},{20,4},{24,8},{28,12},{1,17},{... | collective-permute-start | bytes 786440 | tf_op jit(solution)/shard_map/ppermute | solution.py:18
  13.3 18.1 %collective-permute-start.7 = (bf16[128,1024]{1,0:T(8,128)(2,1)S(1)}, bf16[128,1024]{1,0:T(8,128)(2,1)S(1)}, u32[]{:S(2)}, u32[]{:S(2)}) collective-permute-start(bf16[128,1024]{1,0:T(8,128)(2,1)S(1)} %get-tuple-element.32), channel_id=1, source_target_pairs={{0,4},{4,0},{8,12},{12,8},{16,20},{20,16},{24,28},{28,24},{1,5},{5... | collective-permute-start | bytes 786440 | tf_op jit(solution)/shard_map/ppermute | solution.py:18
  18.0 5.6 %collective-permute-start.10 = (f32[128,128]{1,0:T(8,128)S(1)}, f32[128,128]{1,0:T(8,128)S(1)}, u32[]{:S(2)}, u32[]{:S(2)}) collective-permute-start(f32[128,128]{1,0:T(8,128)S(1)} %shard_map.121), channel_id=1, source_target_pairs={{0,16},{4,20},{8,24},{12,28},{16,0},{20,4},{24,8},{28,12},{1,17},{... | collective-permute-start | bytes 196616 | tf_op jit(solution)/shard_map/ppermute | solution.py:18
  21.6 9.8 %collective-permute-start.6 = (bf16[128,1024]{1,0:T(8,128)(2,1)S(1)}, bf16[128,1024]{1,0:T(8,128)(2,1)}, u32[]{:S(2)}, u32[]{:S(2)}) collective-permute-start(bf16[128,1024]{1,0:T(8,128)(2,1)S(1)} %get-tuple-element.30), channel_id=1, source_target_pairs={{0,4},{4,0},{8,12},{12,8},{16,20},{20,16},{24,28},{28,24},{1,5},{5... | collective-permute-start | bytes 786440 | tf_op jit(solution)/shard_map/ppermute | solution.py:18
  23.5 10.6 %collective-permute-start.3 = (bf16[128,1024]{1,0:T(8,128)(2,1)S(1)}, bf16[128,1024]{1,0:T(8,128)(2,1)S(1)}, u32[]{:S(2)}, u32[]{:S(2)}) collective-permute-start(bf16[128,1024]{1,0:T(8,128)(2,1)S(1)} %get-tuple-element.28), channel_id=1, source_target_pairs={{0,8},{4,12},{8,0},{12,4},{16,24},{20,28},{24,16},{28,20},{1,9},{5... | collective-permute-start | bytes 786440 | tf_op jit(solution)/shard_map/ppermute | solution.py:18
  24.9 20.7 %collective-permute-start.2 = (bf16[128,1024]{1,0:T(8,128)(2,1)S(1)}, bf16[128,1024]{1,0:T(8,128)(2,1)S(1)}, u32[]{:S(2)}, u32[]{:S(2)}) collective-permute-start(bf16[128,1024]{1,0:T(8,128)(2,1)S(1)} %get-tuple-element.26), channel_id=1, source_target_pairs={{0,8},{4,12},{8,0},{12,4},{16,24},{20,28},{24,16},{28,20},{1,9},{5... | collective-permute-start | bytes 786440 | tf_op jit(solution)/shard_map/ppermute | solution.py:18
  30.7 6.8 %collective-permute-start.14 = (bf16[128,1024]{1,0:T(8,128)(2,1)S(1)}, bf16[128,1024]{1,0:T(8,128)(2,1)S(1)}, u32[]{:S(2)}, u32[]{:S(2)}) collective-permute-start(bf16[128,1024]{1,0:T(8,128)(2,1)S(1)} %get-tuple-element.49), channel_id=1, source_target_pairs={{0,2},{1,3},{2,0},{3,1},{4,6},{5,7},{6,4},{7,5},{8,10},{9,11},{10,... | collective-permute-start | bytes 786440 | tf_op jit(solution)/shard_map/ppermute | solution.py:18
  32.6 7.3 %collective-permute-start.12 = (f32[128,128]{1,0:T(8,128)S(1)}, f32[128,128]{1,0:T(8,128)S(1)}, u32[]{:S(2)}, u32[]{:S(2)}) collective-permute-start(f32[128,128]{1,0:T(8,128)S(1)} %add.69), channel_id=1, source_target_pairs={{0,8},{4,12},{8,0},{12,4},{16,24},{20,28},{24,16},{28,20},{1,9},{5... | collective-permute-start | bytes 196616 | tf_op jit(solution)/shard_map/ppermute | solution.py:18
  34.2 12.2 %collective-permute-start.4 = (bf16[128,1024]{1,0:T(8,128)(2,1)S(1)}, bf16[128,1024]{1,0:T(8,128)(2,1)S(1)}, u32[]{:S(2)}, u32[]{:S(2)}) collective-permute-start(bf16[128,1024]{1,0:T(8,128)(2,1)S(1)} %add_convert_fusion.6), channel_id=1, source_target_pairs={{0,4},{4,0},{8,12},{12,8},{16,20},{20,16},{24,28},{28,24},{1,5},{5... | collective-permute-start | bytes 786440 | tf_op jit(solution)/shard_map/ppermute | solution.py:18
  37.5 9.1 %collective-permute-start.15 = (bf16[128,1024]{1,0:T(8,128)(2,1)S(1)}, bf16[128,1024]{1,0:T(8,128)(2,1)S(1)}, u32[]{:S(2)}, u32[]{:S(2)}) collective-permute-start(bf16[128,1024]{1,0:T(8,128)(2,1)S(1)} %get-tuple-element.38.refs_2_), channel_id=1, source_target_pairs={{0,8},{4,12},{8,0},{12,4},{16,24},{20,28},{24,16},{28,20},{1,9},{5... | collective-permute-start | bytes 786440 | tf_op jit(solution)/shard_map/ppermute | solution.py:18
  39.1 12.9 %collective-permute-start.19 = (bf16[128,1024]{1,0:T(8,128)(2,1)S(1)}, bf16[128,1024]{1,0:T(8,128)(2,1)S(1)}, u32[]{:S(2)}, u32[]{:S(2)}) collective-permute-start(bf16[128,1024]{1,0:T(8,128)(2,1)S(1)} %get-tuple-element.38.refs_2_), channel_id=1, source_target_pairs={{0,4},{4,0},{8,12},{12,8},{16,20},{20,16},{24,28},{28,24},{1,5},{5... | collective-permute-start | bytes 786440 | tf_op jit(solution)/shard_map/ppermute | solution.py:18
  44.2 7.7 %collective-permute-start.17 = (bf16[128,1024]{1,0:T(8,128)(2,1)S(1)}, bf16[128,1024]{1,0:T(8,128)(2,1)S(1)}, u32[]{:S(2)}, u32[]{:S(2)}) collective-permute-start(bf16[128,1024]{1,0:T(8,128)(2,1)S(1)} %collective-permute-done.14.refs_3_), channel_id=1, source_target_pairs={{0,4},{4,0},{8,12},{12,8},{16,20},{20,16},{24,28},{28,24},{1,5},{5... | collective-permute-start | bytes 786440 | tf_op jit(solution)/shard_map/ppermute | solution.py:18
  45.6 8.8 %collective-permute-start.20 = (bf16[128,1024]{1,0:T(8,128)(2,1)S(1)}, bf16[128,1024]{1,0:T(8,128)(2,1)S(1)}, u32[]{:S(2)}, u32[]{:S(2)}) collective-permute-start(bf16[128,1024]{1,0:T(8,128)(2,1)S(1)} %collective-permute-done.14.refs_3_), channel_id=1, source_target_pairs={{0,8},{4,12},{8,0},{12,4},{16,24},{20,28},{24,16},{28,20},{1,9},{5... | collective-permute-start | bytes 786440 | tf_op jit(solution)/shard_map/ppermute | solution.py:18
  46.4 14.2 %collective-permute-start.26 = (f32[64,1024]{1,0:T(8,128)S(1)}, f32[64,1024]{1,0:T(8,128)S(1)}, u32[]{:S(2)}, u32[]{:S(2)}) collective-permute-start(f32[64,1024]{1,0:T(8,128)S(1)} %fusion.1), channel_id=1, source_target_pairs={{0,1},{1,0},{2,3},{3,2},{4,5},{5,4},{6,7},{7,6},{8,9},{9,8},{10,11... | collective-permute-start | bytes 786440 | tf_op jit(solution)/shard_map/ppermute | solution.py:18
  46.6 24.0 %collective-permute-start.8 = (bf16[128,1024]{1,0:T(8,128)(2,1)S(1)}, bf16[128,1024]{1,0:T(8,128)(2,1)S(1)}, u32[]{:S(2)}, u32[]{:S(2)}) collective-permute-start(bf16[128,1024]{1,0:T(8,128)(2,1)S(1)} %get-tuple-element.47), channel_id=1, source_target_pairs={{0,8},{4,12},{8,0},{12,4},{16,24},{20,28},{24,16},{28,20},{1,9},{5... | collective-permute-start | bytes 786440 | tf_op jit(solution)/shard_map/ppermute | solution.py:18
  51.9 8.9 %collective-permute-start.25 = (f32[1024,64]{0,1:T(8,128)S(1)}, f32[1024,64]{0,1:T(8,128)S(1)}, u32[]{:S(2)}, u32[]{:S(2)}) collective-permute-start(f32[1024,64]{0,1:T(8,128)S(1)} %fusion), channel_id=1, source_target_pairs={{0,1},{1,0},{2,3},{3,2},{4,5},{5,4},{6,7},{7,6},{8,9},{9,8},{10,11... | collective-permute-start | bytes 786440 | tf_op jit(solution)/shard_map/ppermute | solution.py:18
  51.9 18.7 %collective-permute-start.5 = (bf16[128,1024]{1,0:T(8,128)(2,1)S(1)}, bf16[128,1024]{1,0:T(8,128)(2,1)S(1)}, u32[]{:S(2)}, u32[]{:S(2)}) collective-permute-start(bf16[128,1024]{1,0:T(8,128)(2,1)S(1)} %add_convert_fusion.5), channel_id=1, source_target_pairs={{0,2},{1,3},{2,0},{3,1},{4,6},{5,7},{6,4},{7,5},{8,10},{9,11},{10,... | collective-permute-start | bytes 786440 | tf_op jit(solution)/shard_map/ppermute | solution.py:18
  54.4 8.3 %collective-permute-start.16 = (bf16[128,1024]{1,0:T(8,128)(2,1)S(1)}, bf16[128,1024]{1,0:T(8,128)(2,1)S(1)}, u32[]{:S(2)}, u32[]{:S(2)}) collective-permute-start(bf16[128,1024]{1,0:T(8,128)(2,1)S(1)} %collective-permute-done.15.refs_6_), channel_id=1, source_target_pairs={{0,4},{4,0},{8,12},{12,8},{16,20},{20,16},{24,28},{28,24},{1,5},{5... | collective-permute-start | bytes 786440 | tf_op jit(solution)/shard_map/ppermute | solution.py:18
  60.6 6.9 %collective-permute-start.18 = (bf16[128,1024]{1,0:T(8,128)(2,1)S(1)}, bf16[128,1024]{1,0:T(8,128)(2,1)S(1)}, u32[]{:S(2)}, u32[]{:S(2)}) collective-permute-start(bf16[128,1024]{1,0:T(8,128)(2,1)S(1)} %collective-permute-done.17.refs_5_), channel_id=1, source_target_pairs={{0,8},{4,12},{8,0},{12,4},{16,24},{20,28},{24,16},{28,20},{1,9},{5... | collective-permute-start | bytes 786440 | tf_op jit(solution)/shard_map/ppermute | solution.py:18
  60.8 13.1 %collective-permute-start.27 = (bf16[64,1024]{1,0:T(8,128)(2,1)S(1)}, bf16[64,1024]{1,0:T(8,128)(2,1)S(1)}, u32[]{:S(2)}, u32[]{:S(2)}) collective-permute-start(bf16[64,1024]{1,0:T(8,128)(2,1)S(1)} %add_convert_fusion.8), channel_id=1, source_target_pairs={{0,2},{1,3},{2,0},{3,1},{4,6},{5,7},{6,4},{7,5},{8,10},{9,11},{10,... | collective-permute-start | bytes 393224 | tf_op jit(solution)/shard_map/ppermute | solution.py:18
  70.8 12.3 %collective-permute-start.9 = (bf16[128,1024]{1,0:T(8,128)(2,1)S(1)}, bf16[128,1024]{1,0:T(8,128)(2,1)S(1)}, u32[]{:S(2)}, u32[]{:S(2)}) collective-permute-start(bf16[128,1024]{1,0:T(8,128)(2,1)S(1)} %get-tuple-element.45), channel_id=1, source_target_pairs={{0,16},{4,20},{8,24},{12,28},{16,0},{20,4},{24,8},{28,12},{1,17},{... | collective-permute-start | bytes 786440 | tf_op jit(solution)/shard_map/ppermute | solution.py:18
  74.6 9.4 %collective-permute-start.21 = (bf16[128,1024]{1,0:T(8,128)(2,1)S(1)}, bf16[128,1024]{1,0:T(8,128)(2,1)S(1)}, u32[]{:S(2)}, u32[]{:S(2)}) collective-permute-start(bf16[128,1024]{1,0:T(8,128)(2,1)S(1)} %get-tuple-element.43), channel_id=1, source_target_pairs={{0,2},{1,3},{2,0},{3,1},{4,6},{5,7},{6,4},{7,5},{8,10},{9,11},{10,... | collective-permute-start | bytes 786440 | tf_op jit(solution)/shard_map/ppermute | solution.py:18
  (21 other events, 169.7 us)

commit v3 on v2

v3 whole, which is shorter than its diff:
```python
import functools

import jax
import jax.numpy as jnp
from jax import lax
from jax.experimental import pallas as pl
from jax.experimental.pallas import tpu as pltpu
from jax.sharding import PartitionSpec as P

BLK = 128
F32 = jnp.float32
BF16 = jnp.bfloat16
NT = (((1,), (1,)), ((), ()))
TN = (((0,), (0,)), ((), ()))
MIB = 1024 * 1024


def swap(value, axis, mask):
    size = lax.axis_size(axis)
    return lax.ppermute(value, axis, [(i, i ^ mask) for i in range(size)])


def tree_sum(terms):
    while len(terms) > 1:
        terms = [terms[i] + terms[i + 1] for i in range(0, len(terms), 2)]
    return terms[0]


def pick(options, index):
    value = options[0]
    for place in range(1, len(options)):
        value = jnp.where(index == place, options[place], value)
    return value


def after(values, *others):
    return values if not others else lax.optimization_barrier((values, others))[0]


def added(*terms):
    return sum(term.astype(F32) for term in terms).astype(BF16)


def position():
    feat_at, tok_at = lax.axis_index("feat"), lax.axis_index("tok")
    return feat_at // 2, feat_at % 2, tok_at


def call(kernel, limit, weight, out_shapes, scratch, flops, scalars, near, far=(), far_outs=0):
    space, apart = pl.BlockSpec(memory_space=pltpu.VMEM), pl.BlockSpec(memory_space=pltpu.HBM)
    shapes = [jax.ShapeDtypeStruct(shape, dtype) for shape, dtype in out_shapes]
    size = sum(a.size * a.dtype.itemsize for a in (*near, *far))

    def body(*refs):
        sources, refs = refs[: len(scalars)], refs[len(scalars) :]
        if not scalars:
            return kernel(*refs)
        *refs, index_ref, count_ref, sems = refs
        copies = start_copies(list(zip(sources, (index_ref, count_ref))), sems)

        def ready():
            for copy in copies:
                copy.wait()

        return kernel(index_ref, count_ref, ready, *refs)

    held = [pltpu.SMEM(a.shape, a.dtype) for a in scalars]
    return pl.pallas_call(
        body,
        out_shape=shapes,
        in_specs=[apart] * len(scalars) + [space] * len(near) + [apart] * len(far),
        out_specs=[space] * (len(shapes) - far_outs) + [apart] * far_outs,
        scratch_shapes=scratch + held + [pltpu.SemaphoreType.DMA((2,))] * (len(held) > 0),
        compiler_params=pltpu.CompilerParams(vmem_limit_bytes=limit * MIB),
        cost_estimate=pl.CostEstimate(
            flops=int(flops * weight), bytes_accessed=int(size * weight), transcendentals=0
        ),
    )(*scalars, *near, *far)


def start_copies(pairs, sems):
    copies = [pltpu.make_async_copy(src, dst, sems.at[i]) for i, (src, dst) in enumerate(pairs)]
    for copy in copies:
        copy.start()
    return copies


def column_half(half, shard):
    return pl.ds(pl.multiple_of(half * shard, shard), shard)


def for_slots(index_ref, count_ref, slots, first, wide, body):
    for slot in range(slots):
        local = index_ref[1, slot] * BLK - first

        @pl.when((slot < count_ref[0]) & (local >= 0) & (local < wide))
        def _():
            rows = pl.ds(pl.multiple_of(index_ref[0, slot] * BLK, BLK), BLK)
            body(slot, rows, pl.ds(pl.multiple_of(local, BLK), BLK))


def low_kernel(x_in, g_in, down_in, up_in, out_ref, x_ref, g_ref, down_ref, up_ref, sems):
    copies = start_copies([(x_in, x_ref), (down_in, down_ref), (g_in, g_ref), (up_in, up_ref)], sems)
    rank = up_ref.shape[0]
    copies[0].wait()
    copies[1].wait()
    out_ref[:, :rank] = lax.dot_general(x_ref[...], down_ref[...], NT, preferred_element_type=F32)
    copies[2].wait()
    copies[3].wait()
    out_ref[:, rank:] = lax.dot_general(g_ref[...], up_ref[...], NT, preferred_element_type=F32)


def forward_kernel(index_ref, count_ref, ready, far_in, near_in, vals_in, own_in, other_in, *refs):
    outs, (x_ref, w_ref, vals_ref, acc, out_ref, sems, out_sems) = refs[:8], refs[8:]
    r, c, t = position()
    twist = (r ^ t) & 1
    rows, shard = far_in.shape
    places = [(tile, p) for tile in (0, 1) for p in (1, 0)]

    def tile_copy(i):
        tile, p = places[i]
        source = (own_in, other_in)[tile].at[:, column_half(p ^ c, shard)]
        return pltpu.make_async_copy(source, w_ref.at[i], sems.at[i])

    pairs = [(near_in, x_ref.at[rows:, :]), (far_in, x_ref.at[:rows, :]), (vals_in, vals_ref)]
    copies = [pltpu.make_async_copy(s, d, sems.at[4 + i]) for i, (s, d) in enumerate(pairs)]
    for copy in copies:
        copy.start()
    for i in range(len(places)):
        tile_copy(i).start()
    for copy in copies:
        copy.wait()
    ready()
    for i, (tile, p) in enumerate(places):
        tile_copy(i).wait()
        acc[...] = jnp.dot(x_ref[...], w_ref[i], preferred_element_type=F32)

        def body(slot, block_rows, block_columns):
            acc[:, block_columns] += jnp.dot(
                x_ref[:, block_rows], vals_ref[slot], preferred_element_type=F32
            )

        first = (2 * (t ^ tile) + (p ^ c)) * shard
        for_slots(index_ref, count_ref, vals_ref.shape[0], first, shard, body)
        out_ref[i] = acc[...].astype(BF16)
        for q in (1, 0):

            @pl.when(q ^ twist == tile)
            def _():
                at = 2 * (1 - q) + 1 - p
                pltpu.make_async_copy(out_ref.at[i, :rows], outs[at], out_sems.at[2 * i]).start()
                pltpu.make_async_copy(out_ref.at[i, rows:], outs[4 + at], out_sems.at[2 * i + 1]).start()

    for i in range(8):
        pltpu.make_async_copy(out_ref.at[0, :rows], outs[0], out_sems.at[i]).wait()


def start_tile(w_in, target, sem, q, p):
    r, c, t = position()
    half = column_half(p ^ c, target.shape[1])
    for tile in range(2):

        @pl.when(q ^ ((r ^ t) & 1) == tile)
        def _():
            pltpu.make_async_copy(w_in[tile].at[:, half], target, sem).start()

    return pltpu.make_async_copy(w_in[0].at[:, half], target, sem)


def pull(index_ref, count_ref, x_refs, g_refs, vals_ref, w_ref, acc, both, blocks_ref, q, p):
    r, c, t = position()
    rows, shard = x_refs[0].shape
    for part in range(2):
        both[part * rows : (part + 1) * rows, :] = g_refs[part][...]
    acc[...] += lax.dot_general(both[...], w_ref[...], NT, preferred_element_type=F32)

    def body(slot, block_rows, block_columns):
        g_columns = both[:, block_columns]
        acc[:, block_rows] += lax.dot_general(
            g_columns, vals_ref[slot], NT, preferred_element_type=F32
        )
        for part in range(2):
            blocks_ref[slot] += lax.dot_general(
                x_refs[part][:, block_rows],
                g_columns[part * rows : (part + 1) * rows],
                TN,
                preferred_element_type=F32,
            )

    first = (2 * (t ^ q ^ ((r ^ t) & 1)) + (p ^ c)) * shard
    for_slots(index_ref, count_ref, vals_ref.shape[0], first, shard, body)


def early_kernel(index_ref, count_ref, ready, *refs):
    x_refs, g_refs, vals_in, w_in = refs[:2], refs[2:8], refs[8], refs[9:11]
    acc, blocks_ref, last_ref, vals_ref, w_ref, both, sems = refs[11:]
    vals_copy = pltpu.make_async_copy(vals_in, vals_ref, sems.at[4])
    vals_copy.start()
    chunks = ((0, 0), (0, 1), (1, 0))
    copies = [start_tile(w_in, w_ref.at[i], sems.at[i], q, p) for i, (q, p) in enumerate(chunks)]
    last_copy = start_tile(w_in, last_ref, sems.at[3], 1, 1)
    acc[...] = jnp.zeros_like(acc)
    blocks_ref[...] = jnp.zeros_like(blocks_ref)
    vals_copy.wait()
    ready()
    for i, (q, p) in enumerate(chunks):
        copies[i].wait()
        pair = g_refs[2 * i : 2 * i + 2]
        pull(index_ref, count_ref, x_refs, pair, vals_ref, w_ref.at[i], acc, both, blocks_ref, q, p)
    last_copy.wait()


def late_kernel(index_ref, count_ref, ready, *refs):
    x_refs, g_refs, acc_in, blocks_in, vals_ref, w_ref = refs[:2], refs[2:4], *refs[4:8]
    own_ref, *rest_refs, blocks_ref, acc, both = refs[8:]
    acc[...] = acc_in[...]
    blocks_ref[...] = blocks_in[...]
    ready()
    pull(index_ref, count_ref, x_refs, g_refs, vals_ref, w_ref, acc, both, blocks_ref, 1, 1)
    rows = own_ref.shape[0]
    own_ref[...] = acc[:rows, :]
    for place, rest_ref in enumerate(rest_refs):
        rest_ref[...] = acc[(place + 1) * rows : (place + 2) * rows, :].astype(BF16)


def on_device(activations, w_base, blk_vals, blk_index, blk_count, a_down, b_up, grad_out):
    tok_rows, shard = activations.shape
    n_tok = lax.axis_size("tok")
    grad_scale = float(tok_rows * n_tok) ** (-0.5)
    groups = n_tok // 2
    half_groups = groups // 2
    set_rows = half_groups * tok_rows
    rank = a_down.shape[1]
    r, c, t = position()
    turn = (r ^ t) >> 1
    scalars = (blk_index.T, blk_count)
    product = 2 * set_rows * shard * shard
    tall, tile_half = (2 * set_rows, shard), (shard, shard)

    def joined(parts):
        return parts[0] if len(parts) == 1 else jnp.concatenate(parts, axis=0)

    def parted(near, far):
        both = [near[j * tok_rows : (j + 1) * tok_rows] for j in range(half_groups)]
        return both + [far[j * tok_rows : (j + 1) * tok_rows] for j in range(half_groups)]

    other_tile = swap(w_base, "tok", 1)
    x_groups = [activations] + [swap(activations, "tok", 2 * j) for j in range(1, groups)]
    x_near, x_far = joined(x_groups[:half_groups]), joined(x_groups[half_groups:])
    x_pair = (x_near, x_far)
    cot_seen = [grad_out] + [swap(grad_out, "feat", 4 * step) for step in range(1, groups)]

    low_in = (activations, grad_out, a_down.T, b_up)
    (low,) = call(
        low_kernel,
        60,
        1,
        [((tok_rows, 2 * rank), F32)],
        [pltpu.VMEM(a.shape, a.dtype) for a in low_in] + [pltpu.SemaphoreType.DMA((4,))],
        4 * tok_rows * shard * rank,
        (),
        (),
        low_in,
    )
    low = after(low)
    low = low + swap(low, "feat", 1)

    x_far_now = after(x_far, low)

    far_11, far_10, far_01, far_00, near_11, near_10, near_01, near_00 = call(
        forward_kernel,
        60,
        1,
        [((set_rows, shard), BF16)] * 8,
        [
            pltpu.VMEM(tall, BF16),
            pltpu.VMEM((4, *tile_half), BF16),
            pltpu.VMEM(blk_vals.shape, BF16),
            pltpu.VMEM(tall, F32),
            pltpu.VMEM((4, *tall), BF16),
            pltpu.SemaphoreType.DMA((7,)),
            pltpu.SemaphoreType.DMA((8,)),
        ],
        8 * product,
        scalars,
        (),
        (x_far_now, x_near, blk_vals, w_base, other_tile),
        8,
    )
    far_1 = after((far_11, far_10))
    got_far_11, got_far_10 = swap(far_1[0], "feat", 2), swap(far_1[1], "feat", 2)
    got_near_11, got_near_01 = swap(near_11, "feat", 1), swap(near_01, "feat", 1)
    low = after(low)
    low = low + swap(low, "feat", 2)

    cot_seen = after(cot_seen)
    cot_own = [pick(cot_seen, turn)]
    for j in range(1, groups):
        cot_own.append(swap(pick(cot_seen, turn ^ j), "tok", 2 * j))
    g_near, g_far = joined(cot_own[:half_groups]), joined(cot_own[half_groups:])
    far_01 = added(far_01, after(got_far_11, g_near))
    got_far_01 = swap(far_01, "feat", 1)

    near_10 = added(near_10, after(got_near_11, far_01))
    got_near_10 = swap(near_10, "feat", 2)
    far_00 = added(far_00, after(got_far_10, near_10))
    near_00 = added(near_00, after(got_near_01, near_10))
    g_near = after(g_near, far_01)
    g_far = after(g_far, near_10)
    g_far_01, g_near_10 = swap(g_far, "feat", 1), swap(g_near, "feat", 2)
    g_near_01, g_far_10 = swap(g_near, "feat", 1), swap(g_far, "feat", 2)
    low = after(low, g_far)
    mask = 4
    while mask < lax.axis_size("feat"):
        low = low + swap(low, "feat", mask)
        mask *= 2
    far = added(far_00, after(got_far_01, g_far))

    parts = parted(far, far)
    got_parts = {j: swap(parts[j], "tok", 2 * j) for j in range(half_groups, groups)}
    near = added(near_00, after(got_near_10))
    g_near_11 = swap(after(g_near_10, near), "feat", 1)
    g_far_11 = swap(after(g_far_01), "feat", 2)
    parts = parted(near, far)
    got_parts.update({j: swap(parts[j], "tok", 2 * j) for j in range(1, half_groups)})
    parts = [parts[0]] + [got_parts[j] for j in range(1, groups)]
    total = pick(parts, turn).astype(F32)
    sent = [pick(parts, turn ^ step) for step in range(1, groups)]
    got_total = [swap(part, "feat", 4 * step) for step, part in enumerate(sent, 1)]
    low = after(low.astype(BF16))
    u_half, v_half = low[:, :rank], low[:, rank:]
    up = jnp.dot(u_half.T, grad_out, preferred_element_type=F32)
    up = (up + swap(up, "tok", 1)).astype(BF16)
    got_v = [swap(v_half, "tok", 2 * j) for j in range(1, groups)]
    v_groups = [v_half] + after(got_v, near)
    down = tree_sum(
        [jnp.dot(x.T, v, preferred_element_type=F32) for x, v in zip(x_groups, v_groups)]
    )

    acc, blocks, last_tile, vals_seen = call(
        early_kernel,
        32,
        1,
        [(tall, F32), (blk_vals.shape, F32), (tile_half, BF16), (blk_vals.shape, BF16)],
        [
            pltpu.VMEM((3, *tile_half), BF16),
            pltpu.VMEM(tall, BF16),
            pltpu.SemaphoreType.DMA((5,)),
        ],
        6 * product,
        scalars,
        (*x_pair, after(g_near), g_far, g_near_01, g_far_01, g_near_10, g_far_10),
        (blk_vals, w_base, other_tile),
    )
    own, *rest, blocks = call(
        late_kernel,
        32,
        1,
        [((tok_rows, shard), F32)]
        + [((tok_rows, shard), BF16)] * (groups - 1)
        + [(blk_vals.shape, F32)],
        [pltpu.VMEM(tall, F32), pltpu.VMEM(tall, BF16)],
        2 * product,
        scalars,
        (*x_pair, after(g_near_11), g_far_11, acc, blocks, vals_seen, last_tile),
    )
    rest = after(rest)
    got_rest = [swap(rest[j - 1], "tok", 2 * j) for j in range(1, groups)]

    blocks = blocks.astype(BF16)
    down = down + swap(down, "tok", 1)
    mask = 2
    while mask < n_tok:
        up = up.astype(F32) + swap(up.astype(BF16), "tok", mask).astype(F32)
        blocks = blocks + swap(blocks, "tok", mask)
        mask *= 2
    blocks = blocks.astype(F32) + swap(blocks, "tok", 1).astype(F32)

    for got in got_total:
        total = total + got.astype(F32)
    projected = (total + jnp.dot(u_half, b_up, preferred_element_type=F32)).astype(BF16)
    for got in got_rest:
        own = own + got.astype(F32)
    grad_x = (own + jnp.dot(v_half, a_down.T, preferred_element_type=F32)).astype(BF16)
    return projected, grad_x, blocks * grad_scale, down * grad_scale, up * grad_scale


def solution(mesh):
    in_specs = (
        P("tok", "feat"),
        P("feat", "tok"),
        P("feat", None, None),
        P("feat", None),
        P("feat"),
        P("feat", None),
        P(None, "feat"),
        P("tok", "feat"),
    )
    out_specs = (
        P("tok", "feat"),
        P("tok", "feat"),
        P("feat", None, None),
        P("feat", None),
        P(None, "feat"),
    )
    return jax.shard_map(
        on_device, mesh=mesh, in_specs=in_specs, out_specs=out_specs, check_vma=False
    )
```

time: 85.3 us -> 76 us (0.89)
  local copies, waits for them, and re-layouts: 9.77 us -> 0.83 us
  waiting for transfers between devices: 25.6 us -> 19.5 us
  Pallas kernels: 9.64 us -> 13.4 us
  starting transfers between devices: 30.7 us -> 32.2 us
    unnamed x34 -> x22, local copies, waits for them, and re-layouts: 9.69 us -> 0.75 us
    ppermute x28, waiting for transfers between devices: 25.6 us -> 19.5 us  [swap(): return lax.ppermute(value, axis, [(i, i ^ mask) for i in range(size)])]
    pallas_call x5 -> x4, Pallas kernels: 9.64 us -> 13.4 us  [call(): pl.pallas_call(body, out_shape=shapes, in_specs=[apart] * len(scalars) +...]
    select_n x3 -> x2, other arithmetic: 2.37 us -> 0.24 us  [pick(): value = jnp.where(index == place, options[place], value)]
    convert_element_type x4 -> x5, other arithmetic: 0.23 us -> 2.25 us  [the longest x3 2.21 us: added(): return sum((term.astype(F32) for term in terms)).astype(BF16)]
    ppermute x28, starting transfers between devices: 30.7 us -> 32.2 us  [swap(): return lax.ppermute(value, axis, [(i, i ^ mask) for i in range(size)])]
  transfers between devices with their start and end apart: 28 -> 28, of which waited for: 9 -> 10; matrix products, arithmetic and copies ran while one was open for 8% -> 10% of each run, Pallas kernels for 11% -> 18%
where the time goes in v3:
time: 76 us; the launch traced here: 75.7 us
  starting transfers between devices  32.2 us (42%)
  waiting for transfers between devices  19.5 us (26%)
  Pallas kernels  13.4 us (18%)
  other arithmetic  6.36 us (8%)
  matrix products  1.87 us (2%)
  between operations  1.58 us (2%)
  local copies, waits for them, and re-layouts  0.83 us (1%)
    ppermute x28, starting transfers between devices, swap(): return lax.ppermute(value, axis, [(i, i ^ mask) for i in range(size)])  32.2 us
    ppermute x28, waiting for transfers between devices, swap(): return lax.ppermute(value, axis, [(i, i ^ mask) for i in range(size)])  19.5 us
    pallas_call x4, Pallas kernels, call(): pl.pallas_call(body, out_shape=shapes, in_specs=[apart] * len(scalars) +...  13.4 us
    convert_element_type x3, other arithmetic, added(): return sum((term.astype(F32) for term in terms)).astype(BF16)  2.21 us
  transfers between devices with their start and end apart: 28, of which 10 were waited for; matrix products, arithmetic and copies ran while one was open for 10% of the time, Pallas kernels for 18%

profile of v3, /device:TPU:0, one launch (start us, length us, event | category | flops | bytes accessed | tf_op | source)
XLA Modules:
  0.0 75.7 jit_solution(13067940253821465021)
XLA Ops:
  1.1 2.6 %collective-permute-start = (bf16[128,1024]{1,0:T(8,128)(2,1)}, bf16[128,1024]{1,0:T(8,128)(2,1)S(1)}, u32[]{:S(2)}, u32[]{:S(2)}) collective-permute-start(bf16[128,1024]{1,0:T(8,128)(2,1)} %refs_2_.3), channel_id=1, source_target_pairs={{0,2},{1,3},{2,0},{3,1},{4,6},{5,7},{6,4},{7,5},{8,10},{9,11},{10,... | collective-permute-start | bytes 786440 | tf_op jit(solution)/shard_map/ppermute | solution.py:20
  3.7 2.2 %shard_map.119 = f32[128,128]{1,0:T(8,128)} custom-call(bf16[128,1024]{1,0:T(8,128)(2,1)} %refs_2_.3, bf16[128,1024]{1,0:T(8,128)(2,1)} %refs_1_.4, bf16[64,1024]{1,0:T(8,128)(2,1)} %bitcast.13, bf16[64,1024]{1,0:T(8,128)(2,1)} %refs_3_.2), custom_call_target="tpu_custom_call" | custom-call | flops 33554432 | bytes 786432 | tf_op jit(solution)/shard_map/pallas_call | solution.py:68
  6.0 1.6 %collective-permute-start.1 = (f32[128,128]{1,0:T(8,128)}, f32[128,128]{1,0:T(8,128)S(1)}, u32[]{:S(2)}, u32[]{:S(2)}) collective-permute-start(f32[128,128]{1,0:T(8,128)} %shard_map.119), channel_id=1, source_target_pairs={{0,4},{4,0},{8,12},{12,8},{16,20},{20,16},{24,28},{28,24},{1,5},{5... | collective-permute-start | bytes 196616 | tf_op jit(solution)/shard_map/ppermute | solution.py:20
  7.6 2.6 %collective-permute-start.6 = (bf16[128,1024]{1,0:T(8,128)(2,1)}, bf16[128,1024]{1,0:T(8,128)(2,1)S(1)}, u32[]{:S(2)}, u32[]{:S(2)}) collective-permute-start(bf16[128,1024]{1,0:T(8,128)(2,1)} %refs_1_.4), channel_id=1, source_target_pairs={{0,16},{4,20},{8,24},{12,28},{16,0},{20,4},{24,8},{28,12},{1,17},{... | collective-permute-start | bytes 786440 | tf_op jit(solution)/shard_map/ppermute | solution.py:20
  11.7 1.6 %collective-permute-start.13 = (f32[128,128]{1,0:T(8,128)S(1)}, f32[128,128]{1,0:T(8,128)S(1)}, u32[]{:S(2)}, u32[]{:S(2)}) collective-permute-start(f32[128,128]{1,0:T(8,128)S(1)} %add.61), channel_id=1, source_target_pairs={{0,8},{4,12},{8,0},{12,4},{16,24},{20,28},{24,16},{28,20},{1,9},{5... | collective-permute-start | bytes 196616 | tf_op jit(solution)/shard_map/ppermute | solution.py:20
  13.9 6.0 %shard_map.120 = (bf16[128,1024]{1,0:T(8,128)(2,1)}, bf16[128,1024]{1,0:T(8,128)(2,1)}, bf16[128,1024]{1,0:T(8,128)(2,1)}, bf16[128,1024]{1,0:T(8,128)(2,1)}, bf...) custom-call(s32[2,3]{1,0:T(2,128)} %bitcast.10, ...), custom_call_target="tpu_custom_call" | custom-call | flops 2147483648 | bytes 9011200 | tf_op jit(solution)/shard_map/pallas_call | solution.py:68
  20.6 1.4 %collective-permute-start.4 = (bf16[128,1024]{1,0:T(8,128)(2,1)}, bf16[128,1024]{1,0:T(8,128)(2,1)S(1)}, u32[]{:S(2)}, u32[]{:S(2)}) collective-permute-start(bf16[128,1024]{1,0:T(8,128)(2,1)} %get-tuple-element.35), channel_id=1, source_target_pairs={{0,4},{4,0},{8,12},{12,8},{16,20},{20,16},{24,28},{28,24},{1,5},{5... | collective-permute-start | bytes 786440 | tf_op jit(solution)/shard_map/ppermute | solution.py:20
  23.5 1.5 %collective-permute-start.3 = (bf16[128,1024]{1,0:T(8,128)(2,1)}, bf16[128,1024]{1,0:T(8,128)(2,1)S(1)}, u32[]{:S(2)}, u32[]{:S(2)}) collective-permute-start(bf16[128,1024]{1,0:T(8,128)(2,1)} %get-tuple-element.33), channel_id=1, source_target_pairs={{0,8},{4,12},{8,0},{12,4},{16,24},{20,28},{24,16},{28,20},{1,9},{5... | collective-permute-start | bytes 786440 | tf_op jit(solution)/shard_map/ppermute | solution.py:20
  25.0 4.6 %collective-permute-done.5 = bf16[128,1024]{1,0:T(8,128)(2,1)S(1)} collective-permute-done((bf16[128,1024]{1,0:T(8,128)(2,1)}, bf16[128,1024]{1,0:T(8,128)(2,1)S(1)}, u32[]{:S(2)}, u32[]{:S(2)}) %collective-permute-start.5) | collective-permute-done | bytes 262176 | tf_op jit(solution)/shard_map/ppermute | solution.py:20
  31.7 1.8 %collective-permute-start.14 = (f32[128,128]{1,0:T(8,128)S(1)}, f32[128,128]{1,0:T(8,128)S(1)}, u32[]{:S(2)}, u32[]{:S(2)}) collective-permute-start(f32[128,128]{1,0:T(8,128)S(1)} %add.69), channel_id=1, source_target_pairs={{0,16},{4,20},{8,24},{12,28},{16,0},{20,4},{24,8},{28,12},{1,17},{... | collective-permute-start | bytes 196616 | tf_op jit(solution)/shard_map/ppermute | solution.py:20
  33.5 1.7 %collective-permute-start.7 = (bf16[128,1024]{1,0:T(8,128)(2,1)S(1)}, bf16[128,1024]{1,0:T(8,128)(2,1)S(1)}, u32[]{:S(2)}, u32[]{:S(2)}) collective-permute-start(bf16[128,1024]{1,0:T(8,128)(2,1)S(1)} %add_convert_fusion.7), channel_id=1, source_target_pairs={{0,4},{4,0},{8,12},{12,8},{16,20},{20,16},{24,28},{28,24},{1,5},{5... | collective-permute-start | bytes 786440 | tf_op jit(solution)/shard_map/ppermute | solution.py:20
  35.6 1.3 %collective-permute-start.20 = (bf16[128,1024]{1,0:T(8,128)(2,1)S(1)}, bf16[128,1024]{1,0:T(8,128)(2,1)S(1)}, u32[]{:S(2)}, u32[]{:S(2)}) collective-permute-start(bf16[128,1024]{1,0:T(8,128)(2,1)S(1)} %collective-permute-done.8.refs_5_), channel_id=1, source_target_pairs={{0,8},{4,12},{8,0},{12,4},{16,24},{20,28},{24,16},{28,20},{1,9},{5... | collective-permute-start | bytes 786440 | tf_op jit(solution)/shard_map/ppermute | solution.py:20
  38.2 4.5 %collective-permute-done.7 = bf16[128,1024]{1,0:T(8,128)(2,1)S(1)} collective-permute-done((bf16[128,1024]{1,0:T(8,128)(2,1)S(1)}, bf16[128,1024]{1,0:T(8,128)(2,1)S(1)}, u32[]{:S(2)}, u32[]{:S(2)}) %collective-permute-start.7) | collective-permute-done | bytes 262176 | tf_op jit(solution)/shard_map/ppermute | solution.py:20
  43.4 2.6 %collective-permute-start.11 = (bf16[128,1024]{1,0:T(8,128)(2,1)S(1)}, bf16[128,1024]{1,0:T(8,128)(2,1)S(1)}, u32[]{:S(2)}, u32[]{:S(2)}) collective-permute-start(bf16[128,1024]{1,0:T(8,128)(2,1)S(1)} %add_convert_fusion.6), channel_id=1, source_target_pairs={{0,8},{4,12},{8,0},{12,4},{16,24},{20,28},{24,16},{28,20},{1,9},{5... | collective-permute-start | bytes 786440 | tf_op jit(solution)/shard_map/ppermute | solution.py:20
  46.0 2.1 %collective-permute-done.17.refs_7_ = bf16[128,1024]{1,0:T(8,128)(2,1)S(1)} collective-permute-done((bf16[128,1024]{1,0:T(8,128)(2,1)S(1)}, bf16[128,1024]{1,0:T(8,128)(2,1)S(1)}, u32[]{:S(2)}, u32[]{:S(2)}) %collective-permute-start.17) | collective-permute-done | bytes 262176 | tf_op jit(solution)/shard_map/ppermute | solution.py:20
  48.6 1.6 %collective-permute-start.9 = (bf16[128,1024]{1,0:T(8,128)(2,1)S(1)}, bf16[128,1024]{1,0:T(8,128)(2,1)S(1)}, u32[]{:S(2)}, u32[]{:S(2)}) collective-permute-start(bf16[128,1024]{1,0:T(8,128)(2,1)S(1)} %add_convert_fusion.4), channel_id=1, source_target_pairs={{0,2},{1,3},{2,0},{3,1},{4,6},{5,7},{6,4},{7,5},{8,10},{9,11},{10,... | collective-permute-start | bytes 786440 | tf_op jit(solution)/shard_map/ppermute | solution.py:20
  50.4 1.3 %collective-permute-start.18 = (bf16[128,1024]{1,0:T(8,128)(2,1)S(1)}, bf16[128,1024]{1,0:T(8,128)(2,1)S(1)}, u32[]{:S(2)}, u32[]{:S(2)}) collective-permute-start(bf16[128,1024]{1,0:T(8,128)(2,1)S(1)} %collective-permute-done.17.refs_7_), channel_id=1, source_target_pairs={{0,8},{4,12},{8,0},{12,4},{16,24},{20,28},{24,16},{28,20},{1,9},{5... | collective-permute-start | bytes 786440 | tf_op jit(solution)/shard_map/ppermute | solution.py:20
  52.2 3.7 %shard_map.121 = (f32[256,1024]{1,0:T(8,128)S(1)}, f32[3,128,128]{2,1,0:T(8,128)S(1)}, bf16[1024,1024]{1,0:T(8,128)(2,1)S(1)}, bf16[3,128,128]{2,1,0:T(8,128)(2,1)S(1)}) custom-call(s32[2,3]{1,0:T(2,128)S(1)} %bitcast.11, s32[1]{0:T(128)S(6)} %copy.13.refs_1_, bf16[128,1024]{1,0:T(8,128)(2,1)S(1)} %copy-done.1, bf16[128,1024]{1,0:T(8,128)(2,1)S(1)} %copy-done.3, ...), custom_call_target="tpu_custom_call" | custom-call | flops 1610612736 | bytes 10584064 | tf_op jit(solution)/shard_map/pallas_call | solution.py:68
  57.6 1.9 %collective-permute-start.16 = (bf16[128,1024]{1,0:T(8,128)(2,1)S(1)}, bf16[128,1024]{1,0:T(8,128)(2,1)S(1)}, u32[]{:S(2)}, u32[]{:S(2)}) collective-permute-start(bf16[128,1024]{1,0:T(8,128)(2,1)S(1)} %collective-permute-done.15.refs_8_), channel_id=1, source_target_pairs={{0,4},{4,0},{8,12},{12,8},{16,20},{20,16},{24,28},{28,24},{1,5},{5... | collective-permute-start | bytes 786440 | tf_op jit(solution)/shard_map/ppermute | solution.py:20
  59.5 2.0 %collective-permute-start.12 = (bf16[128,1024]{1,0:T(8,128)(2,1)S(1)}, bf16[128,1024]{1,0:T(8,128)(2,1)S(1)}, u32[]{:S(2)}, u32[]{:S(2)}) collective-permute-start(bf16[128,1024]{1,0:T(8,128)(2,1)S(1)} %get-tuple-element.57), channel_id=1, source_target_pairs={{0,16},{4,20},{8,24},{12,28},{16,0},{20,4},{24,8},{28,12},{1,17},{... | collective-permute-start | bytes 786440 | tf_op jit(solution)/shard_map/ppermute | solution.py:20
  62.0 2.0 %collective-permute-done.16.refs_4_ = bf16[128,1024]{1,0:T(8,128)(2,1)S(1)} collective-permute-done((bf16[128,1024]{1,0:T(8,128)(2,1)S(1)}, bf16[128,1024]{1,0:T(8,128)(2,1)S(1)}, u32[]{:S(2)}, u32[]{:S(2)}) %collective-permute-start.16) | collective-permute-done | bytes 262176 | tf_op jit(solution)/shard_map/ppermute | solution.py:20
  64.1 1.4 %shard_map.122 = (f32[128,1024]{1,0:T(8,128)S(1)}, bf16[128,1024]{1,0:T(8,128)(2,1)S(1)}, f32[3,128,128]{2,1,0:T(8,128)S(1)}) custom-call(s32[2,3]{1,0:T(2,128)S(1)} %bitcast.12, s32[1]{0:T(128)S(6)} %copy.13.refs_1_, bf16[128,1024]{1,0:T(8,128)(2,1)S(1)} %copy-done.1, bf16[128,1024]{1,0:T(8,128)(2,1)S(1)} %copy-done.3, ...), custom_call_target="tpu_custom_call" | custom-call | flops 536870912 | bytes 4489216 | tf_op jit(solution)/shard_map/pallas_call | solution.py:68
  65.5 1.5 %collective-permute-start.22 = (bf16[3,128,128]{2,1,0:T(8,128)(2,1)S(1)}, bf16[3,128,128]{2,1,0:T(8,128)(2,1)S(1)}, u32[]{:S(2)}, u32[]{:S(2)}) collective-permute-start(bf16[3,128,128]{2,1,0:T(8,128)(2,1)S(1)} %convert_element_type.114), channel_id=1, source_target_pairs={{0,2},{1,3},{2,0},{3,1},{4,6},{5,7},{6,4},{7,5},{8,10},{9,11},{10,... | collective-permute-start | bytes 294920 | tf_op jit(solution)/shard_map/ppermute | solution.py:20
  67.6 3.3 %collective-permute-done.12 = bf16[128,1024]{1,0:T(8,128)(2,1)S(1)} collective-permute-done((bf16[128,1024]{1,0:T(8,128)(2,1)S(1)}, bf16[128,1024]{1,0:T(8,128)(2,1)S(1)}, u32[]{:S(2)}, u32[]{:S(2)}) %collective-permute-start.12) | collective-permute-done | bytes 262176 | tf_op jit(solution)/shard_map/ppermute | solution.py:20
  (79 shorter events, 17.3 us)
Async XLA Ops:
  0.6 12.6 %collective-permute-start.2 = (bf16[1024,2048]{1,0:T(8,128)(2,1)}, bf16[1024,2048]{1,0:T(8,128)(2,1)}, u32[]{:S(2)}, u32[]{:S(2)}) collective-permute-start(bf16[1024,2048]{1,0:T(8,128)(2,1)} %refs_11_.1), channel_id=1, source_target_pairs={{0,1},{1,0},{2,3},{3,2},{4,5},{5,4},{6,7},{7,6},{8,9},{9,8},{10,11... | collective-permute-start | bytes 12582920 | tf_op jit(solution)/shard_map/ppermute | solution.py:20
  1.1 12.1 %collective-permute-start = (bf16[128,1024]{1,0:T(8,128)(2,1)}, bf16[128,1024]{1,0:T(8,128)(2,1)S(1)}, u32[]{:S(2)}, u32[]{:S(2)}) collective-permute-start(bf16[128,1024]{1,0:T(8,128)(2,1)} %refs_2_.3), channel_id=1, source_target_pairs={{0,2},{1,3},{2,0},{3,1},{4,6},{5,7},{6,4},{7,5},{8,10},{9,11},{10,... | collective-permute-start | bytes 786440 | tf_op jit(solution)/shard_map/ppermute | solution.py:20
  7.6 14.8 %collective-permute-start.6 = (bf16[128,1024]{1,0:T(8,128)(2,1)}, bf16[128,1024]{1,0:T(8,128)(2,1)S(1)}, u32[]{:S(2)}, u32[]{:S(2)}) collective-permute-start(bf16[128,1024]{1,0:T(8,128)(2,1)} %refs_1_.4), channel_id=1, source_target_pairs={{0,16},{4,20},{8,24},{12,28},{16,0},{20,4},{24,8},{28,12},{1,17},{... | collective-permute-start | bytes 786440 | tf_op jit(solution)/shard_map/ppermute | solution.py:20
  11.7 8.9 %collective-permute-start.13 = (f32[128,128]{1,0:T(8,128)S(1)}, f32[128,128]{1,0:T(8,128)S(1)}, u32[]{:S(2)}, u32[]{:S(2)}) collective-permute-start(f32[128,128]{1,0:T(8,128)S(1)} %add.61), channel_id=1, source_target_pairs={{0,8},{4,12},{8,0},{12,4},{16,24},{20,28},{24,16},{28,20},{1,9},{5... | collective-permute-start | bytes 196616 | tf_op jit(solution)/shard_map/ppermute | solution.py:20
  20.1 9.5 %collective-permute-start.5 = (bf16[128,1024]{1,0:T(8,128)(2,1)}, bf16[128,1024]{1,0:T(8,128)(2,1)S(1)}, u32[]{:S(2)}, u32[]{:S(2)}) collective-permute-start(bf16[128,1024]{1,0:T(8,128)(2,1)} %get-tuple-element.37), channel_id=1, source_target_pairs={{0,8},{4,12},{8,0},{12,4},{16,24},{20,28},{24,16},{28,20},{1,9},{5... | collective-permute-start | bytes 786440 | tf_op jit(solution)/shard_map/ppermute | solution.py:20
  20.6 10.0 %collective-permute-start.4 = (bf16[128,1024]{1,0:T(8,128)(2,1)}, bf16[128,1024]{1,0:T(8,128)(2,1)S(1)}, u32[]{:S(2)}, u32[]{:S(2)}) collective-permute-start(bf16[128,1024]{1,0:T(8,128)(2,1)} %get-tuple-element.35), channel_id=1, source_target_pairs={{0,4},{4,0},{8,12},{12,8},{16,20},{20,16},{24,28},{28,24},{1,5},{5... | collective-permute-start | bytes 786440 | tf_op jit(solution)/shard_map/ppermute | solution.py:20
  22.4 9.3 %collective-permute-start.8 = (bf16[128,1024]{1,0:T(8,128)(2,1)S(1)}, bf16[128,1024]{1,0:T(8,128)(2,1)S(1)}, u32[]{:S(2)}, u32[]{:S(2)}) collective-permute-start(bf16[128,1024]{1,0:T(8,128)(2,1)S(1)} %get-tuple-element.59), channel_id=1, source_target_pairs={{0,2},{1,3},{2,0},{3,1},{4,6},{5,7},{6,4},{7,5},{8,10},{9,11},{10,... | collective-permute-start | bytes 786440 | tf_op jit(solution)/shard_map/ppermute | solution.py:20
  23.0 12.6 %collective-permute-start.10 = (bf16[128,1024]{1,0:T(8,128)(2,1)}, bf16[128,1024]{1,0:T(8,128)(2,1)S(1)}, u32[]{:S(2)}, u32[]{:S(2)}) collective-permute-start(bf16[128,1024]{1,0:T(8,128)(2,1)} %get-tuple-element.44), channel_id=1, source_target_pairs={{0,4},{4,0},{8,12},{12,8},{16,20},{20,16},{24,28},{28,24},{1,5},{5... | collective-permute-start | bytes 786440 | tf_op jit(solution)/shard_map/ppermute | solution.py:20
  23.5 13.3 %collective-permute-start.3 = (bf16[128,1024]{1,0:T(8,128)(2,1)}, bf16[128,1024]{1,0:T(8,128)(2,1)S(1)}, u32[]{:S(2)}, u32[]{:S(2)}) collective-permute-start(bf16[128,1024]{1,0:T(8,128)(2,1)} %get-tuple-element.33), channel_id=1, source_target_pairs={{0,8},{4,12},{8,0},{12,4},{16,24},{20,28},{24,16},{28,20},{1,9},{5... | collective-permute-start | bytes 786440 | tf_op jit(solution)/shard_map/ppermute | solution.py:20
  31.7 5.9 %collective-permute-start.14 = (f32[128,128]{1,0:T(8,128)S(1)}, f32[128,128]{1,0:T(8,128)S(1)}, u32[]{:S(2)}, u32[]{:S(2)}) collective-permute-start(f32[128,128]{1,0:T(8,128)S(1)} %add.69), channel_id=1, source_target_pairs={{0,16},{4,20},{8,24},{12,28},{16,0},{20,4},{24,8},{28,12},{1,17},{... | collective-permute-start | bytes 196616 | tf_op jit(solution)/shard_map/ppermute | solution.py:20
  33.5 9.2 %collective-permute-start.7 = (bf16[128,1024]{1,0:T(8,128)(2,1)S(1)}, bf16[128,1024]{1,0:T(8,128)(2,1)S(1)}, u32[]{:S(2)}, u32[]{:S(2)}) collective-permute-start(bf16[128,1024]{1,0:T(8,128)(2,1)S(1)} %add_convert_fusion.7), channel_id=1, source_target_pairs={{0,4},{4,0},{8,12},{12,8},{16,20},{20,16},{24,28},{28,24},{1,5},{5... | collective-permute-start | bytes 786440 | tf_op jit(solution)/shard_map/ppermute | solution.py:20
  35.2 12.9 %collective-permute-start.17 = (bf16[128,1024]{1,0:T(8,128)(2,1)S(1)}, bf16[128,1024]{1,0:T(8,128)(2,1)S(1)}, u32[]{:S(2)}, u32[]{:S(2)}) collective-permute-start(bf16[128,1024]{1,0:T(8,128)(2,1)S(1)} %collective-permute-done.8.refs_5_), channel_id=1, source_target_pairs={{0,4},{4,0},{8,12},{12,8},{16,20},{20,16},{24,28},{28,24},{1,5},{5... | collective-permute-start | bytes 786440 | tf_op jit(solution)/shard_map/ppermute | solution.py:20
  35.6 13.0 %collective-permute-start.20 = (bf16[128,1024]{1,0:T(8,128)(2,1)S(1)}, bf16[128,1024]{1,0:T(8,128)(2,1)S(1)}, u32[]{:S(2)}, u32[]{:S(2)}) collective-permute-start(bf16[128,1024]{1,0:T(8,128)(2,1)S(1)} %collective-permute-done.8.refs_5_), channel_id=1, source_target_pairs={{0,8},{4,12},{8,0},{12,4},{16,24},{20,28},{24,16},{28,20},{1,9},{5... | collective-permute-start | bytes 786440 | tf_op jit(solution)/shard_map/ppermute | solution.py:20
  36.8 13.6 %collective-permute-start.15 = (bf16[128,1024]{1,0:T(8,128)(2,1)S(1)}, bf16[128,1024]{1,0:T(8,128)(2,1)S(1)}, u32[]{:S(2)}, u32[]{:S(2)}) collective-permute-start(bf16[128,1024]{1,0:T(8,128)(2,1)S(1)} %get-tuple-element.47.refs_4_), channel_id=1, source_target_pairs={{0,8},{4,12},{8,0},{12,4},{16,24},{20,28},{24,16},{28,20},{1,9},{5... | collective-permute-start | bytes 786440 | tf_op jit(solution)/shard_map/ppermute | solution.py:20
  42.8 8.9 %collective-permute-start.19 = (bf16[128,1024]{1,0:T(8,128)(2,1)S(1)}, bf16[128,1024]{1,0:T(8,128)(2,1)S(1)}, u32[]{:S(2)}, u32[]{:S(2)}) collective-permute-start(bf16[128,1024]{1,0:T(8,128)(2,1)S(1)} %get-tuple-element.47.refs_4_), channel_id=1, source_target_pairs={{0,4},{4,0},{8,12},{12,8},{16,20},{20,16},{24,28},{28,24},{1,5},{5... | collective-permute-start | bytes 786440 | tf_op jit(solution)/shard_map/ppermute | solution.py:20
  43.4 14.0 %collective-permute-start.11 = (bf16[128,1024]{1,0:T(8,128)(2,1)S(1)}, bf16[128,1024]{1,0:T(8,128)(2,1)S(1)}, u32[]{:S(2)}, u32[]{:S(2)}) collective-permute-start(bf16[128,1024]{1,0:T(8,128)(2,1)S(1)} %add_convert_fusion.6), channel_id=1, source_target_pairs={{0,8},{4,12},{8,0},{12,4},{16,24},{20,28},{24,16},{28,20},{1,9},{5... | collective-permute-start | bytes 786440 | tf_op jit(solution)/shard_map/ppermute | solution.py:20
  48.1 9.5 %collective-permute-start.24 = (bf16[128,64]{1,0:T(8,128)(2,1)S(1)}, bf16[128,64]{1,0:T(8,128)(2,1)S(1)}, u32[]{:S(2)}, u32[]{:S(2)}) collective-permute-start(bf16[128,64]{1,0:T(8,128)(2,1)S(1)} %slice.9), channel_id=1, source_target_pairs={{0,2},{1,3},{2,0},{3,1},{4,6},{5,7},{6,4},{7,5},{8,10},{9,11},{10,... | collective-permute-start | bytes 49160 | tf_op jit(solution)/shard_map/ppermute | solution.py:20
  48.6 8.8 %collective-permute-start.9 = (bf16[128,1024]{1,0:T(8,128)(2,1)S(1)}, bf16[128,1024]{1,0:T(8,128)(2,1)S(1)}, u32[]{:S(2)}, u32[]{:S(2)}) collective-permute-start(bf16[128,1024]{1,0:T(8,128)(2,1)S(1)} %add_convert_fusion.4), channel_id=1, source_target_pairs={{0,2},{1,3},{2,0},{3,1},{4,6},{5,7},{6,4},{7,5},{8,10},{9,11},{10,... | collective-permute-start | bytes 786440 | tf_op jit(solution)/shard_map/ppermute | solution.py:20
  50.4 11.6 %collective-permute-start.18 = (bf16[128,1024]{1,0:T(8,128)(2,1)S(1)}, bf16[128,1024]{1,0:T(8,128)(2,1)S(1)}, u32[]{:S(2)}, u32[]{:S(2)}) collective-permute-start(bf16[128,1024]{1,0:T(8,128)(2,1)S(1)} %collective-permute-done.17.refs_7_), channel_id=1, source_target_pairs={{0,8},{4,12},{8,0},{12,4},{16,24},{20,28},{24,16},{28,20},{1,9},{5... | collective-permute-start | bytes 786440 | tf_op jit(solution)/shard_map/ppermute | solution.py:20
  57.6 6.4 %collective-permute-start.16 = (bf16[128,1024]{1,0:T(8,128)(2,1)S(1)}, bf16[128,1024]{1,0:T(8,128)(2,1)S(1)}, u32[]{:S(2)}, u32[]{:S(2)}) collective-permute-start(bf16[128,1024]{1,0:T(8,128)(2,1)S(1)} %collective-permute-done.15.refs_8_), channel_id=1, source_target_pairs={{0,4},{4,0},{8,12},{12,8},{16,20},{20,16},{24,28},{28,24},{1,5},{5... | collective-permute-start | bytes 786440 | tf_op jit(solution)/shard_map/ppermute | solution.py:20
  59.5 11.4 %collective-permute-start.12 = (bf16[128,1024]{1,0:T(8,128)(2,1)S(1)}, bf16[128,1024]{1,0:T(8,128)(2,1)S(1)}, u32[]{:S(2)}, u32[]{:S(2)}) collective-permute-start(bf16[128,1024]{1,0:T(8,128)(2,1)S(1)} %get-tuple-element.57), channel_id=1, source_target_pairs={{0,16},{4,20},{8,24},{12,28},{16,0},{20,4},{24,8},{28,12},{1,17},{... | collective-permute-start | bytes 786440 | tf_op jit(solution)/shard_map/ppermute | solution.py:20
  62.0 10.0 %collective-permute-start.25 = (f32[1024,64]{0,1:T(8,128)S(1)}, f32[1024,64]{0,1:T(8,128)S(1)}, u32[]{:S(2)}, u32[]{:S(2)}) collective-permute-start(f32[1024,64]{0,1:T(8,128)S(1)} %fusion), channel_id=1, source_target_pairs={{0,1},{1,0},{2,3},{3,2},{4,5},{5,4},{6,7},{7,6},{8,9},{9,8},{10,11... | collective-permute-start | bytes 786440 | tf_op jit(solution)/shard_map/ppermute | solution.py:20
  65.5 6.4 %collective-permute-start.22 = (bf16[3,128,128]{2,1,0:T(8,128)(2,1)S(1)}, bf16[3,128,128]{2,1,0:T(8,128)(2,1)S(1)}, u32[]{:S(2)}, u32[]{:S(2)}) collective-permute-start(bf16[3,128,128]{2,1,0:T(8,128)(2,1)S(1)} %convert_element_type.114), channel_id=1, source_target_pairs={{0,2},{1,3},{2,0},{3,1},{4,6},{5,7},{6,4},{7,5},{8,10},{9,11},{10,... | collective-permute-start | bytes 294920 | tf_op jit(solution)/shard_map/ppermute | solution.py:20
  67.0 7.9 %collective-permute-start.21 = (bf16[128,1024]{1,0:T(8,128)(2,1)S(1)}, bf16[128,1024]{1,0:T(8,128)(2,1)S(1)}, u32[]{:S(2)}, u32[]{:S(2)}) collective-permute-start(bf16[128,1024]{1,0:T(8,128)(2,1)S(1)} %get-tuple-element.54), channel_id=1, source_target_pairs={{0,2},{1,3},{2,0},{3,1},{4,6},{5,7},{6,4},{7,5},{8,10},{9,11},{10,... | collective-permute-start | bytes 786440 | tf_op jit(solution)/shard_map/ppermute | solution.py:20
  (15 other events, 259.6 us)

commit v4 on v3

--- a/solution.py
+++ b/solution.py
@@ -167,21 +167,19 @@
     return pltpu.make_async_copy(w_in[0].at[:, half], target, sem)
 
 
-def pull(index_ref, count_ref, x_refs, g_refs, vals_ref, w_ref, acc, both, blocks_ref, q, p):
+def pull(index_ref, count_ref, x_refs, g_ref, vals_ref, w_ref, acc, blocks_ref, q, p):
     r, c, t = position()
     rows, shard = x_refs[0].shape
-    for part in range(2):
-        both[part * rows : (part + 1) * rows, :] = g_refs[part][...]
-    acc[...] += lax.dot_general(both[...], w_ref[...], NT, preferred_element_type=F32)
+    acc[...] += lax.dot_general(g_ref[...], w_ref[...], NT, preferred_element_type=F32)
 
     def body(slot, block_rows, block_columns):
-        g_columns = both[:, block_columns]
+        g_columns = g_ref[:, block_columns]
         acc[:, block_rows] += lax.dot_general(
             g_columns, vals_ref[slot], NT, preferred_element_type=F32
         )
-        for part in range(2):
+        for part, x_ref in enumerate(x_refs):
             blocks_ref[slot] += lax.dot_general(
-                x_refs[part][:, block_rows],
+                x_ref[:, block_rows],
                 g_columns[part * rows : (part + 1) * rows],
                 TN,
                 preferred_element_type=F32,
@@ -193,7 +191,7 @@
 
 def early_kernel(index_ref, count_ref, ready, *refs):
     x_refs, g_refs, vals_in, w_in = refs[:2], refs[2:8], refs[8], refs[9:11]
-    acc, blocks_ref, last_ref, vals_ref, w_ref, both, sems = refs[11:]
+    near_ref, far_ref, blocks_ref, last_ref, vals_ref, w_ref, both, acc, sems = refs[11:]
     vals_copy = pltpu.make_async_copy(vals_in, vals_ref, sems.at[4])
     vals_copy.start()
     chunks = ((0, 0), (0, 1), (1, 0))
@@ -203,24 +201,26 @@
     blocks_ref[...] = jnp.zeros_like(blocks_ref)
     vals_copy.wait()
     ready()
+    rows = near_ref.shape[0]
     for i, (q, p) in enumerate(chunks):
+        for part in range(2):
+            both[part * rows : (part + 1) * rows, :] = g_refs[2 * i + part][...]
         copies[i].wait()
-        pair = g_refs[2 * i : 2 * i + 2]
-        pull(index_ref, count_ref, x_refs, pair, vals_ref, w_ref.at[i], acc, both, blocks_ref, q, p)
+        pull(index_ref, count_ref, x_refs, both, vals_ref, w_ref.at[i], acc, blocks_ref, q, p)
+    near_ref[...] = acc[:rows, :]
+    far_ref[...] = acc[rows:, :]
     last_copy.wait()
 
 
-def late_kernel(index_ref, count_ref, ready, *refs):
-    x_refs, g_refs, acc_in, blocks_in, vals_ref, w_ref = refs[:2], refs[2:4], *refs[4:8]
-    own_ref, *rest_refs, blocks_ref, acc, both = refs[8:]
+def late_kernel(index_ref, count_ref, ready, x_ref, g_ref, acc_in, blocks_in, vals_ref, w_ref, *refs):
+    *out_refs, blocks_ref, acc = refs
     acc[...] = acc_in[...]
     blocks_ref[...] = blocks_in[...]
     ready()
-    pull(index_ref, count_ref, x_refs, g_refs, vals_ref, w_ref, acc, both, blocks_ref, 1, 1)
-    rows = own_ref.shape[0]
-    own_ref[...] = acc[:rows, :]
-    for place, rest_ref in enumerate(rest_refs):
-        rest_ref[...] = acc[(place + 1) * rows : (place + 2) * rows, :].astype(BF16)
+    pull(index_ref, count_ref, (x_ref,), g_ref, vals_ref, w_ref, acc, blocks_ref, 1, 1)
+    rows = out_refs[0].shape[0]
+    for place, out_ref in enumerate(out_refs):
+        out_ref[...] = acc[place * rows : (place + 1) * rows, :].astype(out_ref.dtype)
 
 
 def on_device(activations, w_base, blk_vals, blk_index, blk_count, a_down, b_up, grad_out):
@@ -314,7 +314,7 @@
     while mask < lax.axis_size("feat"):
         low = low + swap(low, "feat", mask)
         mask *= 2
-    far = added(far_00, after(got_far_01, g_far))
+    far = added(far_00, after(got_far_01, g_near, g_far))
 
     parts = parted(far, far)
     got_parts = {j: swap(parts[j], "tok", 2 * j) for j in range(half_groups, groups)}
@@ -330,21 +330,23 @@
     low = after(low.astype(BF16))
     u_half, v_half = low[:, :rank], low[:, rank:]
     up = jnp.dot(u_half.T, grad_out, preferred_element_type=F32)
-    up = (up + swap(up, "tok", 1)).astype(BF16)
+    up = (up + after(swap(up, "tok", 1))).astype(BF16)
     got_v = [swap(v_half, "tok", 2 * j) for j in range(1, groups)]
     v_groups = [v_half] + after(got_v, near)
     down = tree_sum(
         [jnp.dot(x.T, v, preferred_element_type=F32) for x, v in zip(x_groups, v_groups)]
     )
 
-    acc, blocks, last_tile, vals_seen = call(
+    short = (set_rows, shard)
+    acc_near, acc_far, blocks, last_tile, vals_seen = call(
         early_kernel,
         32,
         1,
-        [(tall, F32), (blk_vals.shape, F32), (tile_half, BF16), (blk_vals.shape, BF16)],
+        [(short, F32)] * 2 + [(blk_vals.shape, F32), (tile_half, BF16), (blk_vals.shape, BF16)],
         [
             pltpu.VMEM((3, *tile_half), BF16),
             pltpu.VMEM(tall, BF16),
+            pltpu.VMEM(tall, F32),
             pltpu.SemaphoreType.DMA((5,)),
         ],
         6 * product,
@@ -352,26 +354,36 @@
         (*x_pair, after(g_near), g_far, g_near_01, g_far_01, g_near_10, g_far_10),
         (blk_vals, w_base, other_tile),
     )
+    piece = (tok_rows, shard)
+    *rest_far, blocks = call(
+        late_kernel,
+        32,
+        0.01,
+        [(piece, BF16)] * half_groups + [(blk_vals.shape, F32)],
+        [pltpu.VMEM(short, F32)],
+        product,
+        scalars,
+        (x_far, after(g_far_11), acc_far, blocks, vals_seen, last_tile),
+    )
     own, *rest, blocks = call(
         late_kernel,
         32,
-        1,
-        [((tok_rows, shard), F32)]
-        + [((tok_rows, shard), BF16)] * (groups - 1)
-        + [(blk_vals.shape, F32)],
-        [pltpu.VMEM(tall, F32), pltpu.VMEM(tall, BF16)],
-        2 * product,
+        0.01,
+        [(piece, F32)] + [(piece, BF16)] * (half_groups - 1) + [(blk_vals.shape, F32)],
+        [pltpu.VMEM(short, F32)],
+        product,
         scalars,
-        (*x_pair, after(g_near_11), g_far_11, acc, blocks, vals_seen, last_tile),
-    )
+        (x_near, g_near_11, acc_near, blocks, vals_seen, last_tile),
+    )
+    rest = [*rest, *rest_far]
     rest = after(rest)
     got_rest = [swap(rest[j - 1], "tok", 2 * j) for j in range(1, groups)]
 
     blocks = blocks.astype(BF16)
-    down = down + swap(down, "tok", 1)
+    down = down + after(swap(down, "tok", 1))
     mask = 2
     while mask < n_tok:
-        up = up.astype(F32) + swap(up.astype(BF16), "tok", mask).astype(F32)
+        up = up.astype(F32) + after(swap(up.astype(BF16), "tok", mask)).astype(F32)
         blocks = blocks + swap(blocks, "tok", mask)
         mask *= 2
     blocks = blocks.astype(F32) + swap(blocks, "tok", 1).astype(F32)

time: 76 us -> 75.2 us (0.989)
  starting transfers between devices: 32.2 us -> 30.3 us
  Pallas kernels: 13.4 us -> 15 us
    ppermute x28, starting transfers between devices: 32.2 us -> 30.3 us  [swap(): return lax.ppermute(value, axis, [(i, i ^ mask) for i in range(size)])]
    pallas_call x4 -> x5, Pallas kernels: 13.4 us -> 15 us  [call(): pl.pallas_call(body, out_shape=shapes, in_specs=[apart] * len(scalars) +...]
  transfers between devices with their start and end apart: 28 -> 28, of which waited for: 10 -> 11; matrix products, arithmetic and copies ran while one was open for 10% -> 10% of each run, Pallas kernels for 18% -> 20%
where the time goes in v4:
time: 75.2 us; the launch traced here: 75 us
  starting transfers between devices  30.3 us (40%)
  waiting for transfers between devices  19.2 us (26%)
  Pallas kernels  15 us (20%)
  other arithmetic  6.32 us (8%)
  matrix products  1.85 us (2%)
  between operations  1.58 us (2%)
  local copies, waits for them, and re-layouts  0.83 us (1%)
    ppermute x28, starting transfers between devices, swap(): return lax.ppermute(value, axis, [(i, i ^ mask) for i in range(size)])  30.3 us
    ppermute x28, waiting for transfers between devices, swap(): return lax.ppermute(value, axis, [(i, i ^ mask) for i in range(size)])  19.2 us
    pallas_call x5, Pallas kernels, call(): pl.pallas_call(body, out_shape=shapes, in_specs=[apart] * len(scalars) +...  15 us
    convert_element_type x3, other arithmetic, added(): return sum((term.astype(F32) for term in terms)).astype(BF16)  2.16 us
  transfers between devices with their start and end apart: 28, of which 11 were waited for; matrix products, arithmetic and copies ran while one was open for 10% of the time, Pallas kernels for 20%

profile of v4, /device:TPU:0, one launch (start us, length us, event | category | flops | bytes accessed | tf_op | source)
XLA Modules:
  0.0 75.0 jit_solution(11301423167677598862)
XLA Ops:
  1.1 2.6 %collective-permute-start = (bf16[128,1024]{1,0:T(8,128)(2,1)}, bf16[128,1024]{1,0:T(8,128)(2,1)S(1)}, u32[]{:S(2)}, u32[]{:S(2)}) collective-permute-start(bf16[128,1024]{1,0:T(8,128)(2,1)} %refs_2_.3), channel_id=1, source_target_pairs={{0,2},{1,3},{2,0},{3,1},{4,6},{5,7},{6,4},{7,5},{8,10},{9,11},{10,... | collective-permute-start | bytes 786440 | tf_op jit(solution)/shard_map/ppermute | solution.py:20
  3.7 2.2 %shard_map.119 = f32[128,128]{1,0:T(8,128)} custom-call(bf16[128,1024]{1,0:T(8,128)(2,1)} %refs_2_.3, bf16[128,1024]{1,0:T(8,128)(2,1)} %refs_1_.5, bf16[64,1024]{1,0:T(8,128)(2,1)} %bitcast.14, bf16[64,1024]{1,0:T(8,128)(2,1)} %refs_3_.2), custom_call_target="tpu_custom_call" | custom-call | flops 33554432 | bytes 786432 | tf_op jit(solution)/shard_map/pallas_call | solution.py:68
  6.0 1.6 %collective-permute-start.1 = (f32[128,128]{1,0:T(8,128)}, f32[128,128]{1,0:T(8,128)S(1)}, u32[]{:S(2)}, u32[]{:S(2)}) collective-permute-start(f32[128,128]{1,0:T(8,128)} %shard_map.119), channel_id=1, source_target_pairs={{0,4},{4,0},{8,12},{12,8},{16,20},{20,16},{24,28},{28,24},{1,5},{5... | collective-permute-start | bytes 196616 | tf_op jit(solution)/shard_map/ppermute | solution.py:20
  7.6 2.6 %collective-permute-start.6 = (bf16[128,1024]{1,0:T(8,128)(2,1)}, bf16[128,1024]{1,0:T(8,128)(2,1)S(1)}, u32[]{:S(2)}, u32[]{:S(2)}) collective-permute-start(bf16[128,1024]{1,0:T(8,128)(2,1)} %refs_1_.5), channel_id=1, source_target_pairs={{0,16},{4,20},{8,24},{12,28},{16,0},{20,4},{24,8},{28,12},{1,17},{... | collective-permute-start | bytes 786440 | tf_op jit(solution)/shard_map/ppermute | solution.py:20
  11.7 1.6 %collective-permute-start.13 = (f32[128,128]{1,0:T(8,128)S(1)}, f32[128,128]{1,0:T(8,128)S(1)}, u32[]{:S(2)}, u32[]{:S(2)}) collective-permute-start(f32[128,128]{1,0:T(8,128)S(1)} %add.61), channel_id=1, source_target_pairs={{0,8},{4,12},{8,0},{12,4},{16,24},{20,28},{24,16},{28,20},{1,9},{5... | collective-permute-start | bytes 196616 | tf_op jit(solution)/shard_map/ppermute | solution.py:20
  14.0 6.1 %shard_map.120 = (bf16[128,1024]{1,0:T(8,128)(2,1)}, bf16[128,1024]{1,0:T(8,128)(2,1)}, bf16[128,1024]{1,0:T(8,128)(2,1)}, bf16[128,1024]{1,0:T(8,128)(2,1)}, bf...) custom-call(s32[2,3]{1,0:T(2,128)} %bitcast.10, ...), custom_call_target="tpu_custom_call" | custom-call | flops 2147483648 | bytes 9011200 | tf_op jit(solution)/shard_map/pallas_call | solution.py:68
  20.5 1.4 %collective-permute-start.4 = (bf16[128,1024]{1,0:T(8,128)(2,1)}, bf16[128,1024]{1,0:T(8,128)(2,1)S(1)}, u32[]{:S(2)}, u32[]{:S(2)}) collective-permute-start(bf16[128,1024]{1,0:T(8,128)(2,1)} %get-tuple-element.37), channel_id=1, source_target_pairs={{0,4},{4,0},{8,12},{12,8},{16,20},{20,16},{24,28},{28,24},{1,5},{5... | collective-permute-start | bytes 786440 | tf_op jit(solution)/shard_map/ppermute | solution.py:20
  23.0 1.1 %collective-permute-start.3 = (bf16[128,1024]{1,0:T(8,128)(2,1)}, bf16[128,1024]{1,0:T(8,128)(2,1)S(1)}, u32[]{:S(2)}, u32[]{:S(2)}) collective-permute-start(bf16[128,1024]{1,0:T(8,128)(2,1)} %get-tuple-element.35), channel_id=1, source_target_pairs={{0,8},{4,12},{8,0},{12,4},{16,24},{20,28},{24,16},{28,20},{1,9},{5... | collective-permute-start | bytes 786440 | tf_op jit(solution)/shard_map/ppermute | solution.py:20
  24.9 4.7 %collective-permute-done.5 = bf16[128,1024]{1,0:T(8,128)(2,1)S(1)} collective-permute-done((bf16[128,1024]{1,0:T(8,128)(2,1)}, bf16[128,1024]{1,0:T(8,128)(2,1)S(1)}, u32[]{:S(2)}, u32[]{:S(2)}) %collective-permute-start.5) | collective-permute-done | bytes 262176 | tf_op jit(solution)/shard_map/ppermute | solution.py:20
  31.7 2.5 %collective-permute-start.14 = (f32[128,128]{1,0:T(8,128)S(1)}, f32[128,128]{1,0:T(8,128)S(1)}, u32[]{:S(2)}, u32[]{:S(2)}) collective-permute-start(f32[128,128]{1,0:T(8,128)S(1)} %add.69), channel_id=1, source_target_pairs={{0,16},{4,20},{8,24},{12,28},{16,0},{20,4},{24,8},{28,12},{1,17},{... | collective-permute-start | bytes 196616 | tf_op jit(solution)/shard_map/ppermute | solution.py:20
  34.2 1.2 %collective-permute-start.7 = (bf16[128,1024]{1,0:T(8,128)(2,1)S(1)}, bf16[128,1024]{1,0:T(8,128)(2,1)S(1)}, u32[]{:S(2)}, u32[]{:S(2)}) collective-permute-start(bf16[128,1024]{1,0:T(8,128)(2,1)S(1)} %add_convert_fusion.7), channel_id=1, source_target_pairs={{0,4},{4,0},{8,12},{12,8},{16,20},{20,16},{24,28},{28,24},{1,5},{5... | collective-permute-start | bytes 786440 | tf_op jit(solution)/shard_map/ppermute | solution.py:20
  37.3 1.2 %collective-permute-start.18 = (bf16[128,1024]{1,0:T(8,128)(2,1)S(1)}, bf16[128,1024]{1,0:T(8,128)(2,1)S(1)}, u32[]{:S(2)}, u32[]{:S(2)}) collective-permute-start(bf16[128,1024]{1,0:T(8,128)(2,1)S(1)} %collective-permute-done.8.refs_5_), channel_id=1, source_target_pairs={{0,4},{4,0},{8,12},{12,8},{16,20},{20,16},{24,28},{28,24},{1,5},{5... | collective-permute-start | bytes 786440 | tf_op jit(solution)/shard_map/ppermute | solution.py:20
  39.2 4.2 %collective-permute-done.7 = bf16[128,1024]{1,0:T(8,128)(2,1)S(1)} collective-permute-done((bf16[128,1024]{1,0:T(8,128)(2,1)S(1)}, bf16[128,1024]{1,0:T(8,128)(2,1)S(1)}, u32[]{:S(2)}, u32[]{:S(2)}) %collective-permute-start.7) | collective-permute-done | bytes 262176 | tf_op jit(solution)/shard_map/ppermute | solution.py:20
  45.9 2.2 %collective-permute-done.17.refs_6_ = bf16[128,1024]{1,0:T(8,128)(2,1)S(1)} collective-permute-done((bf16[128,1024]{1,0:T(8,128)(2,1)S(1)}, bf16[128,1024]{1,0:T(8,128)(2,1)S(1)}, u32[]{:S(2)}, u32[]{:S(2)}) %collective-permute-start.17) | collective-permute-done | bytes 262176 | tf_op jit(solution)/shard_map/ppermute | solution.py:20
  48.6 2.3 %collective-permute-done.18.refs_7_ = bf16[128,1024]{1,0:T(8,128)(2,1)S(1)} collective-permute-done((bf16[128,1024]{1,0:T(8,128)(2,1)S(1)}, bf16[128,1024]{1,0:T(8,128)(2,1)S(1)}, u32[]{:S(2)}, u32[]{:S(2)}) %collective-permute-start.18) | collective-permute-done | bytes 262176 | tf_op jit(solution)/shard_map/ppermute | solution.py:20
  50.9 2.4 %collective-permute-start.20 = (bf16[128,1024]{1,0:T(8,128)(2,1)S(1)}, bf16[128,1024]{1,0:T(8,128)(2,1)S(1)}, u32[]{:S(2)}, u32[]{:S(2)}) collective-permute-start(bf16[128,1024]{1,0:T(8,128)(2,1)S(1)} %collective-permute-done.18.refs_7_), channel_id=1, source_target_pairs={{0,8},{4,12},{8,0},{12,4},{16,24},{20,28},{24,16},{28,20},{1,9},{5... | collective-permute-start | bytes 786440 | tf_op jit(solution)/shard_map/ppermute | solution.py:20
  53.6 3.8 %shard_map.121 = (f32[128,1024]{1,0:T(8,128)S(1)}, f32[128,1024]{1,0:T(8,128)S(1)}, f32[3,128,128]{2,1,0:T(8,128)S(1)}, bf16[1024,1024]{1,0:T(8,128)(2,1)S(1)}, bf16[3,128,128]{2,1,0:T(8,128)(2,1)S(1)}) custom-call(s32[2,3]{1,0:T(2,128)S(1)} %bitcast.11, s32[1]{0:T(128)S(6)} %copy.13.refs_1_, bf16[128,1024]{1,0:T(8,128)(2,1)S(1)} %copy-done.1, ...), custom_call_target="tpu_custom_call" | custom-call | flops 1610612736 | bytes 10584064 | tf_op jit(solution)/shard_map/pallas_call | solution.py:68
  59.2 1.2 %collective-permute-start.12 = (bf16[128,1024]{1,0:T(8,128)(2,1)S(1)}, bf16[128,1024]{1,0:T(8,128)(2,1)S(1)}, u32[]{:S(2)}, u32[]{:S(2)}) collective-permute-start(bf16[128,1024]{1,0:T(8,128)(2,1)S(1)} %get-tuple-element.61), channel_id=1, source_target_pairs={{0,16},{4,20},{8,24},{12,28},{16,0},{20,4},{24,8},{28,12},{1,17},{... | collective-permute-start | bytes 786440 | tf_op jit(solution)/shard_map/ppermute | solution.py:20
  60.4 1.2 %collective-permute-start.16 = (bf16[128,1024]{1,0:T(8,128)(2,1)S(1)}, bf16[128,1024]{1,0:T(8,128)(2,1)S(1)}, u32[]{:S(2)}, u32[]{:S(2)}) collective-permute-start(bf16[128,1024]{1,0:T(8,128)(2,1)S(1)} %collective-permute-done.15.refs_8_), channel_id=1, source_target_pairs={{0,4},{4,0},{8,12},{12,8},{16,20},{20,16},{24,28},{28,24},{1,5},{5... | collective-permute-start | bytes 786440 | tf_op jit(solution)/shard_map/ppermute | solution.py:20
  61.6 1.4 %shard_map.122 = (bf16[128,1024]{1,0:T(8,128)(2,1)S(1)}, f32[3,128,128]{2,1,0:T(8,128)S(1)}) custom-call(s32[2,3]{1,0:T(2,128)S(1)} %bitcast.12, s32[1]{0:T(128)S(6)} %copy.13.refs_1_, bf16[128,1024]{1,0:T(8,128)(2,1)S(1)} %copy-done.3, bf16[128,1024]{1,0:T(8,128)(2,1)S(1)} %collective-permute-done.20.refs_3_, f32[128,1024]{1,0:T(8,128)S(1)} %get-tuple-element.52.refs_4_, ...), custom_call_target="tpu_custom_call" | custom-call | flops 2684354 | bytes 34406 | tf_op jit(solution)/shard_map/pallas_call | solution.py:68
  63.1 1.3 %collective-permute-start.21 = (bf16[128,1024]{1,0:T(8,128)(2,1)S(1)}, bf16[128,1024]{1,0:T(8,128)(2,1)S(1)}, u32[]{:S(2)}, u32[]{:S(2)}) collective-permute-start(bf16[128,1024]{1,0:T(8,128)(2,1)S(1)} %get-tuple-element.58), channel_id=1, source_target_pairs={{0,2},{1,3},{2,0},{3,1},{4,6},{5,7},{6,4},{7,5},{8,10},{9,11},{10,... | collective-permute-start | bytes 786440 | tf_op jit(solution)/shard_map/ppermute | solution.py:20
  65.0 1.8 %collective-permute-done.16.refs_3_ = bf16[128,1024]{1,0:T(8,128)(2,1)S(1)} collective-permute-done((bf16[128,1024]{1,0:T(8,128)(2,1)S(1)}, bf16[128,1024]{1,0:T(8,128)(2,1)S(1)}, u32[]{:S(2)}, u32[]{:S(2)}) %collective-permute-start.16) | collective-permute-done | bytes 262176 | tf_op jit(solution)/shard_map/ppermute | solution.py:20
  66.8 1.4 %shard_map.123 = (f32[128,1024]{1,0:T(8,128)S(1)}, f32[3,128,128]{2,1,0:T(8,128)S(1)}) custom-call(s32[2,3]{1,0:T(2,128)S(1)} %bitcast.13, s32[1]{0:T(128)S(6)} %copy.13.refs_1_, bf16[128,1024]{1,0:T(8,128)(2,1)S(1)} %copy-done.1, bf16[128,1024]{1,0:T(8,128)(2,1)S(1)} %collective-permute-done.16.refs_3_, f32[128,1024]{1,0:T(8,128)S(1)} %get-tuple-element.51.refs_4_, ...), custom_call_target="tpu_custom_call" | custom-call | flops 2684354 | bytes 34406 | tf_op jit(solution)/shard_map/pallas_call | solution.py:68
  70.3 1.1 %collective-permute-done.12 = bf16[128,1024]{1,0:T(8,128)(2,1)S(1)} collective-permute-done((bf16[128,1024]{1,0:T(8,128)(2,1)S(1)}, bf16[128,1024]{1,0:T(8,128)(2,1)S(1)}, u32[]{:S(2)}, u32[]{:S(2)}) %collective-permute-start.12) | collective-permute-done | bytes 262176 | tf_op jit(solution)/shard_map/ppermute | solution.py:20
  (80 shorter events, 20.1 us)
Async XLA Ops:
  0.6 12.7 %collective-permute-start.2 = (bf16[1024,2048]{1,0:T(8,128)(2,1)}, bf16[1024,2048]{1,0:T(8,128)(2,1)}, u32[]{:S(2)}, u32[]{:S(2)}) collective-permute-start(bf16[1024,2048]{1,0:T(8,128)(2,1)} %refs_11_.1), channel_id=1, source_target_pairs={{0,1},{1,0},{2,3},{3,2},{4,5},{5,4},{6,7},{7,6},{8,9},{9,8},{10,11... | collective-permute-start | bytes 12582920 | tf_op jit(solution)/shard_map/ppermute | solution.py:20
  1.1 12.2 %collective-permute-start = (bf16[128,1024]{1,0:T(8,128)(2,1)}, bf16[128,1024]{1,0:T(8,128)(2,1)S(1)}, u32[]{:S(2)}, u32[]{:S(2)}) collective-permute-start(bf16[128,1024]{1,0:T(8,128)(2,1)} %refs_2_.3), channel_id=1, source_target_pairs={{0,2},{1,3},{2,0},{3,1},{4,6},{5,7},{6,4},{7,5},{8,10},{9,11},{10,... | collective-permute-start | bytes 786440 | tf_op jit(solution)/shard_map/ppermute | solution.py:20
  7.6 14.8 %collective-permute-start.6 = (bf16[128,1024]{1,0:T(8,128)(2,1)}, bf16[128,1024]{1,0:T(8,128)(2,1)S(1)}, u32[]{:S(2)}, u32[]{:S(2)}) collective-permute-start(bf16[128,1024]{1,0:T(8,128)(2,1)} %refs_1_.5), channel_id=1, source_target_pairs={{0,16},{4,20},{8,24},{12,28},{16,0},{20,4},{24,8},{28,12},{1,17},{... | collective-permute-start | bytes 786440 | tf_op jit(solution)/shard_map/ppermute | solution.py:20
  11.7 8.8 %collective-permute-start.13 = (f32[128,128]{1,0:T(8,128)S(1)}, f32[128,128]{1,0:T(8,128)S(1)}, u32[]{:S(2)}, u32[]{:S(2)}) collective-permute-start(f32[128,128]{1,0:T(8,128)S(1)} %add.61), channel_id=1, source_target_pairs={{0,8},{4,12},{8,0},{12,4},{16,24},{20,28},{24,16},{28,20},{1,9},{5... | collective-permute-start | bytes 196616 | tf_op jit(solution)/shard_map/ppermute | solution.py:20
  20.1 9.5 %collective-permute-start.5 = (bf16[128,1024]{1,0:T(8,128)(2,1)}, bf16[128,1024]{1,0:T(8,128)(2,1)S(1)}, u32[]{:S(2)}, u32[]{:S(2)}) collective-permute-start(bf16[128,1024]{1,0:T(8,128)(2,1)} %get-tuple-element.39), channel_id=1, source_target_pairs={{0,8},{4,12},{8,0},{12,4},{16,24},{20,28},{24,16},{28,20},{1,9},{5... | collective-permute-start | bytes 786440 | tf_op jit(solution)/shard_map/ppermute | solution.py:20
  20.5 10.2 %collective-permute-start.4 = (bf16[128,1024]{1,0:T(8,128)(2,1)}, bf16[128,1024]{1,0:T(8,128)(2,1)S(1)}, u32[]{:S(2)}, u32[]{:S(2)}) collective-permute-start(bf16[128,1024]{1,0:T(8,128)(2,1)} %get-tuple-element.37), channel_id=1, source_target_pairs={{0,4},{4,0},{8,12},{12,8},{16,20},{20,16},{24,28},{28,24},{1,5},{5... | collective-permute-start | bytes 786440 | tf_op jit(solution)/shard_map/ppermute | solution.py:20
  22.4 9.3 %collective-permute-start.8 = (bf16[128,1024]{1,0:T(8,128)(2,1)S(1)}, bf16[128,1024]{1,0:T(8,128)(2,1)S(1)}, u32[]{:S(2)}, u32[]{:S(2)}) collective-permute-start(bf16[128,1024]{1,0:T(8,128)(2,1)S(1)} %get-tuple-element.63), channel_id=1, source_target_pairs={{0,2},{1,3},{2,0},{3,1},{4,6},{5,7},{6,4},{7,5},{8,10},{9,11},{10,... | collective-permute-start | bytes 786440 | tf_op jit(solution)/shard_map/ppermute | solution.py:20
  23.0 13.5 %collective-permute-start.3 = (bf16[128,1024]{1,0:T(8,128)(2,1)}, bf16[128,1024]{1,0:T(8,128)(2,1)S(1)}, u32[]{:S(2)}, u32[]{:S(2)}) collective-permute-start(bf16[128,1024]{1,0:T(8,128)(2,1)} %get-tuple-element.35), channel_id=1, source_target_pairs={{0,8},{4,12},{8,0},{12,4},{16,24},{20,28},{24,16},{28,20},{1,9},{5... | collective-permute-start | bytes 786440 | tf_op jit(solution)/shard_map/ppermute | solution.py:20
  24.1 13.2 %collective-permute-start.10 = (bf16[128,1024]{1,0:T(8,128)(2,1)}, bf16[128,1024]{1,0:T(8,128)(2,1)S(1)}, u32[]{:S(2)}, u32[]{:S(2)}) collective-permute-start(bf16[128,1024]{1,0:T(8,128)(2,1)} %get-tuple-element.47), channel_id=1, source_target_pairs={{0,4},{4,0},{8,12},{12,8},{16,20},{20,16},{24,28},{28,24},{1,5},{5... | collective-permute-start | bytes 786440 | tf_op jit(solution)/shard_map/ppermute | solution.py:20
  31.7 6.8 %collective-permute-start.14 = (f32[128,128]{1,0:T(8,128)S(1)}, f32[128,128]{1,0:T(8,128)S(1)}, u32[]{:S(2)}, u32[]{:S(2)}) collective-permute-start(f32[128,128]{1,0:T(8,128)S(1)} %add.69), channel_id=1, source_target_pairs={{0,16},{4,20},{8,24},{12,28},{16,0},{20,4},{24,8},{28,12},{1,17},{... | collective-permute-start | bytes 196616 | tf_op jit(solution)/shard_map/ppermute | solution.py:20
  34.2 9.2 %collective-permute-start.7 = (bf16[128,1024]{1,0:T(8,128)(2,1)S(1)}, bf16[128,1024]{1,0:T(8,128)(2,1)S(1)}, u32[]{:S(2)}, u32[]{:S(2)}) collective-permute-start(bf16[128,1024]{1,0:T(8,128)(2,1)S(1)} %add_convert_fusion.7), channel_id=1, source_target_pairs={{0,4},{4,0},{8,12},{12,8},{16,20},{20,16},{24,28},{28,24},{1,5},{5... | collective-permute-start | bytes 786440 | tf_op jit(solution)/shard_map/ppermute | solution.py:20
  35.5 10.3 %collective-permute-start.15 = (bf16[128,1024]{1,0:T(8,128)(2,1)S(1)}, bf16[128,1024]{1,0:T(8,128)(2,1)S(1)}, u32[]{:S(2)}, u32[]{:S(2)}) collective-permute-start(bf16[128,1024]{1,0:T(8,128)(2,1)S(1)} %get-tuple-element.43.refs_4_), channel_id=1, source_target_pairs={{0,8},{4,12},{8,0},{12,4},{16,24},{20,28},{24,16},{28,20},{1,9},{5... | collective-permute-start | bytes 786440 | tf_op jit(solution)/shard_map/ppermute | solution.py:20
  36.5 11.6 %collective-permute-start.17 = (bf16[128,1024]{1,0:T(8,128)(2,1)S(1)}, bf16[128,1024]{1,0:T(8,128)(2,1)S(1)}, u32[]{:S(2)}, u32[]{:S(2)}) collective-permute-start(bf16[128,1024]{1,0:T(8,128)(2,1)S(1)} %get-tuple-element.43.refs_4_), channel_id=1, source_target_pairs={{0,4},{4,0},{8,12},{12,8},{16,20},{20,16},{24,28},{28,24},{1,5},{5... | collective-permute-start | bytes 786440 | tf_op jit(solution)/shard_map/ppermute | solution.py:20
  37.3 13.6 %collective-permute-start.18 = (bf16[128,1024]{1,0:T(8,128)(2,1)S(1)}, bf16[128,1024]{1,0:T(8,128)(2,1)S(1)}, u32[]{:S(2)}, u32[]{:S(2)}) collective-permute-start(bf16[128,1024]{1,0:T(8,128)(2,1)S(1)} %collective-permute-done.8.refs_5_), channel_id=1, source_target_pairs={{0,4},{4,0},{8,12},{12,8},{16,20},{20,16},{24,28},{28,24},{1,5},{5... | collective-permute-start | bytes 786440 | tf_op jit(solution)/shard_map/ppermute | solution.py:20
  38.8 5.9 %collective-permute-start.26 = (f32[64,1024]{1,0:T(8,128)S(1)}, f32[64,1024]{1,0:T(8,128)S(1)}, u32[]{:S(2)}, u32[]{:S(2)}) collective-permute-start(f32[64,1024]{1,0:T(8,128)S(1)} %fusion.1), channel_id=1, source_target_pairs={{0,1},{1,0},{2,3},{3,2},{4,5},{5,4},{6,7},{7,6},{8,9},{9,8},{10,11... | collective-permute-start | bytes 786440 | tf_op jit(solution)/shard_map/ppermute | solution.py:20
  43.5 9.8 %collective-permute-start.19 = (bf16[128,1024]{1,0:T(8,128)(2,1)S(1)}, bf16[128,1024]{1,0:T(8,128)(2,1)S(1)}, u32[]{:S(2)}, u32[]{:S(2)}) collective-permute-start(bf16[128,1024]{1,0:T(8,128)(2,1)S(1)} %collective-permute-done.8.refs_5_), channel_id=1, source_target_pairs={{0,8},{4,12},{8,0},{12,4},{16,24},{20,28},{24,16},{28,20},{1,9},{5... | collective-permute-start | bytes 786440 | tf_op jit(solution)/shard_map/ppermute | solution.py:20
  44.7 14.3 %collective-permute-start.11 = (bf16[128,1024]{1,0:T(8,128)(2,1)S(1)}, bf16[128,1024]{1,0:T(8,128)(2,1)S(1)}, u32[]{:S(2)}, u32[]{:S(2)}) collective-permute-start(bf16[128,1024]{1,0:T(8,128)(2,1)S(1)} %add_convert_fusion.6), channel_id=1, source_target_pairs={{0,8},{4,12},{8,0},{12,4},{16,24},{20,28},{24,16},{28,20},{1,9},{5... | collective-permute-start | bytes 786440 | tf_op jit(solution)/shard_map/ppermute | solution.py:20
  45.8 18.7 %collective-permute-start.24 = (bf16[128,64]{1,0:T(8,128)(2,1)S(1)}, bf16[128,64]{1,0:T(8,128)(2,1)S(1)}, u32[]{:S(2)}, u32[]{:S(2)}) collective-permute-start(bf16[128,64]{1,0:T(8,128)(2,1)S(1)} %slice.9), channel_id=1, source_target_pairs={{0,2},{1,3},{2,0},{3,1},{4,6},{5,7},{6,4},{7,5},{8,10},{9,11},{10,... | collective-permute-start | bytes 49160 | tf_op jit(solution)/shard_map/ppermute | solution.py:20
  48.1 10.9 %collective-permute-start.9 = (bf16[128,1024]{1,0:T(8,128)(2,1)S(1)}, bf16[128,1024]{1,0:T(8,128)(2,1)S(1)}, u32[]{:S(2)}, u32[]{:S(2)}) collective-permute-start(bf16[128,1024]{1,0:T(8,128)(2,1)S(1)} %add_convert_fusion.4), channel_id=1, source_target_pairs={{0,2},{1,3},{2,0},{3,1},{4,6},{5,7},{6,4},{7,5},{8,10},{9,11},{10,... | collective-permute-start | bytes 786440 | tf_op jit(solution)/shard_map/ppermute | solution.py:20
  50.9 10.7 %collective-permute-start.20 = (bf16[128,1024]{1,0:T(8,128)(2,1)S(1)}, bf16[128,1024]{1,0:T(8,128)(2,1)S(1)}, u32[]{:S(2)}, u32[]{:S(2)}) collective-permute-start(bf16[128,1024]{1,0:T(8,128)(2,1)S(1)} %collective-permute-done.18.refs_7_), channel_id=1, source_target_pairs={{0,8},{4,12},{8,0},{12,4},{16,24},{20,28},{24,16},{28,20},{1,9},{5... | collective-permute-start | bytes 786440 | tf_op jit(solution)/shard_map/ppermute | solution.py:20
  59.2 12.2 %collective-permute-start.12 = (bf16[128,1024]{1,0:T(8,128)(2,1)S(1)}, bf16[128,1024]{1,0:T(8,128)(2,1)S(1)}, u32[]{:S(2)}, u32[]{:S(2)}) collective-permute-start(bf16[128,1024]{1,0:T(8,128)(2,1)S(1)} %get-tuple-element.61), channel_id=1, source_target_pairs={{0,16},{4,20},{8,24},{12,28},{16,0},{20,4},{24,8},{28,12},{1,17},{... | collective-permute-start | bytes 786440 | tf_op jit(solution)/shard_map/ppermute | solution.py:20
  60.4 6.4 %collective-permute-start.16 = (bf16[128,1024]{1,0:T(8,128)(2,1)S(1)}, bf16[128,1024]{1,0:T(8,128)(2,1)S(1)}, u32[]{:S(2)}, u32[]{:S(2)}) collective-permute-start(bf16[128,1024]{1,0:T(8,128)(2,1)S(1)} %collective-permute-done.15.refs_8_), channel_id=1, source_target_pairs={{0,4},{4,0},{8,12},{12,8},{16,20},{20,16},{24,28},{28,24},{1,5},{5... | collective-permute-start | bytes 786440 | tf_op jit(solution)/shard_map/ppermute | solution.py:20
  63.1 6.4 %collective-permute-start.21 = (bf16[128,1024]{1,0:T(8,128)(2,1)S(1)}, bf16[128,1024]{1,0:T(8,128)(2,1)S(1)}, u32[]{:S(2)}, u32[]{:S(2)}) collective-permute-start(bf16[128,1024]{1,0:T(8,128)(2,1)S(1)} %get-tuple-element.58), channel_id=1, source_target_pairs={{0,2},{1,3},{2,0},{3,1},{4,6},{5,7},{6,4},{7,5},{8,10},{9,11},{10,... | collective-permute-start | bytes 786440 | tf_op jit(solution)/shard_map/ppermute | solution.py:20
  64.9 8.1 %collective-permute-start.25 = (f32[1024,64]{0,1:T(8,128)S(1)}, f32[1024,64]{0,1:T(8,128)S(1)}, u32[]{:S(2)}, u32[]{:S(2)}) collective-permute-start(f32[1024,64]{0,1:T(8,128)S(1)} %fusion), channel_id=1, source_target_pairs={{0,1},{1,0},{2,3},{3,2},{4,5},{5,4},{6,7},{7,6},{8,9},{9,8},{10,11... | collective-permute-start | bytes 786440 | tf_op jit(solution)/shard_map/ppermute | solution.py:20
  (15 other events, 262.8 us)

commit v5 on v4

--- a/solution.py
+++ b/solution.py
@@ -340,7 +340,7 @@
     short = (set_rows, shard)
     acc_near, acc_far, blocks, last_tile, vals_seen = call(
         early_kernel,
-        32,
+        20,
         1,
         [(short, F32)] * 2 + [(blk_vals.shape, F32), (tile_half, BF16), (blk_vals.shape, BF16)],
         [

time: 75.2 us -> 75.2 us (level)
  starting transfers between devices: 30.3 us -> 32.4 us
  waiting for transfers between devices: 19.2 us -> 17.3 us
    ppermute x28, starting transfers between devices: 30.3 us -> 32.4 us  [swap(): return lax.ppermute(value, axis, [(i, i ^ mask) for i in range(size)])]
    ppermute x28, waiting for transfers between devices: 19.2 us -> 17.3 us  [swap(): return lax.ppermute(value, axis, [(i, i ^ mask) for i in range(size)])]
where the time goes in v5:
time: 75.2 us; the launch traced here: 74.9 us
  starting transfers between devices  32.4 us (43%)
  waiting for transfers between devices  17.3 us (23%)
  Pallas kernels  14.6 us (19%)
  other arithmetic  6.32 us (8%)
  matrix products  1.86 us (2%)
  between operations  1.59 us (2%)
  local copies, waits for them, and re-layouts  0.83 us (1%)
    ppermute x28, starting transfers between devices, swap(): return lax.ppermute(value, axis, [(i, i ^ mask) for i in range(size)])  32.4 us
    ppermute x28, waiting for transfers between devices, swap(): return lax.ppermute(value, axis, [(i, i ^ mask) for i in range(size)])  17.3 us
    pallas_call x5, Pallas kernels, call(): pl.pallas_call(body, out_shape=shapes, in_specs=[apart] * len(scalars) +...  14.6 us
    convert_element_type x3, other arithmetic, added(): return sum((term.astype(F32) for term in terms)).astype(BF16)  2.16 us
  transfers between devices with their start and end apart: 28, of which 11 were waited for; matrix products, arithmetic and copies ran while one was open for 10% of the time, Pallas kernels for 20%

profile of v5, /device:TPU:0, one launch (start us, length us, event | category | flops | bytes accessed | tf_op | source)
XLA Modules:
  0.0 74.9 jit_solution(2726340869747513220)
XLA Ops:
  1.1 2.6 %collective-permute-start = (bf16[128,1024]{1,0:T(8,128)(2,1)}, bf16[128,1024]{1,0:T(8,128)(2,1)S(1)}, u32[]{:S(2)}, u32[]{:S(2)}) collective-permute-start(bf16[128,1024]{1,0:T(8,128)(2,1)} %refs_2_.3), channel_id=1, source_target_pairs={{0,2},{1,3},{2,0},{3,1},{4,6},{5,7},{6,4},{7,5},{8,10},{9,11},{10,... | collective-permute-start | bytes 786440 | tf_op jit(solution)/shard_map/ppermute | solution.py:20
  3.7 2.2 %shard_map.119 = f32[128,128]{1,0:T(8,128)} custom-call(bf16[128,1024]{1,0:T(8,128)(2,1)} %refs_2_.3, bf16[128,1024]{1,0:T(8,128)(2,1)} %refs_1_.5, bf16[64,1024]{1,0:T(8,128)(2,1)} %bitcast.14, bf16[64,1024]{1,0:T(8,128)(2,1)} %refs_3_.2), custom_call_target="tpu_custom_call" | custom-call | flops 33554432 | bytes 786432 | tf_op jit(solution)/shard_map/pallas_call | solution.py:68
  6.0 1.6 %collective-permute-start.1 = (f32[128,128]{1,0:T(8,128)}, f32[128,128]{1,0:T(8,128)S(1)}, u32[]{:S(2)}, u32[]{:S(2)}) collective-permute-start(f32[128,128]{1,0:T(8,128)} %shard_map.119), channel_id=1, source_target_pairs={{0,4},{4,0},{8,12},{12,8},{16,20},{20,16},{24,28},{28,24},{1,5},{5... | collective-permute-start | bytes 196616 | tf_op jit(solution)/shard_map/ppermute | solution.py:20
  7.6 2.6 %collective-permute-start.6 = (bf16[128,1024]{1,0:T(8,128)(2,1)}, bf16[128,1024]{1,0:T(8,128)(2,1)S(1)}, u32[]{:S(2)}, u32[]{:S(2)}) collective-permute-start(bf16[128,1024]{1,0:T(8,128)(2,1)} %refs_1_.5), channel_id=1, source_target_pairs={{0,16},{4,20},{8,24},{12,28},{16,0},{20,4},{24,8},{28,12},{1,17},{... | collective-permute-start | bytes 786440 | tf_op jit(solution)/shard_map/ppermute | solution.py:20
  11.7 1.6 %collective-permute-start.13 = (f32[128,128]{1,0:T(8,128)S(1)}, f32[128,128]{1,0:T(8,128)S(1)}, u32[]{:S(2)}, u32[]{:S(2)}) collective-permute-start(f32[128,128]{1,0:T(8,128)S(1)} %add.61), channel_id=1, source_target_pairs={{0,8},{4,12},{8,0},{12,4},{16,24},{20,28},{24,16},{28,20},{1,9},{5... | collective-permute-start | bytes 196616 | tf_op jit(solution)/shard_map/ppermute | solution.py:20
  14.0 5.9 %shard_map.120 = (bf16[128,1024]{1,0:T(8,128)(2,1)}, bf16[128,1024]{1,0:T(8,128)(2,1)}, bf16[128,1024]{1,0:T(8,128)(2,1)}, bf16[128,1024]{1,0:T(8,128)(2,1)}, bf...) custom-call(s32[2,3]{1,0:T(2,128)} %bitcast.10, ...), custom_call_target="tpu_custom_call" | custom-call | flops 2147483648 | bytes 9011200 | tf_op jit(solution)/shard_map/pallas_call | solution.py:68
  20.5 1.4 %collective-permute-start.4 = (bf16[128,1024]{1,0:T(8,128)(2,1)}, bf16[128,1024]{1,0:T(8,128)(2,1)S(1)}, u32[]{:S(2)}, u32[]{:S(2)}) collective-permute-start(bf16[128,1024]{1,0:T(8,128)(2,1)} %get-tuple-element.37), channel_id=1, source_target_pairs={{0,4},{4,0},{8,12},{12,8},{16,20},{20,16},{24,28},{28,24},{1,5},{5... | collective-permute-start | bytes 786440 | tf_op jit(solution)/shard_map/ppermute | solution.py:20
  23.0 1.2 %collective-permute-start.3 = (bf16[128,1024]{1,0:T(8,128)(2,1)}, bf16[128,1024]{1,0:T(8,128)(2,1)S(1)}, u32[]{:S(2)}, u32[]{:S(2)}) collective-permute-start(bf16[128,1024]{1,0:T(8,128)(2,1)} %get-tuple-element.35), channel_id=1, source_target_pairs={{0,8},{4,12},{8,0},{12,4},{16,24},{20,28},{24,16},{28,20},{1,9},{5... | collective-permute-start | bytes 786440 | tf_op jit(solution)/shard_map/ppermute | solution.py:20
  24.2 1.1 %collective-permute-start.10 = (bf16[128,1024]{1,0:T(8,128)(2,1)}, bf16[128,1024]{1,0:T(8,128)(2,1)S(1)}, u32[]{:S(2)}, u32[]{:S(2)}) collective-permute-start(bf16[128,1024]{1,0:T(8,128)(2,1)} %get-tuple-element.47), channel_id=1, source_target_pairs={{0,4},{4,0},{8,12},{12,8},{16,20},{20,16},{24,28},{28,24},{1,5},{5... | collective-permute-start | bytes 786440 | tf_op jit(solution)/shard_map/ppermute | solution.py:20
  25.2 4.3 %collective-permute-done.5 = bf16[128,1024]{1,0:T(8,128)(2,1)S(1)} collective-permute-done((bf16[128,1024]{1,0:T(8,128)(2,1)}, bf16[128,1024]{1,0:T(8,128)(2,1)S(1)}, u32[]{:S(2)}, u32[]{:S(2)}) %collective-permute-start.5) | collective-permute-done | bytes 262176 | tf_op jit(solution)/shard_map/ppermute | solution.py:20
  31.6 2.5 %collective-permute-start.14 = (f32[128,128]{1,0:T(8,128)S(1)}, f32[128,128]{1,0:T(8,128)S(1)}, u32[]{:S(2)}, u32[]{:S(2)}) collective-permute-start(f32[128,128]{1,0:T(8,128)S(1)} %add.69), channel_id=1, source_target_pairs={{0,16},{4,20},{8,24},{12,28},{16,0},{20,4},{24,8},{28,12},{1,17},{... | collective-permute-start | bytes 196616 | tf_op jit(solution)/shard_map/ppermute | solution.py:20
  34.1 1.8 %collective-permute-start.7 = (bf16[128,1024]{1,0:T(8,128)(2,1)S(1)}, bf16[128,1024]{1,0:T(8,128)(2,1)S(1)}, u32[]{:S(2)}, u32[]{:S(2)}) collective-permute-start(bf16[128,1024]{1,0:T(8,128)(2,1)S(1)} %add_convert_fusion.7), channel_id=1, source_target_pairs={{0,4},{4,0},{8,12},{12,8},{16,20},{20,16},{24,28},{28,24},{1,5},{5... | collective-permute-start | bytes 786440 | tf_op jit(solution)/shard_map/ppermute | solution.py:20
  37.2 1.8 %collective-permute-start.18 = (bf16[128,1024]{1,0:T(8,128)(2,1)S(1)}, bf16[128,1024]{1,0:T(8,128)(2,1)S(1)}, u32[]{:S(2)}, u32[]{:S(2)}) collective-permute-start(bf16[128,1024]{1,0:T(8,128)(2,1)S(1)} %collective-permute-done.8.refs_5_), channel_id=1, source_target_pairs={{0,4},{4,0},{8,12},{12,8},{16,20},{20,16},{24,28},{28,24},{1,5},{5... | collective-permute-start | bytes 786440 | tf_op jit(solution)/shard_map/ppermute | solution.py:20
  39.6 3.7 %collective-permute-done.7 = bf16[128,1024]{1,0:T(8,128)(2,1)S(1)} collective-permute-done((bf16[128,1024]{1,0:T(8,128)(2,1)S(1)}, bf16[128,1024]{1,0:T(8,128)(2,1)S(1)}, u32[]{:S(2)}, u32[]{:S(2)}) %collective-permute-start.7) | collective-permute-done | bytes 262176 | tf_op jit(solution)/shard_map/ppermute | solution.py:20
  45.7 2.1 %collective-permute-done.17.refs_6_ = bf16[128,1024]{1,0:T(8,128)(2,1)S(1)} collective-permute-done((bf16[128,1024]{1,0:T(8,128)(2,1)S(1)}, bf16[128,1024]{1,0:T(8,128)(2,1)S(1)}, u32[]{:S(2)}, u32[]{:S(2)}) %collective-permute-start.17) | collective-permute-done | bytes 262176 | tf_op jit(solution)/shard_map/ppermute | solution.py:20
  48.6 2.0 %collective-permute-done.18.refs_7_ = bf16[128,1024]{1,0:T(8,128)(2,1)S(1)} collective-permute-done((bf16[128,1024]{1,0:T(8,128)(2,1)S(1)}, bf16[128,1024]{1,0:T(8,128)(2,1)S(1)}, u32[]{:S(2)}, u32[]{:S(2)}) %collective-permute-start.18) | collective-permute-done | bytes 262176 | tf_op jit(solution)/shard_map/ppermute | solution.py:20
  50.6 2.4 %collective-permute-start.20 = (bf16[128,1024]{1,0:T(8,128)(2,1)S(1)}, bf16[128,1024]{1,0:T(8,128)(2,1)S(1)}, u32[]{:S(2)}, u32[]{:S(2)}) collective-permute-start(bf16[128,1024]{1,0:T(8,128)(2,1)S(1)} %collective-permute-done.18.refs_7_), channel_id=1, source_target_pairs={{0,8},{4,12},{8,0},{12,4},{16,24},{20,28},{24,16},{28,20},{1,9},{5... | collective-permute-start | bytes 786440 | tf_op jit(solution)/shard_map/ppermute | solution.py:20
  53.6 3.6 %shard_map.121 = (f32[128,1024]{1,0:T(8,128)S(1)}, f32[128,1024]{1,0:T(8,128)S(1)}, f32[3,128,128]{2,1,0:T(8,128)S(1)}, bf16[1024,1024]{1,0:T(8,128)(2,1)S(1)}, bf16[3,128,128]{2,1,0:T(8,128)(2,1)S(1)}) custom-call(s32[2,3]{1,0:T(2,128)S(1)} %bitcast.11, s32[1]{0:T(128)S(6)} %copy.13.refs_1_, bf16[128,1024]{1,0:T(8,128)(2,1)S(1)} %copy-done.1, ...), custom_call_target="tpu_custom_call" | custom-call | flops 1610612736 | bytes 10584064 | tf_op jit(solution)/shard_map/pallas_call | solution.py:68
  58.9 1.4 %collective-permute-start.12 = (bf16[128,1024]{1,0:T(8,128)(2,1)S(1)}, bf16[128,1024]{1,0:T(8,128)(2,1)S(1)}, u32[]{:S(2)}, u32[]{:S(2)}) collective-permute-start(bf16[128,1024]{1,0:T(8,128)(2,1)S(1)} %get-tuple-element.61), channel_id=1, source_target_pairs={{0,16},{4,20},{8,24},{12,28},{16,0},{20,4},{24,8},{28,12},{1,17},{... | collective-permute-start | bytes 786440 | tf_op jit(solution)/shard_map/ppermute | solution.py:20
  60.3 1.7 %collective-permute-start.16 = (bf16[128,1024]{1,0:T(8,128)(2,1)S(1)}, bf16[128,1024]{1,0:T(8,128)(2,1)S(1)}, u32[]{:S(2)}, u32[]{:S(2)}) collective-permute-start(bf16[128,1024]{1,0:T(8,128)(2,1)S(1)} %collective-permute-done.15.refs_8_), channel_id=1, source_target_pairs={{0,4},{4,0},{8,12},{12,8},{16,20},{20,16},{24,28},{28,24},{1,5},{5... | collective-permute-start | bytes 786440 | tf_op jit(solution)/shard_map/ppermute | solution.py:20
  62.0 1.4 %shard_map.122 = (bf16[128,1024]{1,0:T(8,128)(2,1)S(1)}, f32[3,128,128]{2,1,0:T(8,128)S(1)}) custom-call(s32[2,3]{1,0:T(2,128)S(1)} %bitcast.12, s32[1]{0:T(128)S(6)} %copy.13.refs_1_, bf16[128,1024]{1,0:T(8,128)(2,1)S(1)} %copy-done.3, bf16[128,1024]{1,0:T(8,128)(2,1)S(1)} %collective-permute-done.20.refs_3_, f32[128,1024]{1,0:T(8,128)S(1)} %get-tuple-element.52.refs_4_, ...), custom_call_target="tpu_custom_call" | custom-call | flops 2684354 | bytes 34406 | tf_op jit(solution)/shard_map/pallas_call | solution.py:68
  65.0 1.7 %collective-permute-done.16.refs_3_ = bf16[128,1024]{1,0:T(8,128)(2,1)S(1)} collective-permute-done((bf16[128,1024]{1,0:T(8,128)(2,1)S(1)}, bf16[128,1024]{1,0:T(8,128)(2,1)S(1)}, u32[]{:S(2)}, u32[]{:S(2)}) %collective-permute-start.16) | collective-permute-done | bytes 262176 | tf_op jit(solution)/shard_map/ppermute | solution.py:20
  66.7 1.4 %shard_map.123 = (f32[128,1024]{1,0:T(8,128)S(1)}, f32[3,128,128]{2,1,0:T(8,128)S(1)}) custom-call(s32[2,3]{1,0:T(2,128)S(1)} %bitcast.13, s32[1]{0:T(128)S(6)} %copy.13.refs_1_, bf16[128,1024]{1,0:T(8,128)(2,1)S(1)} %copy-done.1, bf16[128,1024]{1,0:T(8,128)(2,1)S(1)} %collective-permute-done.16.refs_3_, f32[128,1024]{1,0:T(8,128)S(1)} %get-tuple-element.51.refs_4_, ...), custom_call_target="tpu_custom_call" | custom-call | flops 2684354 | bytes 34406 | tf_op jit(solution)/shard_map/pallas_call | solution.py:68
  68.1 1.1 %collective-permute-start.22 = (bf16[3,128,128]{2,1,0:T(8,128)(2,1)S(1)}, bf16[3,128,128]{2,1,0:T(8,128)(2,1)S(1)}, u32[]{:S(2)}, u32[]{:S(2)}) collective-permute-start(bf16[3,128,128]{2,1,0:T(8,128)(2,1)S(1)} %convert_element_type.114), channel_id=1, source_target_pairs={{0,2},{1,3},{2,0},{3,1},{4,6},{5,7},{6,4},{7,5},{8,10},{9,11},{10,... | collective-permute-start | bytes 294920 | tf_op jit(solution)/shard_map/ppermute | solution.py:20
  (80 shorter events, 20.2 us)
Async XLA Ops:
  0.6 12.7 %collective-permute-start.2 = (bf16[1024,2048]{1,0:T(8,128)(2,1)}, bf16[1024,2048]{1,0:T(8,128)(2,1)}, u32[]{:S(2)}, u32[]{:S(2)}) collective-permute-start(bf16[1024,2048]{1,0:T(8,128)(2,1)} %refs_11_.1), channel_id=1, source_target_pairs={{0,1},{1,0},{2,3},{3,2},{4,5},{5,4},{6,7},{7,6},{8,9},{9,8},{10,11... | collective-permute-start | bytes 12582920 | tf_op jit(solution)/shard_map/ppermute | solution.py:20
  1.1 12.2 %collective-permute-start = (bf16[128,1024]{1,0:T(8,128)(2,1)}, bf16[128,1024]{1,0:T(8,128)(2,1)S(1)}, u32[]{:S(2)}, u32[]{:S(2)}) collective-permute-start(bf16[128,1024]{1,0:T(8,128)(2,1)} %refs_2_.3), channel_id=1, source_target_pairs={{0,2},{1,3},{2,0},{3,1},{4,6},{5,7},{6,4},{7,5},{8,10},{9,11},{10,... | collective-permute-start | bytes 786440 | tf_op jit(solution)/shard_map/ppermute | solution.py:20
  7.6 14.8 %collective-permute-start.6 = (bf16[128,1024]{1,0:T(8,128)(2,1)}, bf16[128,1024]{1,0:T(8,128)(2,1)S(1)}, u32[]{:S(2)}, u32[]{:S(2)}) collective-permute-start(bf16[128,1024]{1,0:T(8,128)(2,1)} %refs_1_.5), channel_id=1, source_target_pairs={{0,16},{4,20},{8,24},{12,28},{16,0},{20,4},{24,8},{28,12},{1,17},{... | collective-permute-start | bytes 786440 | tf_op jit(solution)/shard_map/ppermute | solution.py:20
  11.7 8.8 %collective-permute-start.13 = (f32[128,128]{1,0:T(8,128)S(1)}, f32[128,128]{1,0:T(8,128)S(1)}, u32[]{:S(2)}, u32[]{:S(2)}) collective-permute-start(f32[128,128]{1,0:T(8,128)S(1)} %add.61), channel_id=1, source_target_pairs={{0,8},{4,12},{8,0},{12,4},{16,24},{20,28},{24,16},{28,20},{1,9},{5... | collective-permute-start | bytes 196616 | tf_op jit(solution)/shard_map/ppermute | solution.py:20
  20.0 9.5 %collective-permute-start.5 = (bf16[128,1024]{1,0:T(8,128)(2,1)}, bf16[128,1024]{1,0:T(8,128)(2,1)S(1)}, u32[]{:S(2)}, u32[]{:S(2)}) collective-permute-start(bf16[128,1024]{1,0:T(8,128)(2,1)} %get-tuple-element.39), channel_id=1, source_target_pairs={{0,8},{4,12},{8,0},{12,4},{16,24},{20,28},{24,16},{28,20},{1,9},{5... | collective-permute-start | bytes 786440 | tf_op jit(solution)/shard_map/ppermute | solution.py:20
  20.5 10.0 %collective-permute-start.4 = (bf16[128,1024]{1,0:T(8,128)(2,1)}, bf16[128,1024]{1,0:T(8,128)(2,1)S(1)}, u32[]{:S(2)}, u32[]{:S(2)}) collective-permute-start(bf16[128,1024]{1,0:T(8,128)(2,1)} %get-tuple-element.37), channel_id=1, source_target_pairs={{0,4},{4,0},{8,12},{12,8},{16,20},{20,16},{24,28},{28,24},{1,5},{5... | collective-permute-start | bytes 786440 | tf_op jit(solution)/shard_map/ppermute | solution.py:20
  22.4 9.1 %collective-permute-start.8 = (bf16[128,1024]{1,0:T(8,128)(2,1)S(1)}, bf16[128,1024]{1,0:T(8,128)(2,1)S(1)}, u32[]{:S(2)}, u32[]{:S(2)}) collective-permute-start(bf16[128,1024]{1,0:T(8,128)(2,1)S(1)} %get-tuple-element.63), channel_id=1, source_target_pairs={{0,2},{1,3},{2,0},{3,1},{4,6},{5,7},{6,4},{7,5},{8,10},{9,11},{10,... | collective-permute-start | bytes 786440 | tf_op jit(solution)/shard_map/ppermute | solution.py:20
  23.0 13.9 %collective-permute-start.3 = (bf16[128,1024]{1,0:T(8,128)(2,1)}, bf16[128,1024]{1,0:T(8,128)(2,1)S(1)}, u32[]{:S(2)}, u32[]{:S(2)}) collective-permute-start(bf16[128,1024]{1,0:T(8,128)(2,1)} %get-tuple-element.35), channel_id=1, source_target_pairs={{0,8},{4,12},{8,0},{12,4},{16,24},{20,28},{24,16},{28,20},{1,9},{5... | collective-permute-start | bytes 786440 | tf_op jit(solution)/shard_map/ppermute | solution.py:20
  24.2 13.0 %collective-permute-start.10 = (bf16[128,1024]{1,0:T(8,128)(2,1)}, bf16[128,1024]{1,0:T(8,128)(2,1)S(1)}, u32[]{:S(2)}, u32[]{:S(2)}) collective-permute-start(bf16[128,1024]{1,0:T(8,128)(2,1)} %get-tuple-element.47), channel_id=1, source_target_pairs={{0,4},{4,0},{8,12},{12,8},{16,20},{20,16},{24,28},{28,24},{1,5},{5... | collective-permute-start | bytes 786440 | tf_op jit(solution)/shard_map/ppermute | solution.py:20
  31.6 7.4 %collective-permute-start.14 = (f32[128,128]{1,0:T(8,128)S(1)}, f32[128,128]{1,0:T(8,128)S(1)}, u32[]{:S(2)}, u32[]{:S(2)}) collective-permute-start(f32[128,128]{1,0:T(8,128)S(1)} %add.69), channel_id=1, source_target_pairs={{0,16},{4,20},{8,24},{12,28},{16,0},{20,4},{24,8},{28,12},{1,17},{... | collective-permute-start | bytes 196616 | tf_op jit(solution)/shard_map/ppermute | solution.py:20
  34.1 9.2 %collective-permute-start.7 = (bf16[128,1024]{1,0:T(8,128)(2,1)S(1)}, bf16[128,1024]{1,0:T(8,128)(2,1)S(1)}, u32[]{:S(2)}, u32[]{:S(2)}) collective-permute-start(bf16[128,1024]{1,0:T(8,128)(2,1)S(1)} %add_convert_fusion.7), channel_id=1, source_target_pairs={{0,4},{4,0},{8,12},{12,8},{16,20},{20,16},{24,28},{28,24},{1,5},{5... | collective-permute-start | bytes 786440 | tf_op jit(solution)/shard_map/ppermute | solution.py:20
  35.9 9.7 %collective-permute-start.15 = (bf16[128,1024]{1,0:T(8,128)(2,1)S(1)}, bf16[128,1024]{1,0:T(8,128)(2,1)S(1)}, u32[]{:S(2)}, u32[]{:S(2)}) collective-permute-start(bf16[128,1024]{1,0:T(8,128)(2,1)S(1)} %get-tuple-element.43.refs_4_), channel_id=1, source_target_pairs={{0,8},{4,12},{8,0},{12,4},{16,24},{20,28},{24,16},{28,20},{1,9},{5... | collective-permute-start | bytes 786440 | tf_op jit(solution)/shard_map/ppermute | solution.py:20
  36.9 10.8 %collective-permute-start.17 = (bf16[128,1024]{1,0:T(8,128)(2,1)S(1)}, bf16[128,1024]{1,0:T(8,128)(2,1)S(1)}, u32[]{:S(2)}, u32[]{:S(2)}) collective-permute-start(bf16[128,1024]{1,0:T(8,128)(2,1)S(1)} %get-tuple-element.43.refs_4_), channel_id=1, source_target_pairs={{0,4},{4,0},{8,12},{12,8},{16,20},{20,16},{24,28},{28,24},{1,5},{5... | collective-permute-start | bytes 786440 | tf_op jit(solution)/shard_map/ppermute | solution.py:20
  37.2 13.4 %collective-permute-start.18 = (bf16[128,1024]{1,0:T(8,128)(2,1)S(1)}, bf16[128,1024]{1,0:T(8,128)(2,1)S(1)}, u32[]{:S(2)}, u32[]{:S(2)}) collective-permute-start(bf16[128,1024]{1,0:T(8,128)(2,1)S(1)} %collective-permute-done.8.refs_5_), channel_id=1, source_target_pairs={{0,4},{4,0},{8,12},{12,8},{16,20},{20,16},{24,28},{28,24},{1,5},{5... | collective-permute-start | bytes 786440 | tf_op jit(solution)/shard_map/ppermute | solution.py:20
  39.2 5.3 %collective-permute-start.26 = (f32[64,1024]{1,0:T(8,128)S(1)}, f32[64,1024]{1,0:T(8,128)S(1)}, u32[]{:S(2)}, u32[]{:S(2)}) collective-permute-start(f32[64,1024]{1,0:T(8,128)S(1)} %fusion.1), channel_id=1, source_target_pairs={{0,1},{1,0},{2,3},{3,2},{4,5},{5,4},{6,7},{7,6},{8,9},{9,8},{10,11... | collective-permute-start | bytes 786440 | tf_op jit(solution)/shard_map/ppermute | solution.py:20
  43.3 9.7 %collective-permute-start.19 = (bf16[128,1024]{1,0:T(8,128)(2,1)S(1)}, bf16[128,1024]{1,0:T(8,128)(2,1)S(1)}, u32[]{:S(2)}, u32[]{:S(2)}) collective-permute-start(bf16[128,1024]{1,0:T(8,128)(2,1)S(1)} %collective-permute-done.8.refs_5_), channel_id=1, source_target_pairs={{0,8},{4,12},{8,0},{12,4},{16,24},{20,28},{24,16},{28,20},{1,9},{5... | collective-permute-start | bytes 786440 | tf_op jit(solution)/shard_map/ppermute | solution.py:20
  44.5 14.2 %collective-permute-start.11 = (bf16[128,1024]{1,0:T(8,128)(2,1)S(1)}, bf16[128,1024]{1,0:T(8,128)(2,1)S(1)}, u32[]{:S(2)}, u32[]{:S(2)}) collective-permute-start(bf16[128,1024]{1,0:T(8,128)(2,1)S(1)} %add_convert_fusion.6), channel_id=1, source_target_pairs={{0,8},{4,12},{8,0},{12,4},{16,24},{20,28},{24,16},{28,20},{1,9},{5... | collective-permute-start | bytes 786440 | tf_op jit(solution)/shard_map/ppermute | solution.py:20
  45.6 18.8 %collective-permute-start.24 = (bf16[128,64]{1,0:T(8,128)(2,1)S(1)}, bf16[128,64]{1,0:T(8,128)(2,1)S(1)}, u32[]{:S(2)}, u32[]{:S(2)}) collective-permute-start(bf16[128,64]{1,0:T(8,128)(2,1)S(1)} %slice.9), channel_id=1, source_target_pairs={{0,2},{1,3},{2,0},{3,1},{4,6},{5,7},{6,4},{7,5},{8,10},{9,11},{10,... | collective-permute-start | bytes 49160 | tf_op jit(solution)/shard_map/ppermute | solution.py:20
  47.8 10.9 %collective-permute-start.9 = (bf16[128,1024]{1,0:T(8,128)(2,1)S(1)}, bf16[128,1024]{1,0:T(8,128)(2,1)S(1)}, u32[]{:S(2)}, u32[]{:S(2)}) collective-permute-start(bf16[128,1024]{1,0:T(8,128)(2,1)S(1)} %add_convert_fusion.4), channel_id=1, source_target_pairs={{0,2},{1,3},{2,0},{3,1},{4,6},{5,7},{6,4},{7,5},{8,10},{9,11},{10,... | collective-permute-start | bytes 786440 | tf_op jit(solution)/shard_map/ppermute | solution.py:20
  50.6 11.5 %collective-permute-start.20 = (bf16[128,1024]{1,0:T(8,128)(2,1)S(1)}, bf16[128,1024]{1,0:T(8,128)(2,1)S(1)}, u32[]{:S(2)}, u32[]{:S(2)}) collective-permute-start(bf16[128,1024]{1,0:T(8,128)(2,1)S(1)} %collective-permute-done.18.refs_7_), channel_id=1, source_target_pairs={{0,8},{4,12},{8,0},{12,4},{16,24},{20,28},{24,16},{28,20},{1,9},{5... | collective-permute-start | bytes 786440 | tf_op jit(solution)/shard_map/ppermute | solution.py:20
  58.9 12.2 %collective-permute-start.12 = (bf16[128,1024]{1,0:T(8,128)(2,1)S(1)}, bf16[128,1024]{1,0:T(8,128)(2,1)S(1)}, u32[]{:S(2)}, u32[]{:S(2)}) collective-permute-start(bf16[128,1024]{1,0:T(8,128)(2,1)S(1)} %get-tuple-element.61), channel_id=1, source_target_pairs={{0,16},{4,20},{8,24},{12,28},{16,0},{20,4},{24,8},{28,12},{1,17},{... | collective-permute-start | bytes 786440 | tf_op jit(solution)/shard_map/ppermute | solution.py:20
  60.3 6.4 %collective-permute-start.16 = (bf16[128,1024]{1,0:T(8,128)(2,1)S(1)}, bf16[128,1024]{1,0:T(8,128)(2,1)S(1)}, u32[]{:S(2)}, u32[]{:S(2)}) collective-permute-start(bf16[128,1024]{1,0:T(8,128)(2,1)S(1)} %collective-permute-done.15.refs_8_), channel_id=1, source_target_pairs={{0,4},{4,0},{8,12},{12,8},{16,20},{20,16},{24,28},{28,24},{1,5},{5... | collective-permute-start | bytes 786440 | tf_op jit(solution)/shard_map/ppermute | solution.py:20
  63.5 6.7 %collective-permute-start.21 = (bf16[128,1024]{1,0:T(8,128)(2,1)S(1)}, bf16[128,1024]{1,0:T(8,128)(2,1)S(1)}, u32[]{:S(2)}, u32[]{:S(2)}) collective-permute-start(bf16[128,1024]{1,0:T(8,128)(2,1)S(1)} %get-tuple-element.58), channel_id=1, source_target_pairs={{0,2},{1,3},{2,0},{3,1},{4,6},{5,7},{6,4},{7,5},{8,10},{9,11},{10,... | collective-permute-start | bytes 786440 | tf_op jit(solution)/shard_map/ppermute | solution.py:20
  64.9 8.0 %collective-permute-start.25 = (f32[1024,64]{0,1:T(8,128)S(1)}, f32[1024,64]{0,1:T(8,128)S(1)}, u32[]{:S(2)}, u32[]{:S(2)}) collective-permute-start(f32[1024,64]{0,1:T(8,128)S(1)} %fusion), channel_id=1, source_target_pairs={{0,1},{1,0},{2,3},{3,2},{4,5},{5,4},{6,7},{7,6},{8,9},{9,8},{10,11... | collective-permute-start | bytes 786440 | tf_op jit(solution)/shard_map/ppermute | solution.py:20
  (15 other events, 262.9 us)
